TPU v7x, 32 devices: a whole 2x2x4 slice. The times are simulated.
32 devices in a mesh: dp: 4 (over z), expert: 8 (over y, x, core).
Axes of the slice: x: 2, y: 2, z: 4, core: 2. Of those that a mesh axis runs over, the one named last changes fastest.
Arguments:
- hidden_in: bfloat16 [32768, 512], P(('dp', 'expert')), may hold values from -6 to 6
- lengths: int32 [32, 32], P(('dp', 'expert')), may hold values from 1 to 64, 1024 in all within a row
- task_ids: int32 [32, 32], P(('dp', 'expert')), may hold values from 0 to 29
- task_experts: int32 [30, 2], replicated, may hold values from 0 to 7, all different within a row
- capacity: int32 [8], replicated, may hold values from 256 to 512, as said below
- task_logits: float32 [30, 8], replicated, may hold values from -4 to 4
- norm_params: bfloat16 [512, 8], P('dp'), may hold values from -0.6 to 1.6
- w_qkv: bfloat16 [512, 2, 1536], P('dp'), may hold values from -0.25 to 0.25
- w_attn: bfloat16 [512, 2, 512], P('dp'), may hold values from -1 to 1
- w_up: bfloat16 [512, 2048], P('dp'), may hold values from -0.25 to 0.25
- w_down: bfloat16 [2048, 512], P('dp'), may hold values from -0.125 to 0.125
- expert_up: bfloat16 [8, 512, 2048], P('expert', 'dp'), may hold values from -0.25 to 0.25
- expert_down: bfloat16 [8, 2048, 512], P('expert', 'dp'), may hold values from -0.5 to 0.5
- cotangent: bfloat16 [32768, 512], P(('dp', 'expert')), may hold values from -6 to 6
Outputs:
- hidden_out: bfloat16 [32768, 512], P(('dp', 'expert'))
- grad_in: float32 [32768, 512], P(('dp', 'expert'))
- grad_task_logits: float32 [30, 8], replicated
- grad_norm_params: float32 [512, 8], P('dp')
- grad_qkv: float32 [512, 2, 1536], P('dp')
- grad_attn: float32 [512, 2, 512], P('dp')
- grad_up: float32 [512, 2048], P('dp')
- grad_down: float32 [2048, 512], P('dp')
- grad_expert_up: float32 [8, 512, 2048], P('expert', 'dp')
- grad_expert_down: float32 [8, 2048, 512], P('expert', 'dp')
Inputs may be any that keep to these rules, and one draw needn't show every extreme that they name: The lengths of each pack sum to 1024, and the longest of each pack has exactly 64 tokens. `task_experts`: each task names two different experts; every expert is named by some task. Some expert has a capacity of exactly 512.
All inputs are finite; a program needn't handle non-finite values.
Results may differ from a plain program's by a relative error of at most 0.02.
Values may be sent and summed in bfloat16 or wider, within the bound.
No kernel may reach another device: no remote copies, remote signals or barrier semaphores. Data moves between devices by JAX's collectives and lax.ppermute only.
A program may use at most 256 MiB of HBM per device.

v0:
```python
import jax
import jax.numpy as jnp
from jax import lax
from jax.sharding import PartitionSpec as P

D = 512
HEADS = 8
PACK = 1024
MOST_LEN = 64


highest = lax.Precision.HIGHEST
epsilon = 1e-05
blocked = -1e30


def norm_rows(hidden, gain, shift):
    centre = jnp.mean(hidden, axis=-1, keepdims=True)
    centered = hidden - centre
    spread = jnp.mean(centered * centered, axis=-1, keepdims=True)
    return centered * lax.rsqrt(spread + epsilon) * gain + shift


def norm_back(hidden, gain, shift, grad_normed):
    _, pullback = jax.vjp(norm_rows, hidden, gain, shift)
    return pullback(grad_normed)


def gelu_back(inner_act, grad_active):
    _, pullback = jax.vjp(jax.nn.gelu, inner_act)
    return pullback(grad_active)[0]


def outer_sum(rows_left, rows_right):
    return lax.dot_general(
        rows_left, rows_right, (((0,), (0,)), ((), ())), preferred_element_type=jnp.float32
    )


def times_back(rows_left, rows_right):
    return lax.dot_general(
        rows_left, rows_right, (((1,), (1,)), ((), ())), preferred_element_type=jnp.float32
    )


def route_block(lengths, task_ids, task_experts, capacity, cap_slots, length):
    pack_count, sentences = lengths.shape
    experts = capacity.shape[0]
    task_count = task_experts.shape[0]
    sent_ends = jnp.cumsum(lengths, axis=1)
    starts = sent_ends - lengths
    position = lax.broadcasted_iota(jnp.int32, (pack_count, length), 1)
    segment = jnp.sum((position[:, :, None] >= sent_ends[:, None, :]).astype(jnp.int32), axis=2)
    member = (segment[:, :, None] == lax.broadcasted_iota(jnp.int32, (1, 1, sentences), 2)).astype(
        jnp.int32
    )
    offset = position - jnp.sum(member * starts[:, None, :], axis=2)
    task_flat = task_ids.reshape(-1)
    task_hot = (task_flat[:, None] == lax.broadcasted_iota(jnp.int32, (1, task_count), 1)).astype(
        jnp.int32
    )
    pair_expert = jnp.sum(task_hot[:, :, None] * task_experts[None, :, :], axis=1)
    pair_len = jnp.broadcast_to(lengths.reshape(-1, 1), pair_expert.shape).reshape(-1)
    pair_flat = pair_expert.reshape(-1)
    expert_hot = (pair_flat[:, None] == lax.broadcasted_iota(jnp.int32, (1, experts), 1)).astype(
        jnp.int32
    )
    running = jnp.cumsum(expert_hot * pair_len[:, None], axis=0)
    filled = jnp.sum(running * expert_hot, axis=1)
    limits = jnp.sum(expert_hot * capacity[None, :], axis=1)
    pair_base = jnp.where(filled <= limits, pair_flat * cap_slots + filled - pair_len, -1)
    token_base = jnp.sum(
        member[:, :, :, None] * pair_base.reshape(pack_count, 1, sentences, 2), axis=2
    )
    tokens = pack_count * length
    slot_ids = jnp.where(
        token_base >= 0, token_base + offset[:, :, None], experts * cap_slots
    ).reshape(tokens, 2)
    pair_index = lax.broadcasted_iota(jnp.int32, (tokens, 2), 0) * 2 + lax.broadcasted_iota(
        jnp.int32, (tokens, 2), 1
    )
    pair_source = (
        jnp.full((experts * cap_slots,), 2 * tokens, jnp.int32)
        .at[slot_ids.reshape(-1)]
        .set(pair_index.reshape(-1), mode="drop")
    )
    task_tok = jnp.sum(member * task_ids[:, None, :], axis=2).reshape(tokens)
    expert_tok = jnp.sum(
        member[:, :, :, None] * pair_expert.reshape(pack_count, 1, sentences, 2), axis=2
    ).reshape(tokens, 2)
    return (slot_ids, pair_source, task_tok, expert_tok, segment)


def score_block(query_rows, key_rows, query_segment, key_segment, score_scale):
    scores = (
        jnp.einsum("qhd,khd->hqk", query_rows, key_rows, preferred_element_type=jnp.float32)
        * score_scale
    )
    return jnp.where((query_segment[:, None] == key_segment[None, :])[None], scores, blocked)


def attention_core(qkv, segment):
    pack_count, length = segment.shape
    block_rows = min(512, length)
    block_count = length // block_rows
    qkv_grid = qkv.reshape(pack_count, length, 3, HEADS, -1)
    score_scale = qkv_grid.shape[-1] ** (-0.5)

    def one_pack(inputs):
        pack_qkv, pack_segment = inputs
        key_rows = pack_qkv[:, 1]
        value_rows = pack_qkv[:, 2]
        query_blocks = pack_qkv[:, 0].reshape(block_count, block_rows, HEADS, -1)
        segment_blocks = pack_segment.reshape(block_count, block_rows)

        def one_block(block_inputs):
            query_rows, query_segment = block_inputs
            scores = score_block(query_rows, key_rows, query_segment, pack_segment, score_scale)
            row_max = jnp.max(scores, axis=-1, keepdims=True)
            raised = jnp.exp(scores - row_max)
            row_total = jnp.sum(raised, axis=-1, keepdims=True)
            soft_weights = (raised / row_total).astype(jnp.bfloat16)
            context = jnp.einsum(
                "hqk,khd->qhd", soft_weights, value_rows, preferred_element_type=jnp.float32
            )
            return (context.astype(jnp.bfloat16), row_max + jnp.log(row_total))

        context, log_total = lax.map(one_block, (query_blocks, segment_blocks))
        return (context.reshape(length, -1), log_total)

    context, log_total = lax.map(one_pack, (qkv_grid, segment))
    return (context.reshape(pack_count * length, -1), log_total)


def attention_back(qkv, segment, log_total, grad_context):
    pack_count, length = segment.shape
    block_rows = min(512, length)
    block_count = length // block_rows
    qkv_grid = qkv.reshape(pack_count, length, 3, HEADS, -1)
    score_scale = qkv_grid.shape[-1] ** (-0.5)
    grad_grid = grad_context.reshape(pack_count, block_count, block_rows, HEADS, -1)

    def one_pack(inputs):
        pack_qkv, pack_segment, pack_total, pack_grad = inputs
        key_rows = pack_qkv[:, 1]
        value_rows = pack_qkv[:, 2]
        query_blocks = pack_qkv[:, 0].reshape(block_count, block_rows, HEADS, -1)
        segment_blocks = pack_segment.reshape(block_count, block_rows)

        def step(carry, block_inputs):
            grad_keys, grad_values = carry
            query_rows, query_segment, row_total, grad_rows = block_inputs
            scores = score_block(query_rows, key_rows, query_segment, pack_segment, score_scale)
            soft_weights = jnp.exp(scores - row_total)
            grad_values = grad_values + jnp.einsum(
                "hqk,qhd->khd",
                soft_weights.astype(jnp.bfloat16),
                grad_rows,
                preferred_element_type=jnp.float32,
            )
            grad_weights = jnp.einsum(
                "qhd,khd->hqk", grad_rows, value_rows, preferred_element_type=jnp.float32
            )
            row_delta = jnp.sum(grad_weights * soft_weights, axis=-1, keepdims=True)
            grad_scores = (soft_weights * (grad_weights - row_delta)).astype(jnp.bfloat16)
            grad_query = (
                jnp.einsum(
                    "hqk,khd->qhd", grad_scores, key_rows, preferred_element_type=jnp.float32
                )
                * score_scale
            )
            grad_keys = (
                grad_keys
                + jnp.einsum(
                    "hqk,qhd->khd", grad_scores, query_rows, preferred_element_type=jnp.float32
                )
                * score_scale
            )
            return ((grad_keys, grad_values), grad_query)

        zero_rows = jnp.zeros(key_rows.shape, jnp.float32)
        (grad_keys, grad_values), grad_query = lax.scan(
            step, (zero_rows, zero_rows), (query_blocks, segment_blocks, pack_total, pack_grad)
        )
        return jnp.stack(
            [grad_query.reshape(length, HEADS, -1), grad_keys, grad_values], axis=1
        ).astype(jnp.bfloat16)

    grad_qkv = lax.map(one_pack, (qkv_grid, segment, log_total, grad_grid))
    return grad_qkv.reshape(pack_count * length, -1)


def attention_forward(hidden, gain, shift, w_qkv_layer, w_attn_layer, segment):
    normed_low = norm_rows(hidden, gain, shift).astype(jnp.bfloat16)
    qkv = jnp.dot(normed_low, w_qkv_layer, preferred_element_type=jnp.float32).astype(jnp.bfloat16)
    context, log_total = attention_core(qkv, segment)
    return (
        jnp.dot(context, w_attn_layer, preferred_element_type=jnp.float32),
        (normed_low, qkv, context, log_total),
    )


def attention_layer_back(hidden, gain, shift, w_qkv_layer, w_attn_layer, segment, saved, grad_out):
    normed_low, qkv, context, log_total = saved
    grad_low = grad_out.astype(jnp.bfloat16)
    grad_attn_w = outer_sum(context, grad_low)
    grad_context = times_back(grad_low, w_attn_layer).astype(jnp.bfloat16)
    grad_qkv = attention_back(qkv, segment, log_total, grad_context)
    grad_qkv_w = outer_sum(normed_low, grad_qkv)
    grad_normed = times_back(grad_qkv, w_qkv_layer)
    grad_hidden, grad_gain, grad_shift = norm_back(hidden, gain, shift, grad_normed)
    return (grad_out + grad_hidden, grad_gain, grad_shift, grad_qkv_w, grad_attn_w)


def feed_forward(hidden, gain, shift, up_weight, down_weight):
    normed_low = norm_rows(hidden, gain, shift).astype(jnp.bfloat16)
    inner_act = jnp.dot(normed_low, up_weight, preferred_element_type=jnp.float32)
    active = jax.nn.gelu(inner_act).astype(jnp.bfloat16)
    return (
        jnp.dot(active, down_weight, preferred_element_type=jnp.float32),
        (normed_low, inner_act, active),
    )


def feed_layer_back(hidden, gain, shift, up_weight, down_weight, saved, grad_out):
    normed_low, inner_act, active = saved
    grad_low = grad_out.astype(jnp.bfloat16)
    grad_down_w = outer_sum(active, grad_low)
    grad_active = times_back(grad_low, down_weight)
    grad_inner = gelu_back(inner_act, grad_active).astype(jnp.bfloat16)
    grad_up_w = outer_sum(normed_low, grad_inner)
    grad_normed = times_back(grad_inner, up_weight)
    grad_hidden, grad_gain, grad_shift = norm_back(hidden, gain, shift, grad_normed)
    return (grad_out + grad_hidden, grad_gain, grad_shift, grad_up_w, grad_down_w)


def expert_hidden(rows_in, up_experts):
    inner_act = jnp.einsum("erd,edf->erf", rows_in, up_experts, preferred_element_type=jnp.float32)
    return (inner_act, jax.nn.gelu(inner_act).astype(jnp.bfloat16))


def local(
    hidden_in,
    lengths,
    task_ids,
    task_experts,
    capacity,
    task_logits,
    norm_params,
    w_qkv,
    w_attn,
    w_up,
    w_down,
    expert_up,
    expert_down,
    cotangent,
):
    experts = capacity.shape[0]
    tok_rows = hidden_in.shape[0]
    cap_slots = max(4 * tok_rows // experts, 2 * MOST_LEN)
    slot_ids, pair_source, task_tok, expert_tok, segment = route_block(
        lengths, task_ids, task_experts, capacity, cap_slots, PACK
    )
    dense_set = (
        lax.all_gather(norm_params, "dp", axis=0, tiled=True),
        lax.all_gather(w_qkv, "dp", axis=0, tiled=True),
        lax.all_gather(w_attn, "dp", axis=0, tiled=True),
        lax.all_gather(w_up, "dp", axis=0, tiled=True),
        lax.all_gather(w_down, "dp", axis=0, tiled=True),
    )
    params = dense_set[0].astype(jnp.float32)
    hidden_zero = hidden_in.astype(jnp.float32)
    attn_one, saved_one = attention_forward(
        hidden_zero, params[:, 0], params[:, 1], dense_set[1][:, 0], dense_set[2][:, 0], segment
    )
    hidden_one = hidden_zero + attn_one
    feed_out, saved_feed = feed_forward(
        hidden_one, params[:, 2], params[:, 3], dense_set[3], dense_set[4]
    )
    hidden_two = hidden_one + feed_out
    attn_two, saved_two = attention_forward(
        hidden_two, params[:, 4], params[:, 5], dense_set[1][:, 1], dense_set[2][:, 1], segment
    )
    hidden_three = hidden_two + attn_two
    normed_moe = norm_rows(hidden_three, params[:, 6], params[:, 7]).astype(jnp.bfloat16)
    padded = jnp.concatenate([normed_moe, jnp.zeros((1, D), jnp.bfloat16)], axis=0)
    buffer = padded[pair_source // 2].reshape(experts, cap_slots, D)
    received = lax.all_to_all(buffer, "expert", split_axis=0, concat_axis=1, tiled=True)
    up_experts, down_experts = (
        lax.all_gather(expert_up, "dp", axis=1, tiled=True),
        lax.all_gather(expert_down, "dp", axis=1, tiled=True),
    )
    inner_act, active = expert_hidden(received, up_experts)
    result = jnp.einsum(
        "erf,efd->erd", active, down_experts, preferred_element_type=jnp.float32
    ).astype(jnp.bfloat16)
    returned = lax.all_to_all(result, "expert", split_axis=1, concat_axis=0, tiled=True)
    flat_out = jnp.concatenate([returned.reshape(-1, D), jnp.zeros((1, D), jnp.bfloat16)], axis=0)
    pair_out = flat_out[slot_ids]
    task_hot = (
        task_tok[:, None] == lax.broadcasted_iota(jnp.int32, (1, task_logits.shape[0]), 1)
    ).astype(jnp.float32)
    expert_hot = (
        expert_tok[:, :, None] == lax.broadcasted_iota(jnp.int32, (1, 1, experts), 2)
    ).astype(jnp.float32)
    gate_table = jnp.dot(task_hot, task_logits, precision=highest)
    logits = jnp.sum(gate_table[:, None, :] * expert_hot, axis=2)
    gate_vals = jax.nn.softmax(logits, axis=-1)
    hidden_out = hidden_three + jnp.sum(gate_vals[:, :, None] * pair_out, axis=1)
    grad_out = cotangent.astype(jnp.float32)
    gate_grad = jnp.sum(grad_out[:, None, :] * pair_out, axis=2)
    logit_grad = gate_vals * (gate_grad - jnp.sum(gate_vals * gate_grad, axis=1, keepdims=True))
    table_grad = jnp.sum(logit_grad[:, :, None] * expert_hot, axis=1)
    logits_part = lax.dot_general(task_hot, table_grad, (((0,), (0,)), ((), ())), precision=highest)
    pair_grad = (gate_vals[:, :, None] * grad_out[:, None, :]).astype(jnp.bfloat16).reshape(-1, D)
    pair_grad = jnp.concatenate([pair_grad, jnp.zeros((1, D), jnp.bfloat16)], axis=0)
    grad_buffer = pair_grad[pair_source].reshape(experts, cap_slots, D)
    grad_received = lax.all_to_all(grad_buffer, "expert", split_axis=0, concat_axis=1, tiled=True)
    rows_back, inner_back, active_back = (received, inner_act, active)
    grad_down_experts = jnp.einsum(
        "erf,erd->efd", active_back, grad_received, preferred_element_type=jnp.float32
    )
    grad_active = jnp.einsum(
        "erd,efd->erf", grad_received, down_experts, preferred_element_type=jnp.float32
    )
    grad_inner = gelu_back(inner_back, grad_active).astype(jnp.bfloat16)
    grad_up_experts = jnp.einsum(
        "erd,erf->edf", rows_back, grad_inner, preferred_element_type=jnp.float32
    )
    grad_rows = jnp.einsum(
        "erf,edf->erd", grad_inner, up_experts, preferred_element_type=jnp.float32
    ).astype(jnp.bfloat16)
    grad_returned = lax.all_to_all(grad_rows, "expert", split_axis=1, concat_axis=0, tiled=True)
    grad_flat = jnp.concatenate(
        [grad_returned.reshape(-1, D), jnp.zeros((1, D), jnp.bfloat16)], axis=0
    )
    grad_normed_moe = jnp.sum(grad_flat[slot_ids].astype(jnp.float32), axis=1)
    grad_hidden, gain_four, shift_four = norm_back(
        hidden_three, params[:, 6], params[:, 7], grad_normed_moe
    )
    grad_hidden = grad_out + grad_hidden
    expert_up_sum, expert_down_sum = (
        lax.psum_scatter(
            grad_up_experts.astype(jnp.bfloat16), "dp", scatter_dimension=1, tiled=True
        ).astype(jnp.float32),
        lax.psum_scatter(
            grad_down_experts.astype(jnp.bfloat16), "dp", scatter_dimension=1, tiled=True
        ).astype(jnp.float32),
    )
    back_set = (
        lax.all_gather(norm_params, "dp", axis=0, tiled=True),
        lax.all_gather(w_qkv, "dp", axis=0, tiled=True),
        lax.all_gather(w_attn, "dp", axis=0, tiled=True),
        lax.all_gather(w_up, "dp", axis=0, tiled=True),
        lax.all_gather(w_down, "dp", axis=0, tiled=True),
    )
    back_params = back_set[0].astype(jnp.float32)
    grad_hidden, gain_three, shift_three, qkv_two, attn_w_two = attention_layer_back(
        hidden_two,
        back_params[:, 4],
        back_params[:, 5],
        back_set[1][:, 1],
        back_set[2][:, 1],
        segment,
        saved_two,
        grad_hidden,
    )
    grad_hidden, gain_two, shift_two, up_w_grad, down_w_grad = feed_layer_back(
        hidden_one,
        back_params[:, 2],
        back_params[:, 3],
        back_set[3],
        back_set[4],
        saved_feed,
        grad_hidden,
    )
    grad_hidden, gain_one, shift_one, qkv_one, attn_w_one = attention_layer_back(
        hidden_zero,
        back_params[:, 0],
        back_params[:, 1],
        back_set[1][:, 0],
        back_set[2][:, 0],
        segment,
        saved_one,
        grad_hidden,
    )
    norm_grad = jnp.stack(
        [gain_one, shift_one, gain_two, shift_two, gain_three, shift_three, gain_four, shift_four],
        axis=1,
    )
    qkv_grad = jnp.stack([qkv_one, qkv_two], axis=1)
    attn_grad = jnp.stack([attn_w_one, attn_w_two], axis=1)
    norm_part, qkv_part, attn_part, up_part, down_part = (
        lax.psum_scatter(
            norm_grad.astype(jnp.bfloat16), "dp", scatter_dimension=0, tiled=True
        ).astype(jnp.float32),
        lax.psum_scatter(
            qkv_grad.astype(jnp.bfloat16), "dp", scatter_dimension=0, tiled=True
        ).astype(jnp.float32),
        lax.psum_scatter(
            attn_grad.astype(jnp.bfloat16), "dp", scatter_dimension=0, tiled=True
        ).astype(jnp.float32),
        lax.psum_scatter(
            up_w_grad.astype(jnp.bfloat16), "dp", scatter_dimension=0, tiled=True
        ).astype(jnp.float32),
        lax.psum_scatter(
            down_w_grad.astype(jnp.bfloat16), "dp", scatter_dimension=0, tiled=True
        ).astype(jnp.float32),
    )
    norm_total, qkv_total, attn_total, up_total, down_total = (
        lax.psum(norm_part.astype(jnp.bfloat16), "expert").astype(jnp.float32),
        lax.psum(qkv_part.astype(jnp.bfloat16), "expert").astype(jnp.float32),
        lax.psum(attn_part.astype(jnp.bfloat16), "expert").astype(jnp.float32),
        lax.psum(up_part.astype(jnp.bfloat16), "expert").astype(jnp.float32),
        lax.psum(down_part.astype(jnp.bfloat16), "expert").astype(jnp.float32),
    )
    logits_total = lax.psum(logits_part, ("dp", "expert"))
    return (
        hidden_out.astype(jnp.bfloat16),
        grad_hidden,
        logits_total,
        norm_total,
        qkv_total,
        attn_total,
        up_total,
        down_total,
        expert_up_sum,
        expert_down_sum,
    )


def solution(mesh):
    in_specs = (
        P(("dp", "expert"), None),
        P(("dp", "expert"), None),
        P(("dp", "expert"), None),
        P(),
        P(),
        P(),
        P("dp", None),
        P("dp", None, None),
        P("dp", None, None),
        P("dp", None),
        P("dp", None),
        P("expert", "dp", None),
        P("expert", "dp", None),
        P(("dp", "expert"), None),
    )
    out_specs = (
        P(("dp", "expert"), None),
        P(("dp", "expert"), None),
        P(),
        P("dp", None),
        P("dp", None, None),
        P("dp", None, None),
        P("dp", None),
        P("dp", None),
        P("expert", "dp", None),
        P("expert", "dp", None),
    )
    return jax.shard_map(local, mesh=mesh, in_specs=in_specs, out_specs=out_specs, check_vma=False)
```

profile of v0, /device:TPU:0, one launch (start us, length us, event | category | flops | bytes accessed | tf_op | source)
XLA Modules:
  0.0 1248.1 jit_solution(17386343798769740064)
XLA Ops:
  13.6 13.7 %all_gather.26 = bf16[512,8]{0,1:T(8,128)(2,1)S(1)} all-gather(bf16[128,8]{0,1:T(8,128)(2,1)S(1)} %copy-done.116), channel_id=1, replica_groups=mesh['dp'=4,'expert'=8] {'dp'}, dimensions={0}, use_global_device_ids=true | all-gather | bytes 10240 | tf_op jit(solution)/shard_map/all_gather | solution.py:265
  40.2 36.2 %all-gather.7.cloned.1.call-done = bf16[512,2,1536]{2,0,1:T(8,128)(2,1)} async-done(((bf16[128,2,1536]{2,0,1:T(8,128)(2,1)}), bf16[512,2,1536]{2,0,1:T(8,128)(2,1)}) %all-gather.7.cloned.1.call-update) | async-done | bytes 3145744 | tf_op jit(solution)/shard_map/all_gather | solution.py:266
  93.2 29.0 %while.90 = (s32[]{:T(128)}, bf16[2,512,8,64]{1,3,2,0:T(8,128)(2,1)}, f32[2,8,512,1]{2,1,3,0:T(8,128)}, s32[2,512]{1,0:T(2,128)S(1)}, s32[1024]{0:T(1024)S(1)}, ...) while((s32[]{:T(128)}, ...), condition=%wide.region_7.8_spmd, body=%wide.region_4.0_spmd.sunk | while | flops 1124855808 | bytes 64104620 | solution.py:128
  129.6 22.6 %all-gather.11.cloned.1.call-done = bf16[512,2048]{1,0:T(8,128)(2,1)} async-done(((bf16[128,2048]{1,0:T(8,128)(2,1)}), bf16[512,2048]{1,0:T(8,128)(2,1)}) %all-gather.11.cloned.1.call-update) | async-done | bytes 2097168 | tf_op jit(solution)/shard_map/all_gather | solution.py:268
  159.6 38.8 %all-gather.13.cloned.1.call-done = bf16[2048,512]{1,0:T(8,128)(2,1)} async-done(((bf16[512,512]{1,0:T(8,128)(2,1)}), bf16[2048,512]{1,0:T(8,128)(2,1)}) %all-gather.13.cloned.1.call-update) | async-done | bytes 2097168 | tf_op jit(solution)/shard_map/all_gather | solution.py:269
  217.2 29.4 %while.91 = (s32[]{:T(128)}, bf16[2,512,8,64]{1,3,2,0:T(8,128)(2,1)}, f32[2,8,512,1]{2,1,3,0:T(8,128)S(1)}, s32[2,512]{1,0:T(2,128)S(1)}, s32[1024]{0:T(1024)S(1...) while((s32[]{:T(128)}, ...), condition=%wide.region_15.16_spmd, body=%wide.region_12.15_spmd.sunk | while | flops 1124855808 | bytes 64104620 | solution.py:128
  253.2 17.4 %gather_fusion = bf16[4096,512]{1,0:T(8,128)(2,1)} fusion(bf16[1025,512]{1,0:T(8,128)(2,1)S(1)} %concatenate.12, s32[4096]{0:T(1024)S(1)} %copy-done.74), kind=kCustom, calls=%fused_computation | custom fusion | bytes 8404992 | tf_op jit(solution)/shard_map/gather | solution.py:287
  290.7 17.3 %gather_fusion.2 = bf16[4096,512]{1,0:T(8,128)(2,1)} fusion(bf16[2049,512]{1,0:T(8,128)(2,1)S(1)} %concatenate.14, s32[4096]{0:T(1024)S(1)} %copy-done.73), kind=kCustom, calls=%fused_computation.2 | custom fusion | bytes 8404992 | tf_op jit(solution)/shard_map/gather | solution.py:317
  308.0 16.4 %all-to-all-done = bf16[8,512,512]{2,1,0:T(8,128)(2,1)} async-done(((bf16[8,512,512]{2,1,0:T(8,128)(2,1)}), bf16[8,512,512]{2,1,0:T(8,128)(2,1)}, u32[]{:S(2)}, u32[]{:S(2)}) %all-to-all-start) | async-done | bytes 4194336 | tf_op jit(solution)/shard_map/all_to_all | solution.py:288
  329.6 23.7 %multiply_convert_fusion.2 = (bf16[4096,2048]{1,0:T(8,128)(2,1)}, f32[4096,2048]{1,0:T(8,128)}) fusion(bf16[4096,512]{1,0:T(8,128)(2,1)} %bitcast.34, bf16[1,512,2048]{2,1,0:T(8,128)(2,1)} %all-gather.15.cloned.1.call-done), kind=kOutput, calls=%fused_computation.100 | convolution fusion | flops 8665432064 | bytes 56623104 | tf_op jit(solution)/shard_map/erd,edf->erf/dot_general | solution.py:238
  353.3 22.9 %all-gather.17.cloned.1.call-done = bf16[1,2048,512]{2,1,0:T(8,128)(2,1)} async-done(((bf16[1,512,512]{2,1,0:T(8,128)(2,1)}), bf16[1,2048,512]{2,1,0:T(8,128)(2,1)}) %all-gather.17.cloned.1.call-update) | async-done | bytes 2097168 | tf_op jit(solution)/shard_map/all_gather | solution.py:291
  378.2 32.0 %fusion.66 = bf16[4096,2048]{1,0:T(8,128)(2,1)} fusion(f32[4096,2048]{1,0:T(8,128)} %get-tuple-element.772, bf16[4096,512]{1,0:T(8,128)(2,1)} %bitcast.40, bf16[1,2048,512]{2,1,0:T(8,128)(2,1)} %all-gather.17.cloned.1.call-done), kind=kOutput, calls=%fused_computation.99 | convolution fusion | flops 8757706752 | bytes 56623104 | tf_op jit(solution)/shard_map/erd,efd->erf/dot_general | solution.py:323
  410.2 12.8 %fusion.75 = bf16[1,4096,512]{2,1,0:T(8,128)(2,1)S(1)} fusion(bf16[4096,2048]{1,0:T(8,128)(2,1)} %fusion.66, bf16[1,512,2048]{2,1,0:T(8,128)(2,1)S(1)} %copy-done.135), kind=kOutput, calls=%fused_computation.116 | convolution fusion | flops 8592031744 | bytes 23068672 | tf_op jit(solution)/shard_map/erf,edf->erd/dot_general | solution.py:330
  423.0 36.4 %copy.210 = bf16[1,4096,512]{2,0,1:T(2,128)(2,1)} copy(bf16[1,4096,512]{2,1,0:T(8,128)(2,1)S(1)} %fusion.75) | data formatting | bytes 8388608 | tf_op jit(solution)/shard_map/convert_element_type | solution.py:332
  459.9 28.6 %reduce.9 = bf16[4096,512]{1,0:T(8,128)(2,1)} reduce(bf16[4096,1,512]{2,1,0:T(2,128)(2,1)} %bitcast.327, bf16[]{:T(256)} %broadcast.882), dimensions={1}, to_apply=%bitcast.242.reduce_sub_computation | reduce | bytes 8388610
  501.5 12.5 fusion.74
  513.9 36.4 %copy.211 = bf16[1,4096,512]{2,0,1:T(2,128)(2,1)} copy(bf16[1,4096,512]{2,1,0:T(8,128)(2,1)S(1)} %fusion.74) | data formatting | bytes 8388608 | tf_op jit(solution)/shard_map/convert_element_type | solution.py:296
  550.4 28.6 %reduce.10 = bf16[4096,512]{1,0:T(8,128)(2,1)} reduce(bf16[4096,1,512]{2,1,0:T(2,128)(2,1)} %bitcast.328, bf16[]{:T(256)} %broadcast.882), dimensions={1}, to_apply=%bitcast.243.reduce_sub_computation | reduce | bytes 8388610
  656.6 12.0 gather_fusion.1
  696.4 119.4 %while.92 = (s32[]{:T(128)}, f32[1024,8,64]{0,2,1:T(8,128)}, f32[1024,8,64]{0,2,1:T(8,128)}, bf16[2,512,8,64]{1,0,3,2:T(2,128)(2,1)}, bf16[2,512,8,64]{1,3,2,0:T...) while((s32[]{:T(128)}, f32[1024,8,64]{0,2,1:T(8,128)}, ...), condition=%wide.region_36.37_spmd.clone, body=%wide.region_34.36_spmd.clone.sunk | while | flops 2725769216 | bytes 180971728 | solution.py:182
  736.2 18.4 %dynamic_update_slice.52 = bf16[2,512,8,64]{1,0,3,2:T(2,128)(2,1)} dynamic-update-slice(bf16[2,512,8,64]{1,0,3,2:T(2,128)(2,1)} %get-tuple-element.1094, bf16[1,512,8,64]{1,0,3,2:T(2,128)(2,1)S(1)} %copy.214, s32[]{:T(128)S(6)} %copy.244, s32[]{:T(128)} %constant.211.clone.1..sunk, s32[]{:T(128)} %constant.211.clone.1..sunk, s32[]{:T(128)} %constant.211.clone.1..sunk) | dynamic-update-slice | bytes 1048580 | tf_op jit(solution)/shard_map/while/body/eval_jaxpr/while/body/jit(dynamic_update_index_in_dim)/dynamic_update_slice | solution.py:182
  797.2 18.4 %dynamic_update_slice.52 = bf16[2,512,8,64]{1,0,3,2:T(2,128)(2,1)} dynamic-update-slice(bf16[2,512,8,64]{1,0,3,2:T(2,128)(2,1)} %get-tuple-element.1094, bf16[1,512,8,64]{1,0,3,2:T(2,128)(2,1)S(1)} %copy.214, s32[]{:T(128)S(6)} %copy.244, s32[]{:T(128)} %constant.211.clone.1..sunk, s32[]{:T(128)} %constant.211.clone.1..sunk, s32[]{:T(128)} %constant.211.clone.1..sunk) | dynamic-update-slice | bytes 1048580 | tf_op jit(solution)/shard_map/while/body/eval_jaxpr/while/body/jit(dynamic_update_index_in_dim)/dynamic_update_slice | solution.py:182
  866.9 119.7 %while.93 = (s32[]{:T(128)}, f32[1024,8,64]{0,2,1:T(8,128)}, f32[1024,8,64]{0,2,1:T(8,128)}, bf16[2,512,8,64]{1,0,3,2:T(2,128)(2,1)}, bf16[2,512,8,64]{1,3,2,0:T...) while((s32[]{:T(128)}, f32[1024,8,64]{0,2,1:T(8,128)}, ...), condition=%wide.region_43.44_spmd.clone, body=%wide.region_41.43_spmd.clone.sunk | while | flops 2725769216 | bytes 180971728 | solution.py:182
  906.9 18.4 %dynamic_update_slice.53 = bf16[2,512,8,64]{1,0,3,2:T(2,128)(2,1)} dynamic-update-slice(bf16[2,512,8,64]{1,0,3,2:T(2,128)(2,1)} %get-tuple-element.1133, bf16[1,512,8,64]{1,0,3,2:T(2,128)(2,1)S(1)} %copy.215, s32[]{:T(128)S(6)} %copy.256, s32[]{:T(128)} %constant.211.clone.1..sunk.1, s32[]{:T(128)} %constant.211.clone.1..sunk.1, s32[]{:T(128)} %constant.211.clone.1..sunk.1) | dynamic-update-slice | bytes 1048580 | tf_op jit(solution)/shard_map/while/body/eval_jaxpr/while/body/jit(dynamic_update_index_in_dim)/dynamic_update_slice | solution.py:182
  968.0 18.4 %dynamic_update_slice.53 = bf16[2,512,8,64]{1,0,3,2:T(2,128)(2,1)} dynamic-update-slice(bf16[2,512,8,64]{1,0,3,2:T(2,128)(2,1)} %get-tuple-element.1133, bf16[1,512,8,64]{1,0,3,2:T(2,128)(2,1)S(1)} %copy.215, s32[]{:T(128)S(6)} %copy.256, s32[]{:T(128)} %constant.211.clone.1..sunk.1, s32[]{:T(128)} %constant.211.clone.1..sunk.1, s32[]{:T(128)} %constant.211.clone.1..sunk.1) | dynamic-update-slice | bytes 1048580 | tf_op jit(solution)/shard_map/while/body/eval_jaxpr/while/body/jit(dynamic_update_index_in_dim)/dynamic_update_slice | solution.py:182
  1010.5 14.8 %fusion.81 = bf16[1,2048,512]{2,1,0:T(8,128)(2,1)} fusion(bf16[4096,2048]{1,0:T(8,128)(2,1)} %get-tuple-element.771, bf16[4096,512]{1,0:T(8,128)(2,1)} %bitcast.40), kind=kOutput, calls=%fused_computation.143 | convolution fusion | flops 8590983168 | bytes 23068672 | tf_op jit(solution)/shard_map/erf,erd->efd/dot_general | solution.py:320
  1025.4 14.7 %fusion.80 = bf16[1,512,2048]{2,1,0:T(8,128)(2,1)} fusion(bf16[4096,512]{1,0:T(8,128)(2,1)} %bitcast.34, bf16[4096,2048]{1,0:T(8,128)(2,1)} %fusion.66), kind=kOutput, calls=%fused_computation.142 | convolution fusion | flops 8590983168 | bytes 23068672 | tf_op jit(solution)/shard_map/erd,erf->edf/dot_general | solution.py:327
  1041.7 15.5 %reduce-scatter.10.cloned.1.call-done = bf16[128,2,1536]{2,0,1:T(8,128)(2,1)} async-done(((bf16[512,2,1536]{2,0,1:T(8,128)(2,1)}), bf16[128,2,1536]{2,0,1:T(8,128)(2,1)}) %reduce-scatter.10.cloned.1.call-update) | async-done | bytes 786448 | tf_op jit(solution)/shard_map/reduce_scatter | solution.py:397
  1057.7 40.3 %psum.42 = f32[30,8]{0,1:T(8,128)} all-reduce(f32[30,8]{0,1:T(8,128)S(1)} %fusion.106), channel_id=1, replica_groups=mesh['dp'=4,'expert'=8] {'dp','expert'}, use_global_device_ids=true, to_apply=%region_49.50 | all-reduce | flops 240 | bytes 1920 | tf_op jit(solution)/shard_map/psum | solution.py:417
  1102.1 13.0 %psum.43 = bf16[128,8]{0,1:T(8,128)(2,1)S(1)} all-reduce(bf16[128,8]{0,1:T(8,128)(2,1)S(1)} %copy.165), channel_id=1, replica_groups=mesh['dp'=4,'expert'=8] {'expert'}, use_global_device_ids=true, to_apply=%region_59.60 | all-reduce | flops 1024 | bytes 4096 | tf_op jit(solution)/shard_map/psum | solution.py:411
  1125.8 43.5 %reduce-scatter.18.cloned.1.call-done = bf16[1,128,2048]{2,1,0:T(8,128)(2,1)} async-done(((bf16[1,512,2048]{2,1,0:T(8,128)(2,1)}), bf16[1,128,2048]{2,1,0:T(8,128)(2,1)}) %reduce-scatter.18.cloned.1.call-update) | async-done | bytes 524304 | tf_op jit(solution)/shard_map/reduce_scatter | solution.py:343
  1171.5 62.4 %all-reduce.7.cloned.1.call-done = (bf16[128,2,1536]{2,0,1:T(8,128)(2,1)}, bf16[128,2,512]{2,0,1:T(8,128)(2,1)}, bf16[128,2048]{1,0:T(8,128)(2,1)}, bf16[512,512]{1,0:T(8,128)(2,1)}) async-done(((bf16[128,2,1536]{2,0,1:T(8,128)(2,1)}, bf16[128,2,512]{2,0,1:T(8,128)(2,1)}, bf16[128,2048]{1,0:T(8,128)(2,1)}, bf16[512,512]{1,0:T(8,128)(2,1)}), (bf16[128,2,1536]{2,0,1:T(8,128)(2,1)}, ...) | async-done | bytes 2097168 | tf_op jit(solution)/shard_map/psum | solution.py:412
  (574 shorter events, 544.1 us)
Async XLA Ops:
  7.2 268.7 %copy-start = (f32[30,8]{0,1:T(8,128)S(1)}, f32[30,8]{0,1:T(8,128)}, u32[]{:S(2)}) copy-start(f32[30,8]{0,1:T(8,128)} %param.27) | copy-start | bytes 2884
  7.2 69.2 %all-gather.7.cloned.1.call-start = ((), (), s32[]{:S(2)}) async-start(), calls=%async_computation.11 | async-start | bytes 3932160 | tf_op jit(solution)/shard_map/all_gather | solution.py:266
  9.5 117.1 %all-gather.9.cloned.1.call-start = ((), (), s32[]{:S(2)}) async-start(), calls=%async_computation.12 | async-start | bytes 1310720 | tf_op jit(solution)/shard_map/all_gather | solution.py:267
  10.3 141.9 %all-gather.11.cloned.1.call-start = ((), (), s32[]{:S(2)}) async-start(), calls=%async_computation.13 | async-start | bytes 2621440 | tf_op jit(solution)/shard_map/all_gather | solution.py:268
  11.1 187.3 %all-gather.13.cloned.1.call-start = ((), (), s32[]{:S(2)}) async-start(), calls=%async_computation.14 | async-start | bytes 2621440 | tf_op jit(solution)/shard_map/all_gather | solution.py:269
  12.3 64.2 %copy-start.69 = (f32[1024]{0:T(1024)}, f32[1024]{0:T(1024)S(1)}, u32[]{:S(2)}) copy-start(f32[1024]{0:T(1024)S(1)} %broadcast_multiply_fusion.3) | copy-start | bytes 12292
  12.8 68.5 %copy-start.77 = (f32[1024]{0:T(1024)}, f32[1024]{0:T(1024)S(1)}, u32[]{:S(2)}) copy-start(f32[1024]{0:T(1024)S(1)} %fusion.121) | copy-start | bytes 12292
  13.6 67.8 %copy-start.83 = (s32[1024]{0:T(1024)}, s32[1024]{0:T(1024)S(1)}, u32[]{:S(2)}) copy-start(s32[1024]{0:T(1024)S(1)} %iota_subtract_fusion) | copy-start | bytes 12292
  27.9 53.5 %copy-start.96 = (f32[512,1]{0,1:T(1,128)}, f32[512,1]{0,1:T(1,128)S(1)}, u32[]{:S(2)}) copy-start(f32[512,1]{0,1:T(1,128)S(1)} %get-tuple-element.763) | copy-start | bytes 6148
  27.9 53.5 %copy-start.119 = (f32[512,1]{0,1:T(1,128)}, f32[512,1]{0,1:T(1,128)S(1)}, u32[]{:S(2)}) copy-start(f32[512,1]{0,1:T(1,128)S(1)} %get-tuple-element.764) | copy-start | bytes 6148
  29.9 51.4 %copy-start.65 = (s32[1024,2]{0,1:T(2,128)}, s32[1024,2]{0,1:T(2,128)S(1)}, u32[]{:S(2)}) copy-start(s32[1024,2]{0,1:T(2,128)S(1)} %get-tuple-element.649) | copy-start | bytes 24580
  129.1 69.2 %copy-start.27 = (f32[1024,512]{1,0:T(8,128)}, f32[1024,512]{1,0:T(8,128)S(1)}, u32[]{:S(2)}) copy-start(f32[1024,512]{1,0:T(8,128)S(1)} %get-tuple-element.766) | copy-start | bytes 6291460
  129.1 23.1 %copy-start.109 = (f32[512,1]{0,1:T(1,128)S(1)}, f32[512,1]{0,1:T(1,128)}, u32[]{:S(2)}) copy-start(f32[512,1]{0,1:T(1,128)} %get-tuple-element.761) | copy-start | bytes 6148
  129.2 30.4 %copy-start.92 = (f32[1024]{0:T(1024)}, f32[1024]{0:T(1024)S(1)}, u32[]{:S(2)}) copy-start(f32[1024]{0:T(1024)S(1)} %broadcast_multiply_fusion.2) | copy-start | bytes 12292
  129.6 30.0 %copy-start.81 = (f32[1024]{0:T(1024)}, f32[1024]{0:T(1024)S(1)}, u32[]{:S(2)}) copy-start(f32[1024]{0:T(1024)S(1)} %multiply_reduce_fusion.12) | copy-start | bytes 12292
  129.6 29.9 %copy-start.103 = (f32[1024]{0:T(1024)}, f32[1024]{0:T(1024)S(1)}, u32[]{:S(2)}) copy-start(f32[1024]{0:T(1024)S(1)} %fusion.122) | copy-start | bytes 12292
  270.6 53.8 %all-to-all-start = ((bf16[8,512,512]{2,1,0:T(8,128)(2,1)}), bf16[8,512,512]{2,1,0:T(8,128)(2,1)}, u32[]{:S(2)}, u32[]{:S(2)}) async-start(bf16[8,512,512]{2,1,0:T(8,128)(2,1)} %bitcast.333), calls=%async_computation | async-start | bytes 8388608 | tf_op jit(solution)/shard_map/all_to_all | solution.py:288
  275.3 54.3 %all-gather.15.cloned.1.call-start = ((), (), s32[]{:S(2)}) async-start(), calls=%async_computation.15 | async-start | bytes 2621440 | tf_op jit(solution)/shard_map/all_gather | solution.py:290
  324.4 53.7 %all-to-all-start.2 = ((bf16[8,512,512]{2,1,0:T(8,128)(2,1)}), bf16[8,512,512]{2,1,0:T(8,128)(2,1)}, u32[]{:S(2)}, u32[]{:S(2)}) async-start(bf16[8,512,512]{2,1,0:T(8,128)(2,1)} %bitcast.334), calls=%async_computation.2 | async-start | bytes 8388608 | tf_op jit(solution)/shard_map/all_to_all | solution.py:318
  329.0 47.2 %all-gather.17.cloned.1.call-start = ((), (), s32[]{:S(2)}) async-start(), calls=%async_computation.16 | async-start | bytes 2621440 | tf_op jit(solution)/shard_map/all_gather | solution.py:291
  378.2 32.0 %copy-start.135 = (bf16[1,512,2048]{2,1,0:T(8,128)(2,1)S(1)}, bf16[1,512,2048]{2,1,0:T(8,128)(2,1)}, u32[]{:S(2)}) copy-start(bf16[1,512,2048]{2,1,0:T(8,128)(2,1)} %all-gather.15.cloned.1.call-done) | copy-start | bytes 6291460
  496.4 90.5 %all-to-all-start.3 = ((bf16[8,2,131072]{2,1,0:T(2,128)(2,1)}), bf16[8,2,131072]{2,1,0:T(2,128)(2,1)}, u32[]{:S(2)}, u32[]{:S(2)}) async-start(bf16[8,2,131072]{2,1,0:T(2,128)(2,1)} %reshape.1022), calls=%async_computation.3 | async-start | bytes 8388608 | tf_op jit(solution)/shard_map/all_to_all | solution.py:333
  586.9 53.8 %all-to-all-start.1 = ((bf16[8,2,131072]{2,1,0:T(2,128)(2,1)}), bf16[8,2,131072]{2,1,0:T(2,128)(2,1)}, u32[]{:S(2)}, u32[]{:S(2)}) async-start(bf16[8,2,131072]{2,1,0:T(2,128)(2,1)} %reshape.1024), calls=%async_computation.1 | async-start | bytes 8388608 | tf_op jit(solution)/shard_map/all_to_all | solution.py:297
  591.6 450.0 %reduce-scatter.12.cloned.1.call-start = ((), (), s32[]{:S(2)}) async-start(), calls=%async_computation.18 | async-start | bytes 1310720 | tf_op jit(solution)/shard_map/reduce_scatter | solution.py:400
  843.0 198.6 %reduce-scatter.16.cloned.1.call-start = ((), (), s32[]{:S(2)}) async-start(), calls=%async_computation.20 | async-start | bytes 2621440 | tf_op jit(solution)/shard_map/reduce_scatter | solution.py:406
  852.4 189.2 %reduce-scatter.14.cloned.1.call-start = ((), (), s32[]{:S(2)}) async-start(), calls=%async_computation.19 | async-start | bytes 2621440 | tf_op jit(solution)/shard_map/reduce_scatter | solution.py:403
  865.3 191.9 %reduce-scatter.10.cloned.1.call-start = ((), (), s32[]{:S(2)}) async-start(), calls=%async_computation.17 | async-start | bytes 3932160 | tf_op jit(solution)/shard_map/reduce_scatter | solution.py:397
  999.8 101.5 %reduce-scatter.22.cloned.1.call-start = ((), (), s32[]{:S(2)}) async-start(), calls=%async_computation.23 | async-start | bytes 163840
  1010.4 113.3 %reduce-scatter.20.cloned.1.call-start = ((), (), s32[]{:S(2)}) async-start(), calls=%async_computation.22 | async-start | bytes 2621440 | tf_op jit(solution)/shard_map/reduce_scatter | solution.py:346
  1025.3 144.0 %reduce-scatter.18.cloned.1.call-start = ((), (), s32[]{:S(2)}) async-start(), calls=%async_computation.21 | async-start | bytes 2621440 | tf_op jit(solution)/shard_map/reduce_scatter | solution.py:343
  1040.1 57.9 %copy-start.17 = (f32[1024,512]{1,0:T(8,128)S(1)}, f32[1024,512]{1,0:T(8,128)}, u32[]{:S(2)}) copy-start(f32[1024,512]{1,0:T(8,128)} %copy-done.16) | copy-start | bytes 6291460
  1040.1 193.8 %all-reduce.7.cloned.1.call-start = ((), (), s32[]{:S(2)}) async-start(), calls=%async_computation.24 | async-start | bytes 4194304 | tf_op jit(solution)/shard_map/psum | solution.py:412
  (134 other events, 553.4 us)
Sparse Core Ops, SparseCore 0:
  10.2 66.1 all-gather.6
  78.6 26.5 all-gather.8
  106.8 45.4 all-gather.10
  153.7 44.6 all-gather.12
  277.4 45.0 all-gather.14
  331.1 45.0 all-gather.16
  843.1 24.0 reduce-scatter.11
  869.6 42.5 reduce-scatter.15
  914.5 43.1 reduce-scatter.13
  999.9 57.2 reduce-scatter.9
  1060.1 19.3 reduce-scatter.21
  1081.7 41.9 reduce-scatter.19
  1126.1 43.2 reduce-scatter.17
  1172.7 61.1 all-reduce.6
where the time goes:
time: 1260 us; the launch traced here: 1250 us
  local copies, waits for them, and re-layouts  362 us (29%)
  matrix products  331 us (26%)
  waiting for transfers between devices  274 us (22%)
  other arithmetic  175 us (14%)
  blocking collectives  67 us (5%)
  starting transfers between devices  19.9 us (2%)
  between operations  16.1 us (1%)
    dynamic_update_slice x8, local copies, waits for them, and re-layouts, one_pack(): lax.scan(step, (zero_rows, zero_rows), (query_blocks, segment_blocks, pac...  77 us
    unnamed x282, local copies, waits for them, and re-layouts  73.2 us
    psum x1, waiting for transfers between devices, local(): lax.psum(qkv_part.astype(jnp.bfloat16), 'expert').astype(jnp.float32)  62.4 us
    unnamed x7, other arithmetic  57.1 us
    reduce_scatter x1, waiting for transfers between devices, local(): lax.psum_scatter(grad_up_experts.astype(jnp.bfloat16), 'dp', scatter_dime...  43.5 us
    psum x1, blocking collectives, local(): logits_total = lax.psum(logits_part, ('dp', 'expert'))  40.3 us
    convert_element_type x4, other arithmetic, step(): (soft_weights * (grad_weights - row_delta)).astype(jnp.bfloat16)  39.9 us
    all_gather x1, waiting for transfers between devices, local(): lax.all_gather(w_down, 'dp', axis=0, tiled=True)  38.8 us
  transfers between devices with their start and end apart: 18, of which 11 were waited for; matrix products, arithmetic and copies ran while one was open for 37% of the time, Pallas kernels for 0%

commit v1 on v0

v1 whole, which is shorter than its diff:
```python
import functools

import jax
import jax.numpy as jnp
from jax import lax
from jax.experimental import pallas as pl
from jax.experimental.pallas import tpu as pltpu
from jax.sharding import PartitionSpec as P

D = 512
FF = 2048
HEADS = 8
HEAD = D // HEADS
PACK = 1024
MOST_LEN = 64
ROWS = 256
QB = 128
KB = QB + 2 * MOST_LEN
EPS = 1e-05
BLOCKED = -1e30
BF = jnp.bfloat16
F32 = jnp.float32
GELU_C = 0.7978845608028654
GELU_A = 0.044715


def mm(left, right):
    return lax.dot_general(left, right, (((1,), (0,)), ((), ())), preferred_element_type=F32)


def mm_t(left, right):
    return lax.dot_general(left, right, (((1,), (1,)), ((), ())), preferred_element_type=F32)


def t_mm(left, right):
    return lax.dot_general(left, right, (((0,), (0,)), ((), ())), preferred_element_type=F32)


def unit_rows(hidden):
    centered = hidden - jnp.mean(hidden, axis=-1, keepdims=True)
    spread = jnp.mean(centered * centered, axis=-1, keepdims=True)
    scale = lax.rsqrt(spread + EPS)
    return centered * scale, scale


def unit_back(unit, scale, gain, grad):
    inner = grad * gain
    first = jnp.mean(inner, axis=-1, keepdims=True)
    second = jnp.mean(inner * unit, axis=-1, keepdims=True)
    return scale * (inner - first - unit * second)


def gelu_both(z):
    square = z * z
    t = jnp.tanh(GELU_C * z * (1.0 + GELU_A * square))
    half = 0.5 * (1.0 + t)
    slope = half + 0.5 * z * (1.0 - t * t) * (GELU_C * (1.0 + 3.0 * GELU_A * square))
    return z * half, slope


def call(kernel, out_shape, *args, grid=None, in_specs=None, out_specs=None, scratch=(), mib=48, flops=0, moved=0,
         alias=None, pos=False):
    extra = {}
    if grid is not None:
        extra = dict(grid=grid, in_specs=in_specs, out_specs=out_specs)
    elif pos:
        held = pl.BlockSpec(memory_space=pltpu.VMEM)
        extra = dict(in_specs=[pl.BlockSpec(memory_space=pltpu.SMEM)] + [held] * (len(args) - 1))
    if alias:
        extra["input_output_aliases"] = alias
    return pl.pallas_call(
        kernel,
        out_shape=out_shape,
        scratch_shapes=scratch,
        compiler_params=pltpu.CompilerParams(vmem_limit_bytes=mib << 20),
        cost_estimate=pl.CostEstimate(flops=flops, bytes_accessed=moved, transcendentals=0),
        **extra,
    )(*args)


def sds(shape, dtype):
    return jax.ShapeDtypeStruct(shape, dtype)


WIRE = 512


def piece_rows(split):
    dp, ex = split
    return D // (dp * ex)


def wired(split):
    dp, ex = split
    return piece_rows(split) % 16 == 0 and ex >= 2


def near(split, pos_ref, j, k):
    dp, ex = split
    return lax.rem(pos_ref[1] + k, dp) * ex + jnp.bitwise_xor(pos_ref[0], j)


def send_rows(split, pos_ref, scr_ref, own_ref, core_ref, at, rows):
    dp, ex = split
    for j in range(ex):
        out = core_ref if j % 2 else own_ref
        for k in range(dp):
            start = pl.multiple_of(near(split, pos_ref, j, k) * rows, rows)
            out[j // 2, k, at : at + rows, :] = scr_ref[pl.ds(start, rows), :]


def wire_shapes(split, blocks):
    dp, ex = split
    shape = (ex // 2, dp, blocks * piece_rows(split), WIRE)
    return [sds(shape, BF), sds(shape, BF)]


def route_kernel(slots, sent_ref, pair_ref, tok_ref, slot_ref):
    t = lax.broadcasted_iota(jnp.int32, (PACK, 128), 0).astype(F32)
    start, end = sent_ref[0:1, :], sent_ref[1:2, :]
    member = (t >= start) & (t < end)

    def pick(value):
        return jnp.sum(jnp.where(member, value, 0.0), axis=1, keepdims=True)

    lane = lax.broadcasted_iota(jnp.int32, (PACK, 8), 1)
    out = jnp.where(lane == 0, pick(start), 0.0)
    out = jnp.where(lane == 1, pick(end), out)
    for k in range(2):
        base = sent_ref[2 + k : 3 + k, :]
        slot = pick(jnp.where(base >= 0, base - start + t + 1.0, 0.0)) - 1.0
        out = jnp.where(lane == 2 + k, slot, out)
    tok_ref[...] = out
    chunk = 512
    base, length, first = pair_ref[0:1, :], pair_ref[1:2, :], pair_ref[2:3, :]
    gate, task = pair_ref[3:4, :], pair_ref[4:5, :]
    for i in range(slots // chunk):
        s = lax.broadcasted_iota(jnp.int32, (chunk, 128), 0).astype(F32) + float(i * chunk)
        held = (base >= 0) & (s >= base) & (s < base + length)

        def take(value, held=held):
            return jnp.sum(jnp.where(held, value, 0.0), axis=1, keepdims=True)

        lane = lax.broadcasted_iota(jnp.int32, (chunk, 8), 1)
        out = jnp.where(lane == 0, take(first - base + s + 1.0) - 1.0, 0.0)
        out = jnp.where(lane == 1, take(gate), out)
        out = jnp.where(lane == 2, take(task + 1.0) - 1.0, out)
        slot_ref[i * chunk : (i + 1) * chunk, :] = out


def head_halves(block):
    low = lax.broadcasted_iota(jnp.int32, (1, 128), 1) < HEAD
    zero = jnp.zeros_like(block)
    return jnp.concatenate([jnp.where(low, block, zero), jnp.where(low, zero, block)], axis=0)


def merge_halves(stacked):
    low = lax.broadcasted_iota(jnp.int32, (1, 128), 1) < HEAD
    return jnp.where(low, stacked[:QB], stacked[QB:])


def key_start(i):
    return jnp.clip(i * QB - MOST_LEN, 0, PACK - KB)


def attention_kernel(norm_at, last, x_ref, np_ref, tok_ref, w_ref, *refs):
    if last:
        h_ref, a_ref, qkv_ref, ctx_ref, c_ref = refs
    else:
        h_ref, a_ref, qkv_ref, ctx_ref = refs
    gain, shift = np_ref[norm_at : norm_at + 1, :], np_ref[norm_at + 1 : norm_at + 2, :]
    for r in range(PACK // ROWS):
        rows = slice(r * ROWS, (r + 1) * ROWS)
        unit, _ = unit_rows(x_ref[rows, :].astype(F32))
        a = (unit * gain + shift).astype(BF)
        a_ref[rows, :] = a
        qkv_ref[rows, :] = mm(a, w_ref[:, 0 : 3 * D]).astype(BF)

    def block(i, carry):
        q0 = pl.multiple_of(i * QB, QB)
        k0 = pl.multiple_of(key_start(i), MOST_LEN)
        start, end = tok_ref[pl.ds(q0, QB), 0:1], tok_ref[pl.ds(q0, QB), 1:2]
        key = (lax.broadcasted_iota(jnp.int32, (QB, KB), 1) + k0).astype(F32)
        mask = (key >= start) & (key < end)
        mask = jnp.concatenate([mask, mask], axis=0)
        for pair in range(HEADS // 2):
            at = pair * 128
            q = head_halves(qkv_ref[pl.ds(q0, QB), at : at + 128] * BF(HEAD**-0.5))
            k = qkv_ref[pl.ds(k0, KB), D + at : D + at + 128]
            v = qkv_ref[pl.ds(k0, KB), 2 * D + at : 2 * D + at + 128]
            scores = jnp.where(mask, mm_t(q, k), BLOCKED)
            raised = jnp.exp(scores - jnp.max(scores, axis=1, keepdims=True))
            probs = (raised * (1.0 / jnp.sum(raised, axis=1, keepdims=True))).astype(BF)
            ctx_ref[pl.ds(q0, QB), at : at + 128] = merge_halves(mm(probs, v)).astype(BF)
        return carry

    lax.fori_loop(0, PACK // QB, block, 0)
    for r in range(PACK // ROWS):
        rows = slice(r * ROWS, (r + 1) * ROWS)
        h = x_ref[rows, :].astype(F32) + mm(ctx_ref[rows, :], w_ref[:, 3 * D : 4 * D])
        h_ref[rows, :] = h
        if last:
            unit, _ = unit_rows(h)
            c_ref[rows, :] = (unit * np_ref[6:7, :] + np_ref[7:8, :]).astype(BF)


def attention_forward(hidden, params, tok, weights, norm_at, last):
    outs = [sds((PACK, D), F32), sds((PACK, D), BF), sds((PACK, 3 * D), BF), sds((PACK, D), BF)]
    if last:
        outs.append(sds((PACK, D), BF))
    return call(
        functools.partial(attention_kernel, norm_at, last),
        outs, hidden, params, tok, weights,
        flops=6_000_000_000, moved=12 << 20, mib=40,
    )


def attention_back_kernel(norm_at, split, pos_ref, dx_ref, x_ref, a_ref, qkv_ref, ctx_ref, np_ref, tok_ref, w_ref,
                          out_ref, gn_ref, *refs):
    wire = wired(split)
    if wire:
        own_ref, core_ref, dctx_ref, dqkv_ref, acc_ref, scr_ref = refs
    else:
        gw_ref, dctx_ref, dqkv_ref, acc_ref = refs
    for r in range(PACK // ROWS):
        rows = slice(r * ROWS, (r + 1) * ROWS)
        dctx_ref[rows, :] = mm_t(dx_ref[rows, :].astype(BF), w_ref[:, 3 * D : 4 * D]).astype(BF)
    acc_ref[...] = jnp.zeros_like(acc_ref)

    def block(i, carry):
        q0 = pl.multiple_of(i * QB, QB)
        k0 = pl.multiple_of(key_start(i), MOST_LEN)
        start, end = tok_ref[pl.ds(k0, KB), 0:1], tok_ref[pl.ds(k0, KB), 1:2]
        query = (lax.broadcasted_iota(jnp.int32, (KB, QB), 1) + q0).astype(F32)
        mask = (query >= start) & (query < end)
        mask = jnp.concatenate([mask, mask], axis=1)
        for pair in range(HEADS // 2):
            at = pair * 128
            q = head_halves(qkv_ref[pl.ds(q0, QB), at : at + 128] * BF(HEAD**-0.5))
            k = qkv_ref[pl.ds(k0, KB), D + at : D + at + 128]
            v = qkv_ref[pl.ds(k0, KB), 2 * D + at : 2 * D + at + 128]
            g = head_halves(dctx_ref[pl.ds(q0, QB), at : at + 128])
            scores = jnp.where(mask, mm_t(k, q), BLOCKED)
            raised = jnp.exp(scores - jnp.max(scores, axis=0, keepdims=True))
            probs = raised * (1.0 / jnp.sum(raised, axis=0, keepdims=True))
            dprobs = mm_t(v, g)
            delta = jnp.sum(probs * dprobs, axis=0, keepdims=True)
            dscores = (probs * (dprobs - delta)).astype(BF)
            acc_ref[pl.ds(k0, KB), at : at + 128] += mm(dscores, q)
            acc_ref[pl.ds(k0, KB), D + at : D + at + 128] += mm(probs.astype(BF), g)
            dq = merge_halves(t_mm(dscores, k)) * (HEAD**-0.5)
            dqkv_ref[pl.ds(q0, QB), at : at + 128] = dq.astype(BF)
        return carry

    lax.fori_loop(0, PACK // QB, block, 0)
    dqkv_ref[:, D:] = acc_ref[...].astype(BF)
    for c in range(4):
        cols = slice(c * D, (c + 1) * D)
        if c < 3:
            grad = t_mm(a_ref[...], dqkv_ref[:, cols]).astype(BF)
        else:
            grad = t_mm(ctx_ref[...], dx_ref[...].astype(BF)).astype(BF)
        if wire:
            scr_ref[...] = grad
            rows = piece_rows(split)
            send_rows(split, pos_ref, scr_ref, own_ref, core_ref, c * rows, rows)
        else:
            gw_ref[:, cols] = grad
    gain = np_ref[norm_at : norm_at + 1, :]
    dgain, dshift = jnp.zeros((1, D), F32), jnp.zeros((1, D), F32)
    for r in range(PACK // ROWS):
        rows = slice(r * ROWS, (r + 1) * ROWS)
        dnorm = mm_t(dqkv_ref[rows, :], w_ref[:, 0 : 3 * D])
        unit, scale = unit_rows(x_ref[rows, :].astype(F32))
        dgain += jnp.sum(dnorm * unit, axis=0, keepdims=True)
        dshift += jnp.sum(dnorm, axis=0, keepdims=True)
        out_ref[rows, :] = dx_ref[rows, :] + unit_back(unit, scale, gain, dnorm)
    gn_ref[0:1, :] = dgain
    gn_ref[1:2, :] = dshift


def attention_backward(pos, dx, hidden, saved, params, tok, weights, norm_at, split):
    a, qkv, ctx = saved
    scratch = [pltpu.VMEM((PACK, D), BF), pltpu.VMEM((PACK, 3 * D), BF), pltpu.VMEM((PACK, 2 * D), F32)]
    if wired(split):
        grads = wire_shapes(split, 4)
        scratch.append(pltpu.VMEM((D, D), BF))
    else:
        grads = [sds((D, 4 * D), BF)]
    out, norm, *grads = call(
        functools.partial(attention_back_kernel, norm_at, split),
        [sds((PACK, D), F32), sds((2, D), F32)] + grads,
        pos, dx, hidden, a, qkv, ctx, params, tok, weights,
        scratch=scratch, pos=True,
        flops=12_000_000_000, moved=16 << 20, mib=48,
    )
    return out, norm, grads


def feed_kernel(x_ref, np_ref, up_ref, down_ref, h_ref, n_ref, act_ref, slope_ref):
    gain, shift = np_ref[2:3, :], np_ref[3:4, :]
    for r in range(PACK // ROWS):
        rows = slice(r * ROWS, (r + 1) * ROWS)
        x = x_ref[rows, :]
        unit, _ = unit_rows(x)
        n = (unit * gain + shift).astype(BF)
        n_ref[rows, :] = n
        act, slope = gelu_both(mm(n, up_ref[...]))
        act = act.astype(BF)
        act_ref[rows, :] = act
        slope_ref[rows, :] = slope.astype(BF)
        h_ref[rows, :] = x + mm(act, down_ref[...])


def feed_forward(hidden, params, up, down):
    return call(
        feed_kernel,
        [sds((PACK, D), F32), sds((PACK, D), BF), sds((PACK, FF), BF), sds((PACK, FF), BF)],
        hidden, params, up, down,
        flops=4_300_000_000, moved=17 << 20, mib=48,
    )


def feed_back_kernel(split, pos_ref, dx_ref, x_ref, n_ref, act_ref, slope_ref, np_ref, up_ref, down_ref,
                     out_ref, gn_ref, *refs):
    wire = wired(split)
    if wire:
        own_ref, core_ref, dz_ref, dy_ref, scr_ref, tall_ref = refs
    else:
        gup_ref, gdown_ref, dz_ref, dy_ref = refs
    gain = np_ref[2:3, :]
    dgain, dshift = jnp.zeros((1, D), F32), jnp.zeros((1, D), F32)
    for r in range(PACK // ROWS):
        rows = slice(r * ROWS, (r + 1) * ROWS)
        dx = dx_ref[rows, :]
        dy = dx.astype(BF)
        dy_ref[rows, :] = dy
        dz = (mm_t(dy, down_ref[...]) * slope_ref[rows, :].astype(F32)).astype(BF)
        dz_ref[rows, :] = dz
        dnorm = mm_t(dz, up_ref[...])
        unit, scale = unit_rows(x_ref[rows, :])
        dgain += jnp.sum(dnorm * unit, axis=0, keepdims=True)
        dshift += jnp.sum(dnorm, axis=0, keepdims=True)
        out_ref[rows, :] = dx + unit_back(unit, scale, gain, dnorm)
    gn_ref[0:1, :] = dgain
    gn_ref[1:2, :] = dshift
    if wire:
        rows = piece_rows(split)
        for c in range(FF // D):
            scr_ref[...] = t_mm(n_ref[...], dz_ref[:, c * D : (c + 1) * D]).astype(BF)
            send_rows(split, pos_ref, scr_ref, own_ref, core_ref, c * rows, rows)
        for c in range(FF // D):
            tall_ref[c * D : (c + 1) * D, :] = t_mm(act_ref[:, c * D : (c + 1) * D], dy_ref[...]).astype(BF)
        send_rows(split, pos_ref, tall_ref, own_ref, core_ref, FF // D * rows, FF // D * rows)
    else:
        gdown_ref[...] = t_mm(act_ref[...], dy_ref[...]).astype(BF)
        gup_ref[...] = t_mm(n_ref[...], dz_ref[...]).astype(BF)


def feed_backward(pos, dx, hidden, saved, params, up, down, split):
    n, act, slope = saved
    scratch = [pltpu.VMEM((PACK, FF), BF), pltpu.VMEM((PACK, D), BF)]
    if wired(split):
        grads = wire_shapes(split, 8)
        scratch += [pltpu.VMEM((D, D), BF), pltpu.VMEM((FF, D), BF)]
    else:
        grads = [sds((D, FF), BF), sds((FF, D), BF)]
    out, norm, *grads = call(
        functools.partial(feed_back_kernel, split),
        [sds((PACK, D), F32), sds((2, D), F32)] + grads,
        pos, dx, hidden, n, act, slope, params, up, down,
        scratch=scratch, pos=True,
        flops=8_600_000_000, moved=26 << 20, mib=58,
    )
    return out, norm, grads


def assemble_kernel(split, blocks, tall, *refs):
    dp, ex = split
    rows = piece_rows(split)
    pos_ref, pieces, outs = refs[0], refs[1 : 1 + ex], refs[1 + ex :]
    for j in range(ex):
        for k in range(dp):
            at = lax.rem(pos_ref[1] + dp - k, dp) * ex + jnp.bitwise_xor(pos_ref[0], j)
            start = pl.multiple_of(at * rows, rows)
            for c in range(blocks):
                outs[0][pl.ds(start, rows), c * WIRE : (c + 1) * WIRE] = pieces[j][k, c * rows : (c + 1) * rows, :]
            if tall:
                high = blocks * rows
                start = pl.multiple_of(at * high, high)
                outs[1][pl.ds(start, high), :] = pieces[j][k, high : 2 * high, :]


def assemble(split, pos, pieces, tall):
    outs = [sds((D, 4 * D), BF)] + ([sds((FF, D), BF)] if tall else [])
    return call(
        functools.partial(assemble_kernel, split, 4, tall), outs, pos, *pieces,
        pos=True, flops=1_000_000, moved=4 << 20, mib=24,
    )


def assemble_norm_kernel(split, *refs):
    dp, ex = split
    rows = piece_rows(split)
    pos_ref, pieces, (w_ref, np_ref, scr_ref) = refs[0], refs[1 : 1 + ex], refs[1 + ex :]
    for j in range(ex):
        for k in range(dp):
            at = lax.rem(pos_ref[1] + dp - k, dp) * ex + jnp.bitwise_xor(pos_ref[0], j)
            start = pl.multiple_of(at * rows, rows)
            for c in range(4):
                w_ref[pl.ds(start, rows), c * WIRE : (c + 1) * WIRE] = pieces[j][k, c * rows : (c + 1) * rows, :]
            scr_ref[pl.ds(start, rows), :] = pieces[j][k, 4 * rows : 5 * rows, 0:128].astype(F32)
    np_ref[...] = jnp.transpose(scr_ref[...])[:8]


def add_core_kernel(own_ref, got_ref, *outs):
    for j, out in enumerate(outs):
        out[...] = (own_ref[j].astype(F32) + got_ref[j].astype(F32)).astype(BF)


def add_all_kernel(count, *refs):
    total = refs[0][...].astype(F32)
    for ref in refs[1:count]:
        total = total + ref[...].astype(F32)
    total = total.astype(BF)
    outs = refs[count:]
    for k, out in enumerate(outs):
        out[...] = total[k] if len(outs) > 1 else total


def spread_kernel(split, layers, feed, *refs):
    dp, ex = split
    rows = piece_rows(split)
    pos_ref, refs = refs[0], refs[1:]
    count = len(layers)
    outs = refs[ex * (count + feed) :]
    for j in range(ex):
        at = jnp.bitwise_xor(pos_ref[0], j)
        start = pl.multiple_of(at * rows, rows)
        for n in range(count):
            piece = refs[n * ex + j][...].astype(F32)
            for c in range(3):
                outs[0][n, pl.ds(start, rows), c * D : (c + 1) * D] = piece[c * rows : (c + 1) * rows]
            outs[1][n, pl.ds(start, rows), :] = piece[3 * rows :]
        if feed:
            piece = refs[count * ex + j][...].astype(F32)
            for c in range(4):
                outs[2][pl.ds(start, rows), c * D : (c + 1) * D] = piece[c * rows : (c + 1) * rows]
            high = pl.multiple_of(at * 4 * rows, 4 * rows)
            outs[3][pl.ds(high, 4 * rows), :] = piece[4 * rows :]


def gather_kernel(gated, slot_ref, src_ref, *outs):
    size = outs[0].shape[0]
    tokens = lax.broadcasted_iota(jnp.int32, (size, PACK), 1).astype(F32)
    for n, out in enumerate(outs):
        slot = slot_ref[n * size : (n + 1) * size, :]
        hot = jnp.where(slot[:, 0:1] == tokens, 1.0, 0.0).astype(BF)
        rows = mm(hot, src_ref[...])
        if gated:
            rows = rows * slot[:, 1:2]
        out[...] = rows.astype(BF)


def gather_rows(slot, source, experts, gated):
    size = slot.shape[0] // experts
    return call(
        functools.partial(gather_kernel, gated), [sds((size, D), BF)] * experts, slot, source,
        flops=2 * slot.shape[0] * PACK * D, moved=6 << 20, mib=32,
    )


def slots_hot(tok_ref, size, n):
    at = lax.broadcasted_iota(jnp.int32, (PACK, size), 1).astype(F32) + float(n * size)
    return jnp.where((tok_ref[:, 2:3] == at) | (tok_ref[:, 3:4] == at), 1.0, 0.0).astype(BF)


def combine_back_kernel(experts, tok_ref, h_ref, cot_ref, np_ref, *refs):
    rows_refs, (out_ref, gn_ref, acc_ref) = refs[:experts], refs[experts:]
    for e, ref in enumerate(rows_refs):
        part = mm(slots_hot(tok_ref, ref.shape[0], e), ref[...])
        acc_ref[...] = part if e == 0 else acc_ref[...] + part
    gain = np_ref[6:7, :]
    dgain, dshift = jnp.zeros((1, D), F32), jnp.zeros((1, D), F32)
    for r in range(PACK // ROWS):
        rows = slice(r * ROWS, (r + 1) * ROWS)
        dnorm = acc_ref[rows, :]
        unit, scale = unit_rows(h_ref[rows, :])
        dgain += jnp.sum(dnorm * unit, axis=0, keepdims=True)
        dshift += jnp.sum(dnorm, axis=0, keepdims=True)
        out_ref[rows, :] = cot_ref[rows, :].astype(F32) + unit_back(unit, scale, gain, dnorm)
    gn_ref[0:1, :] = dgain
    gn_ref[1:2, :] = dshift


def whole(shape):
    return pl.BlockSpec(shape, lambda e: (0,) * len(shape))


def combine_back(tok, rows, hidden, cotangent, params):
    experts = len(rows)
    return call(
        functools.partial(combine_back_kernel, experts),
        [sds((PACK, D), F32), sds((2, D), F32)], tok, hidden, cotangent, params, *rows,
        scratch=[pltpu.VMEM((PACK, D), F32)],
        flops=2 * 4096 * PACK * D, moved=12 << 20, mib=40,
    )


def combine_out_kernel(experts, tok_ref, slot_ref, h_ref, *refs):
    rows_refs, dout_refs = refs[:experts], refs[experts : 2 * experts]
    out_ref, table_ref, acc_ref = refs[2 * experts :]
    size = rows_refs[0].shape[0]
    for e in range(experts):
        rows = rows_refs[e][...].astype(F32)
        slot = slot_ref[e * size : (e + 1) * size, :]
        gate, task = slot[:, 1:2], slot[:, 2:3]
        part = mm(slots_hot(tok_ref, size, e), (rows * gate).astype(BF))
        acc_ref[...] = part if e == 0 else acc_ref[...] + part
        held = task >= 0
        dgate = jnp.sum(rows * dout_refs[e][...].astype(F32), axis=1, keepdims=True)
        dgate = jnp.where(held, dgate / jnp.where(held, gate, 1.0), 0.0)
        tasks = lax.broadcasted_iota(jnp.int32, (size, 128), 1).astype(F32)
        table_ref[e : e + 1, :] = jnp.sum(jnp.where(tasks == task, dgate, 0.0), axis=0, keepdims=True)
    out_ref[...] = (h_ref[...] + acc_ref[...]).astype(BF)


def combine_out(tok, slot, rows, dout, hidden):
    experts = len(rows)
    return call(
        functools.partial(combine_out_kernel, experts),
        [sds((PACK, D), BF), sds((experts, 128), F32)], tok, slot, hidden, *rows, *dout,
        scratch=[pltpu.VMEM((PACK, D), F32)],
        flops=2 * 4096 * PACK * D, moved=14 << 20, mib=40,
    )


def expert_kernel(count, steps, *refs):
    bufs, douts = refs[:count], refs[count : 2 * count]
    up_ref, down_ref = refs[2 * count : 2 * count + 2]
    outs, dbufs = refs[-2 * count - 4 : -count - 4], refs[-count - 4 : -4]
    act_ref, du_ref, buf_ref, dout_ref = refs[-4:]
    i = pl.program_id(0)

    def work(n):
        buf, dout = bufs[n][...], douts[n][...]
        buf_ref[...] = buf
        dout_ref[...] = dout
        act, slope = gelu_both(mm(buf, up_ref[...]))
        act = act.astype(BF)
        act_ref[...] = act
        du = (mm_t(dout, down_ref[...]) * slope).astype(BF)
        du_ref[...] = du
        dbufs[n][...] = mm_t(du, up_ref[...]).astype(BF)
        outs[n][...] = mm(act, down_ref[...]).astype(BF)

    if count == 1:
        work(0)
    else:
        for n in range(count):
            pl.when(i // steps == n)(functools.partial(work, n))


def expert_rows(bufs, douts, up, down, total, at, held):
    rows = bufs[0].shape[0]
    count = len(bufs)
    size = min(256, rows)
    steps = rows // size
    blocks = [
        pl.BlockSpec((size, D), lambda i, n=n: (jnp.clip(i - n * steps, 0, steps - 1), 0)) for n in range(count)
    ]
    first = at // size
    keep = [pl.BlockSpec((size, cols), lambda i: (i + first, 0)) for cols in (FF, FF, D, D)]
    alias = {2 * count + 2 + n: 2 * count + n for n in range(4)} if held else None
    outs = call(
        functools.partial(expert_kernel, count, steps),
        [sds((rows, D), BF)] * (2 * count) + [sds((total, cols), BF) for cols in (FF, FF, D, D)],
        *bufs, *douts, up, down, *held,
        grid=(count * steps,),
        in_specs=blocks + blocks + [whole((D, FF)), whole((FF, D))] + [pl.BlockSpec(memory_space=pl.ANY)] * len(held),
        out_specs=blocks + blocks + keep,
        alias=alias,
        flops=8 * rows * count * D * FF, moved=count * rows * 13 << 10, mib=44,
    )
    return outs[:count], outs[count : 2 * count], outs[2 * count :]


def expert_grad_kernel(steps, act_ref, du_ref, buf_ref, dout_ref, gup_ref, gdown_ref, up_acc, down_acc):
    i = pl.program_id(0)

    @pl.when(i == 0)
    def _():
        up_acc[...] = jnp.zeros_like(up_acc)
        down_acc[...] = jnp.zeros_like(down_acc)

    up_acc[...] += t_mm(buf_ref[...], du_ref[...])
    down_acc[...] += t_mm(act_ref[...], dout_ref[...])

    @pl.when(i == steps - 1)
    def _():
        gup_ref[...] = up_acc[...].astype(BF)
        gdown_ref[...] = down_acc[...].astype(BF)


def expert_grads(act, du, buf, dout):
    rows = buf.shape[0]
    size = 1024
    tile = lambda cols: pl.BlockSpec((size, cols), lambda i: (i, 0))
    return call(
        functools.partial(expert_grad_kernel, rows // size),
        [sds((D, FF), BF), sds((FF, D), BF)], act, du, buf, dout,
        grid=(rows // size,),
        in_specs=[tile(FF), tile(FF), tile(D), tile(D)],
        out_specs=[whole((D, FF)), whole((FF, D))],
        scratch=[pltpu.VMEM((D, FF), F32), pltpu.VMEM((FF, D), F32)],
        flops=4 * rows * D * FF, moved=44 << 20, mib=56,
    )


def route(lengths, task_ids, task_experts, capacity, task_logits, cap_slots, rel):
    sentences = lengths.shape[1]
    experts = capacity.shape[0]
    tasks = task_experts.shape[0]
    lens, ids = lengths.reshape(-1), task_ids.reshape(-1)
    ends = jnp.cumsum(lens)
    starts = ends - lens
    table = jnp.take_along_axis(task_logits, task_experts, axis=1)
    gates = jax.nn.softmax(table, axis=-1)
    hot = ids[:, None] == lax.broadcasted_iota(jnp.int32, (1, tasks), 1)
    expert = jnp.sum(jnp.where(hot[:, :, None], task_experts[None], 0), axis=1)
    gate = jnp.sum(jnp.where(hot[:, :, None], gates[None], 0.0), axis=1)
    pair_expert = expert.reshape(-1)
    pair_len = jnp.repeat(lens, 2)
    expert_hot = (pair_expert[:, None] == lax.broadcasted_iota(jnp.int32, (1, experts), 1)).astype(jnp.int32)
    running = jnp.cumsum(expert_hot * pair_len[:, None], axis=0)
    filled = jnp.sum(running * expert_hot, axis=1)
    limits = jnp.sum(expert_hot * capacity[None, :], axis=1)
    base = jnp.where(filled <= limits, jnp.bitwise_xor(pair_expert, rel) * cap_slots + filled - pair_len, -1)
    base_two = base.reshape(sentences, 2)

    def lanes(rows):
        rows = jnp.stack([row.astype(F32) for row in rows])
        return jnp.pad(rows, ((0, 8 - rows.shape[0]), (0, 128 - rows.shape[1])))

    sent = lanes([starts, ends, base_two[:, 0], base_two[:, 1]])
    pair = lanes([base, pair_len, jnp.repeat(starts, 2), gate.reshape(-1), jnp.repeat(ids, 2)])
    slots = experts * cap_slots
    tok, slot = call(
        functools.partial(route_kernel, slots),
        [sds((PACK, 8), F32), sds((slots, 8), F32)], sent, pair,
        flops=1_000_000, moved=3 << 20, mib=24,
    )
    return tok, slot, gates


def flip(rows, j, ex):
    return lax.ppermute(rows, "expert", [(i, i ^ j) for i in range(ex)])


def turn(rows, k, dp):
    return lax.ppermute(rows, "dp", [(i, (i + k) % dp) for i in range(dp)])


def tie(value, *after):
    return lax.optimization_barrier((value,) + after)[0]


def gather_pieces(piece, split):
    dp, ex = split
    here = jnp.stack([piece] + [turn(piece, k, dp) for k in range(1, dp)])
    even = [here] + [flip(here, j, ex) for j in range(2, ex, 2)]
    got = []
    for one in even:
        got += [one, flip(one, 1, ex)]
    return got


def reduce_pieces(own, core, split):
    dp, ex = split
    rows = own.shape[2]
    got = flip(core, 1, ex)
    sums = call(
        add_core_kernel, [sds((dp, rows, WIRE), BF)] * (ex // 2), own, got,
        flops=1_000_000, moved=own.size * 6, mib=32,
    )
    got = [flip(sums[j], 2 * j, ex) for j in range(1, ex // 2)]
    sums = call(
        functools.partial(add_all_kernel, ex // 2), [sds((rows, WIRE), BF)] * dp, sums[0], *got,
        flops=1_000_000, moved=own.size * 2, mib=32,
    )
    got = [turn(sums[k], k, dp) for k in range(1, dp)]
    mine = call(
        functools.partial(add_all_kernel, dp), [sds((rows, WIRE), BF)], sums[0], *got,
        flops=1_000_000, moved=rows * WIRE * 10, mib=16,
    )[0]
    even = [mine] + [flip(mine, j, ex) for j in range(2, ex, 2)]
    out = []
    for one in even:
        out += [one, flip(one, 1, ex)]
    return out


def local(n_dp, n_ex, hidden_in, lengths, task_ids, task_experts, capacity, task_logits, norm_params,
          w_qkv, w_attn, w_up, w_down, expert_up, expert_down, cotangent):
    experts = capacity.shape[0]
    cap_slots = max(4 * hidden_in.shape[0] // experts, 2 * MOST_LEN)
    both = ("dp", "expert")
    me, here = lax.axis_index("expert"), lax.axis_index("dp")
    pos = jnp.stack([me, here]).astype(jnp.int32)
    split = (n_dp, n_ex)
    wire = wired(split)

    def mine(shard):
        rows = shard.shape[0] // n_ex
        return lax.dynamic_slice_in_dim(shard, me * rows, rows, 0)

    if wire:
        rows = piece_rows(split)

        def blocks(wide):
            return [wide[:, c * WIRE : (c + 1) * WIRE] for c in range(wide.shape[1] // WIRE)]

        norms = jnp.pad(mine(norm_params), ((0, 0), (0, WIRE - 8)))
        qkv, attn = mine(w_qkv), mine(w_attn)
        piece = jnp.concatenate(blocks(qkv[:, 0]) + [attn[:, 0], norms])
        zero = gather_pieces(piece, split)
        feed = gather_pieces(jnp.concatenate(blocks(mine(w_up)) + [mine(w_down)]), split)
        one = gather_pieces(jnp.concatenate(blocks(qkv[:, 1]) + [attn[:, 1]]), split)
        attn_zero, params = call(
            functools.partial(assemble_norm_kernel, split), [sds((D, 4 * D), BF), sds((8, D), F32)], pos, *zero,
            scratch=[pltpu.VMEM((D, 128), F32)], pos=True, flops=1_000_000, moved=4 << 20, mib=24,
        )
        up, down = assemble(split, pos, feed, True)
        attn_one = assemble(split, pos, one, False)[0]
    else:

        def gather_all(shard):
            return lax.all_gather(mine(shard), both, axis=0, tiled=True)

        params = lax.all_gather(norm_params, "dp", axis=0, tiled=True).astype(F32).T
        attn_zero = gather_all(jnp.concatenate([w_qkv[:, 0], w_attn[:, 0]], axis=1))
        up, down = gather_all(w_up), gather_all(w_down)
        attn_one = gather_all(jnp.concatenate([w_qkv[:, 1], w_attn[:, 1]], axis=1))
    up_expert = lax.all_gather(expert_up[0], "dp", axis=0, tiled=True)
    down_expert = lax.all_gather(expert_down[0], "dp", axis=0, tiled=True)

    rel = me if wire else 0
    tok, slot, gates = route(lengths, task_ids, task_experts, capacity, task_logits, cap_slots, rel)

    def exchange(blocks):
        if wire:
            return [blocks[0]] + [flip(blocks[j], j, n_ex) for j in range(1, n_ex)]
        rows = lax.all_to_all(jnp.stack(blocks), "expert", split_axis=0, concat_axis=0, tiled=True)
        return [rows[j] for j in range(n_ex)]

    dout_home = gather_rows(slot, cotangent, experts, True)
    dout = exchange(dout_home)
    h1, *saved_zero = attention_forward(hidden_in, params, tok, attn_zero, 0, False)
    h2, *saved_feed = feed_forward(h1, params, up, down)
    h3, *saved_one, c = attention_forward(h2, params, tok, attn_one, 4, True)
    buf = exchange(gather_rows(slot, c, experts, False))
    out, dbuf, held = [], [], ()
    step = 2
    for j in range(0, experts, step):
        some, back, held = expert_rows(
            buf[j : j + step], dout[j : j + step], up_expert, down_expert, experts * cap_slots, j * cap_slots, held
        )
        out += some
        dbuf += back
    dbuf_home = exchange(dbuf)
    gup_expert, gdown_expert = expert_grads(*held)
    expert_up_sum = lax.psum_scatter(gup_expert, "dp", scatter_dimension=0, tiled=True)
    expert_down_sum = lax.psum_scatter(gdown_expert, "dp", scatter_dimension=0, tiled=True)
    dx, gn_moe = combine_back(tok, dbuf_home, h3, cotangent, params)
    out_home = exchange([tie(one, gn_moe) for one in out])

    dx, gn_one, g_one = attention_backward(pos, dx, h2, saved_one, params, tok, attn_one, 4, split)
    dx, gn_feed, g_feed = feed_backward(pos, dx, h1, saved_feed, params, up, down, split)
    grad_in, gn_zero, g_zero = attention_backward(pos, dx, hidden_in, saved_zero, params, tok, attn_zero, 0, split)
    out_home = [tie(one, gn_zero) for one in out_home]
    hidden_out, table = combine_out(tok, slot, out_home, dout_home, h3)

    small = jnp.concatenate([gn_zero, gn_feed, gn_one, gn_moe], axis=0)
    table = jnp.take(table, jnp.bitwise_xor(jnp.arange(experts), rel), axis=0)
    table = jnp.pad(table, ((0, 0), (0, D - 128)))
    small = jnp.concatenate([small, table], axis=0)
    j = 1
    while j < n_ex:
        small = small + flip(small, j, n_ex)
        j *= 2
    j = 1
    while j < n_dp:
        small = small + lax.ppermute(small, "dp", [(i, i ^ j) for i in range(n_dp)])
        j *= 2
    gn = lax.dynamic_slice_in_dim(small[:8], here * (D // n_dp), D // n_dp, 1).T
    sums = small[8:, : task_logits.shape[0]].T

    if wire:
        parts = [reduce_pieces(*g, split) for g in (g_one, g_feed, g_zero)]
        rows = D // n_dp
        grad_qkv, grad_attn, grad_up, grad_down = call(
            functools.partial(spread_kernel, split, (0, 1), True),
            [sds((2, rows, 3 * D), F32), sds((2, rows, D), F32), sds((rows, FF), F32), sds((FF // n_dp, D), F32)],
            pos, *parts[2], *parts[0], *parts[1],
            pos=True, flops=1_000_000, moved=7 << 20, mib=32,
        )
        grad_qkv, grad_attn = grad_qkv.transpose(1, 0, 2), grad_attn.transpose(1, 0, 2)
    else:

        def reduce_all(grad):
            rows = grad.shape[0] // (n_dp * n_ex)
            grad = grad.reshape(n_dp, n_ex, rows, -1).transpose(1, 0, 2, 3).reshape(grad.shape)
            part = lax.psum_scatter(grad, "expert", scatter_dimension=0, tiled=True)
            part = lax.psum_scatter(part, "dp", scatter_dimension=0, tiled=True)
            return lax.all_gather(part, "expert", axis=0, tiled=True).astype(F32)

        g_one, grad_up, grad_down, g_zero = [reduce_all(g) for g in (*g_one, *g_feed, *g_zero)]
        grad_qkv = jnp.stack([g_zero[:, : 3 * D], g_one[:, : 3 * D]], axis=1)
        grad_attn = jnp.stack([g_zero[:, 3 * D :], g_one[:, 3 * D :]], axis=1)
    hot = task_experts[:, :, None] == lax.broadcasted_iota(jnp.int32, (1, 1, experts), 2)
    pair_sum = jnp.sum(jnp.where(hot, sums[:, None, :], 0.0), axis=2)
    lean = gates[:, 0] * gates[:, 1] * (pair_sum[:, 0] - pair_sum[:, 1])
    grad_logits = jnp.where(hot[:, 0], lean[:, None], 0.0) - jnp.where(hot[:, 1], lean[:, None], 0.0)
    return (
        hidden_out, grad_in, grad_logits, gn, grad_qkv, grad_attn, grad_up, grad_down,
        expert_up_sum.astype(F32)[None], expert_down_sum.astype(F32)[None],
    )


def solution(mesh):
    token = P(("dp", "expert"), None)
    expert = P("expert", "dp", None)
    in_specs = (
        token, token, token, P(), P(), P(), P("dp", None), P("dp", None, None), P("dp", None, None),
        P("dp", None), P("dp", None), expert, expert, token,
    )
    out_specs = (
        token, token, P(), P("dp", None), P("dp", None, None), P("dp", None, None), P("dp", None), P("dp", None),
        expert, expert,
    )
    step = functools.partial(local, mesh.shape["dp"], mesh.shape["expert"])
    return jax.shard_map(step, mesh=mesh, in_specs=in_specs, out_specs=out_specs, check_vma=False)
```

time: 1260 us -> 628 us (0.50)
  matrix products: 331 us -> 0 us
  local copies, waits for them, and re-layouts: 362 us -> 72.9 us
  Pallas kernels: 0 us -> 229 us
  other arithmetic: 175 us -> 8.38 us
  starting transfers between devices: 19.9 us -> 101 us
  waiting for transfers between devices: 274 us -> 198 us
  blocking collectives: 67 us -> 0 us
    dot_general x54 -> x0, matrix products: 331 us -> none  [the longest x4 36.4 us: step(): jnp.einsum('qhd,khd->hqk', grad_rows, value_rows, preferred_element_type=...]
    pallas_call x0 -> x29, Pallas kernels: none -> 229 us  [call(): pl.pallas_call(kernel, out_shape=out_shape, scratch_shapes=scratch, compi...]
    ppermute x0 -> x105, waiting for transfers between devices: none -> 197 us  [the longest x85 150 us: flip(): return lax.ppermute(rows, 'expert', [(i, i ^ j) for i in range(ex)])]
    all_gather x6 -> x2, waiting for transfers between devices: 121 us -> 0.01 us  [the longest x1 0.01 us: local(): up_expert = lax.all_gather(expert_up[0], 'dp', axis=0, tiled=True)]
    ppermute x0 -> x105, starting transfers between devices: none -> 101 us  [the longest x85 71.1 us: flip(): return lax.ppermute(rows, 'expert', [(i, i ^ j) for i in range(ex)])]
    convert_element_type x6 -> x2, local copies, waits for them, and re-layouts: 90.1 us -> 0.22 us  [lanes(): rows = jnp.stack([row.astype(F32) for row in rows])]
    dynamic_update_slice x8 -> x0, local copies, waits for them, and re-layouts: 77 us -> none  [one_pack(): lax.scan(step, (zero_rows, zero_rows), (query_blocks, segment_blocks, pac...]
    reduce_scatter x6 -> x2, waiting for transfers between devices: 67.1 us -> 0.01 us  [the longest x1 0.01 us: local(): lax.psum_scatter(gdown_expert, 'dp', scatter_dimension=0, tiled=True)]
  transfers between devices with their start and end apart: 18 -> 109, of which waited for: 11 -> 32; matrix products, arithmetic and copies ran while one was open for 37% -> 3% of each run, Pallas kernels for 0% -> 30%
where the time goes in v1:
time: 628 us; the launch traced here: 624 us
  Pallas kernels  229 us (36%)
  waiting for transfers between devices  198 us (32%)
  starting transfers between devices  101 us (16%)
  local copies, waits for them, and re-layouts  72.9 us (12%)
  between operations  15.2 us (2%)
  other arithmetic  8.38 us (1%)
    pallas_call x29, Pallas kernels, call(): pl.pallas_call(kernel, out_shape=out_shape, scratch_shapes=scratch, compi...  229 us
    ppermute x85, waiting for transfers between devices, flip(): return lax.ppermute(rows, 'expert', [(i, i ^ j) for i in range(ex)])  150 us
    ppermute x85, starting transfers between devices, flip(): return lax.ppermute(rows, 'expert', [(i, i ^ j) for i in range(ex)])  71.1 us
    unnamed x257, local copies, waits for them, and re-layouts  64.3 us
    ppermute x18, waiting for transfers between devices, turn(): return lax.ppermute(rows, 'dp', [(i, (i + k) % dp) for i in range(dp)])  45.2 us
    ppermute x18, starting transfers between devices, turn(): return lax.ppermute(rows, 'dp', [(i, (i + k) % dp) for i in range(dp)])  23.3 us
  transfers between devices with their start and end apart: 109, of which 32 were waited for; matrix products, arithmetic and copies ran while one was open for 3% of the time, Pallas kernels for 30%

profile of v1, /device:TPU:0, one launch (start us, length us, event | category | flops | bytes accessed | tf_op | source)
XLA Modules:
  0.0 624.1 jit_solution(14498692432095739520)
XLA Ops:
  36.7 25.8 %collective-permute-done.1 = bf16[80,512]{1,0:T(8,128)(2,1)S(1)} collective-permute-done((bf16[80,512]{1,0:T(8,128)(2,1)S(1)}, bf16[80,512]{1,0:T(8,128)(2,1)S(1)}, u32[]{:S(2)}, u32[]{:S(2)}) %collective-permute-start.1) | collective-permute-done | bytes 81952 | tf_op jit(solution)/shard_map/ppermute | solution.py:661
  67.7 4.0 collective-permute-done.24.refs_3_
  73.2 4.4 collective-permute-done.26.refs_5_
  85.1 5.7 collective-permute-done.6.refs_5_
  104.7 4.8 shard_map.221
  114.8 4.9 collective-permute-done.16.refs_5_
  122.3 12.2 %shard_map.215 = (f32[1024,512]{1,0:T(8,128)S(1)}, bf16[1024,512]{1,0:T(8,128)(2,1)S(1)}, bf16[1024,1536]{1,0:T(8,128)(2,1)S(1)}, bf16[1024,512]{1,0:T(8,128)(2,1)S(1)}) custom-call(bf16[1024,512]{1,0:T(8,128)(2,1)S(1)} %copy-done.35, f32[8,512]{1,0:T(8,128)S(1)} %get-tuple-element.141.np_ref, f32[1024,8]{1,0:T(8,128)S(1)} %get-tuple-element.139.tok_ref, ...), custom_call_target="tpu_custom_call" | custom-call | flops 6000000000 | bytes 12582912 | tf_op jit(solution)/shard_map/pallas_call | solution.py:71
  142.8 13.0 %shard_map.217 = (f32[1024,512]{1,0:T(8,128)S(1)}, bf16[1024,512]{1,0:T(8,128)(2,1)S(1)}, bf16[1024,2048]{1,0:T(8,128)(2,1)}, bf16[1024,2048]{1,0:T(8,128)(2,1)}) custom-call(f32[1024,512]{1,0:T(8,128)S(1)} %copy-done.96, f32[8,512]{1,0:T(8,128)S(1)} %get-tuple-element.141.np_ref, bf16[512,2048]{1,0:T(8,128)(2,1)} %copy-done.31, bf16[2048,512]{1,0:T(8,128)(2,1)} %copy-done.32), custom_call_target="tpu_custom_call" | custom-call | flops 4300000256 | bytes 17825792 | tf_op jit(solution)/shard_map/pallas_call | solution.py:71
  159.1 12.3 %shard_map.219 = (f32[1024,512]{1,0:T(8,128)S(1)}, bf16[1024,512]{1,0:T(8,128)(2,1)S(1)}, bf16[1024,1536]{1,0:T(8,128)(2,1)S(1)}, bf16[1024,512]{1,0:T(8,128)(2,1)S(1)}, bf16[1024,512]{1,0:T(8,128)(2,1)S(1)}) custom-call(f32[1024,512]{1,0:T(8,128)S(1)} %copy-done.98, f32[8,512]{1,0:T(8,128)S(1)} %get-tuple-element.141.np_ref, ...), custom_call_target="tpu_custom_call" | custom-call | flops 6000000000 | bytes 12582912 | tf_op jit(solution)/shard_map/pallas_call | solution.py:71
  172.2 5.0 shard_map.220
  195.8 13.5 %shard_map.222 = (bf16[512,512]{1,0:T(8,128)(2,1)S(1)}, bf16[512,512]{1,0:T(8,128)(2,1)S(1)}, bf16[512,512]{1,0:T(8,128)(2,1)S(1)}, bf16[512,512]{1,0:T(8,128)(2...) custom-call(bf16[512,512]{1,0:T(8,128)(2,1)S(1)} %copy-done.109, ...), custom_call_target="tpu_custom_call" | custom-call | flops 8589934592 | bytes 13631488 | tf_op jit(solution)/shard_map/pallas_call | solution.py:71
  214.5 5.8 collective-permute-done.33.refs_0_
  221.1 9.7 %collective-permute-done.34.refs_1_ = bf16[512,512]{1,0:T(8,128)(2,1)S(1)} collective-permute-done((bf16[512,512]{1,0:T(8,128)(2,1)}, bf16[512,512]{1,0:T(8,128)(2,1)S(1)}, u32[]{:S(2)}, u32[]{:S(2)}) %collective-permute-start.34) | collective-permute-done | bytes 524320 | tf_op jit(solution)/shard_map/ppermute | solution.py:657
  232.0 13.9 %shard_map.223 = (bf16[512,512]{1,0:T(8,128)(2,1)}, bf16[512,512]{1,0:T(8,128)(2,1)}, bf16[512,512]{1,0:T(8,128)(2,1)S(1)}, bf16[512,512]{1,0:T(8,128)(2,1)S(1)}...) custom-call(bf16[512,512]{1,0:T(8,128)(2,1)S(1)} %collective-permute, ...), custom_call_target="tpu_custom_call", output_to_operand_aliasing={{4}: (6, {}), {5}: (7, {}), {6}: (8, {}), {7}: (9, {})} | custom-call | flops 8589934592 | bytes 13631488 | tf_op jit(solution)/shard_map/pallas_call | solution.py:71
  251.5 41.5 %collective-permute-done.40.refs_1_ = bf16[512,512]{1,0:T(8,128)(2,1)S(1)} collective-permute-done((bf16[512,512]{1,0:T(8,128)(2,1)S(1)}, bf16[512,512]{1,0:T(8,128)(2,1)S(1)}, u32[]{:S(2)}, u32[]{:S(2)}) %collective-permute-start.40) | collective-permute-done | bytes 524320 | tf_op jit(solution)/shard_map/ppermute | solution.py:657
  293.0 13.5 %shard_map.224 = (bf16[512,512]{1,0:T(8,128)(2,1)S(1)}, bf16[512,512]{1,0:T(8,128)(2,1)S(1)}, bf16[512,512]{1,0:T(8,128)(2,1)S(1)}, bf16[512,512]{1,0:T(8,128)(2...) custom-call(bf16[512,512]{1,0:T(8,128)(2,1)S(1)} %collective-permute, ...), custom_call_target="tpu_custom_call", output_to_operand_aliasing={{4}: (6, {}), {5}: (7, {}), {6}: (8, {}), {7}: (9, {})} | custom-call | flops 8589934592 | bytes 13631488 | tf_op jit(solution)/shard_map/pallas_call | solution.py:71
  307.3 13.8 %shard_map.225 = (bf16[512,512]{1,0:T(8,128)(2,1)S(1)}, bf16[512,512]{1,0:T(8,128)(2,1)S(1)}, bf16[512,512]{1,0:T(8,128)(2,1)S(1)}, bf16[512,512]{1,0:T(8,128)(2...) custom-call(bf16[512,512]{1,0:T(8,128)(2,1)S(1)} %collective-permute, ...), custom_call_target="tpu_custom_call", output_to_operand_aliasing={{4}: (6, {}), {5}: (7, {}), {6}: (8, {}), {7}: (9, {})} | custom-call | flops 8589934592 | bytes 13631488 | tf_op jit(solution)/shard_map/pallas_call | solution.py:71
  324.4 25.2 %shard_map.241 = (bf16[512,2048]{1,0:T(8,128)(2,1)}, bf16[2048,512]{1,0:T(8,128)(2,1)}) custom-call(bf16[4096,2048]{1,0:T(8,128)(2,1)} %get-tuple-element.262.act_ref, bf16[4096,2048]{1,0:T(8,128)(2,1)} %get-tuple-element.263.du_ref, bf16[4096,512]{1,0:T(8,128)(2,1)} %get-tuple-element.264.buf_ref, bf16[4096,512]{1,0:T(8,128)(2,1)} %get-tuple-element.265.dout_ref), custom_call_target="tpu_custom_call" | custom-call | flops 17179869184 | bytes 46137344 | tf_op jit(solution)/shard_map/pallas_call | solution.py:71
  355.6 10.2 %collective-permute-done.49.refs_6_ = bf16[512,512]{1,0:T(8,128)(2,1)S(1)} collective-permute-done((bf16[512,512]{1,0:T(8,128)(2,1)}, bf16[512,512]{1,0:T(8,128)(2,1)S(1)}, u32[]{:S(2)}, u32[]{:S(2)}) %collective-permute-start.49) | collective-permute-done | bytes 524320 | tf_op jit(solution)/shard_map/ppermute | solution.py:657
  366.7 9.4 %collective-permute-done.50.refs_7_ = bf16[512,512]{1,0:T(8,128)(2,1)S(1)} collective-permute-done((bf16[512,512]{1,0:T(8,128)(2,1)}, bf16[512,512]{1,0:T(8,128)(2,1)S(1)}, u32[]{:S(2)}, u32[]{:S(2)}) %collective-permute-start.50) | collective-permute-done | bytes 524320 | tf_op jit(solution)/shard_map/ppermute | solution.py:657
  378.1 9.7 %collective-permute-done.43.refs_4_ = bf16[512,512]{1,0:T(8,128)(2,1)} collective-permute-done((bf16[512,512]{1,0:T(8,128)(2,1)}, bf16[512,512]{1,0:T(8,128)(2,1)}, u32[]{:S(2)}, u32[]{:S(2)}) %collective-permute-start.43) | collective-permute-done | bytes 524320 | tf_op jit(solution)/shard_map/ppermute | solution.py:657
  387.8 11.2 %collective-permute-done.44.refs_5_ = bf16[512,512]{1,0:T(8,128)(2,1)} collective-permute-done((bf16[512,512]{1,0:T(8,128)(2,1)}, bf16[512,512]{1,0:T(8,128)(2,1)}, u32[]{:S(2)}, u32[]{:S(2)}) %collective-permute-start.44) | collective-permute-done | bytes 524320 | tf_op jit(solution)/shard_map/ppermute | solution.py:657
  403.8 7.7 %shard_map.226 = (f32[1024,512]{1,0:T(8,128)S(1)}, f32[2,512]{1,0:T(2,128)S(1)}) custom-call(f32[1024,8]{1,0:T(8,128)S(1)} %copy-done.38, f32[1024,512]{1,0:T(8,128)S(1)} %copy-done.87, bf16[1024,512]{1,0:T(8,128)(2,1)S(1)} %copy-done.34, f32[8,512]{1,0:T(8,128)S(1)} %get-tuple-element.141.np_ref, bf16[512,512]{1,0:T(8,128)(2,1)S(1)} %copy-done.103, ...), custom_call_target="tpu_custom_call" | custom-call | flops 4294967296 | bytes 12582912 | tf_op jit(solution)/shard_map/pallas_call | solution.py:71
  417.2 24.8 %shard_map.227 = (f32[1024,512]{1,0:T(8,128)}, f32[2,512]{1,0:T(2,128)S(1)}, bf16[4,4,64,512]{3,2,1,0:T(8,128)(2,1)S(1)}, bf16[4,4,64,512]{3,2,1,0:T(8,128)(2,1)}) custom-call(s32[2]{0:T(128)S(1)} %pad_add_fusion.refs_0_.pos_ref, f32[1024,512]{1,0:T(8,128)} %copy-done.94, f32[1024,512]{1,0:T(8,128)} %copy-done.97, bf16[1024,512]{1,0:T(8,128)(2,1)S(1)} %copy-done.105, ...), custom_call_target="tpu_custom_call" | custom-call | flops 12000000000 | bytes 16777216 | tf_op jit(solution)/shard_map/pallas_call | solution.py:71
  443.0 18.4 %shard_map.228 = (f32[1024,512]{1,0:T(8,128)}, f32[2,512]{1,0:T(2,128)}, bf16[4,4,128,512]{3,2,1,0:T(8,128)(2,1)}, bf16[4,4,128,512]{3,2,1,0:T(8,128)(2,1)}) custom-call(s32[2]{0:T(128)} %copy-done.26, f32[1024,512]{1,0:T(8,128)} %get-tuple-element.192.dx_ref, f32[1024,512]{1,0:T(8,128)} %copy-done.95, bf16[1024,512]{1,0:T(8,128)(2,1)} %copy-done.99, ...), custom_call_target="tpu_custom_call" | custom-call | flops 8600000512 | bytes 27262976 | tf_op jit(solution)/shard_map/pallas_call | solution.py:71
  467.1 24.0 %shard_map.229 = (f32[1024,512]{1,0:T(8,128)}, f32[2,512]{1,0:T(2,128)S(1)}, bf16[4,4,64,512]{3,2,1,0:T(8,128)(2,1)S(1)}, bf16[4,4,64,512]{3,2,1,0:T(8,128)(2,1)}) custom-call(s32[2]{0:T(128)S(1)} %copy-done.27, f32[1024,512]{1,0:T(8,128)} %get-tuple-element.196.dx_ref, bf16[1024,512]{1,0:T(8,128)(2,1)S(1)} %copy-done.36, bf16[1024,512]{1,0:T(8,128)(2,1)S(1)} %copy-done.111, ...), custom_call_target="tpu_custom_call" | custom-call | flops 12000000000 | bytes 16777216 | tf_op jit(solution)/shard_map/pallas_call | solution.py:71
  493.2 9.7 %shard_map.230 = (bf16[1024,512]{1,0:T(8,128)(2,1)}, f32[8,128]{1,0:T(8,128)S(1)}) custom-call(f32[1024,8]{1,0:T(8,128)S(1)} %copy-done.39, f32[4096,8]{1,0:T(8,128)S(1)} %copy-done.29, f32[1024,512]{1,0:T(8,128)S(1)} %copy-done.88, bf16[512,512]{1,0:T(8,128)(2,1)S(1)} %copy-done.93, bf16[512,512]{1,0:T(8,128)(2,1)S(1)} %collective-permute-done.51.refs_1_, ...), custom_call_target="tpu_custom_call" | custom-call | flops 4294967296 | bytes 14680064 | tf_op jit(solution)/shard_map/pallas_call | solution.py:71
  513.3 4.5 collective-permute-done.59
  521.8 5.8 collective-permute-start.61
  547.7 12.8 %collective-permute-done.66.refs_3_ = bf16[4,64,512]{2,1,0:T(8,128)(2,1)S(1)} collective-permute-done((bf16[4,64,512]{2,1,0:T(8,128)(2,1)S(1)}, bf16[4,64,512]{2,1,0:T(8,128)(2,1)S(1)}, u32[]{:S(2)}, u32[]{:S(2)}) %collective-permute-start.66) | collective-permute-done | bytes 262176 | tf_op jit(solution)/shard_map/ppermute | solution.py:657
  567.8 5.1 collective-permute-done.67.refs_1_
  589.5 4.8 collective-permute-done.96.refs_2_
  (554 shorter events, 221.8 us)
Async XLA Ops:
  7.2 181.2 %all-gather.5.cloned.1.call-start = ((), (), s32[]{:S(2)}) async-start(), calls=%async_computation.4 | async-start | bytes 2621440 | tf_op jit(solution)/shard_map/all_gather | solution.py:744
  8.0 180.5 %all-gather.7.cloned.1.call-start = ((), (), s32[]{:S(2)}) async-start(), calls=%async_computation.5 | async-start | bytes 2621440 | tf_op jit(solution)/shard_map/all_gather | solution.py:745
  20.9 44.7 %collective-permute-start.10 = (bf16[128,512]{1,0:T(8,128)(2,1)S(1)}, bf16[128,512]{1,0:T(8,128)(2,1)S(1)}, u32[]{:S(2)}, u32[]{:S(2)}) collective-permute-start(bf16[128,512]{1,0:T(8,128)(2,1)S(1)} %dynamic-slice_dynamic-update-slice_fusion), channel_id=1, source_target_pairs={{0,8},{8,16},{16,24},{24,0},{1,9},{9,17},{17,25},{25,1},{2,10},{10... | collective-permute-start | bytes 393224 | tf_op jit(solution)/shard_map/ppermute | solution.py:661
  22.6 590.5 %reduce-scatter.5.cloned.1.call-start = ((), (), s32[]{:S(2)}) async-start(), calls=%async_computation.3 | async-start | bytes 2621440 | tf_op jit(solution)/shard_map/reduce_scatter | solution.py:773
  27.7 38.4 %collective-permute-start.11 = (bf16[128,512]{1,0:T(8,128)(2,1)S(1)}, bf16[128,512]{1,0:T(8,128)(2,1)S(1)}, u32[]{:S(2)}, u32[]{:S(2)}) collective-permute-start(bf16[128,512]{1,0:T(8,128)(2,1)S(1)} %dynamic-slice_dynamic-update-slice_fusion), channel_id=1, source_target_pairs={{0,16},{8,24},{16,0},{24,8},{1,17},{9,25},{17,1},{25,9},{2,18},{10... | collective-permute-start | bytes 393224 | tf_op jit(solution)/shard_map/ppermute | solution.py:661
  31.4 34.7 %collective-permute-start.12 = (bf16[128,512]{1,0:T(8,128)(2,1)S(1)}, bf16[128,512]{1,0:T(8,128)(2,1)S(1)}, u32[]{:S(2)}, u32[]{:S(2)}) collective-permute-start(bf16[128,512]{1,0:T(8,128)(2,1)S(1)} %dynamic-slice_dynamic-update-slice_fusion), channel_id=1, source_target_pairs={{0,24},{8,0},{16,8},{24,16},{1,25},{9,1},{17,9},{25,17},{2,26},{10... | collective-permute-start | bytes 393224 | tf_op jit(solution)/shard_map/ppermute | solution.py:661
  31.6 30.9 %collective-permute-start.1 = (bf16[80,512]{1,0:T(8,128)(2,1)S(1)}, bf16[80,512]{1,0:T(8,128)(2,1)S(1)}, u32[]{:S(2)}, u32[]{:S(2)}) collective-permute-start(bf16[80,512]{1,0:T(8,128)(2,1)S(1)} %constant_dynamic-update-slice_fusion), channel_id=1, source_target_pairs={{0,16},{8,24},{16,0},{24,8},{1,17},{9,25},{17,1},{25,9},{2,18},{10... | collective-permute-start | bytes 245768 | tf_op jit(solution)/shard_map/ppermute | solution.py:661
  119.7 65.3 %collective-permute-start.31 = (bf16[512,512]{1,0:T(8,128)(2,1)S(1)}, bf16[512,512]{1,0:T(8,128)(2,1)S(1)}, u32[]{:S(2)}, u32[]{:S(2)}) collective-permute-start(bf16[512,512]{1,0:T(8,128)(2,1)S(1)} %get-tuple-element.152.refs_9_), channel_id=1, source_target_pairs={{0,1},{1,0},{2,3},{3,2},{4,5},{5,4},{6,7},{7,6},{8,9},{9,8},{10,11... | collective-permute-start | bytes 1572872 | tf_op jit(solution)/shard_map/ppermute | solution.py:657
  184.4 61.6 %collective-permute-start.41 = (bf16[512,512]{1,0:T(8,128)(2,1)}, bf16[512,512]{1,0:T(8,128)(2,1)S(1)}, u32[]{:S(2)}, u32[]{:S(2)}) collective-permute-start(bf16[512,512]{1,0:T(8,128)(2,1)} %get-tuple-element.168.refs_12_), channel_id=1, source_target_pairs={{0,4},{1,5},{2,6},{3,7},{4,0},{5,1},{6,2},{7,3},{8,12},{9,13},{10,... | collective-permute-start | bytes 1572872 | tf_op jit(solution)/shard_map/ppermute | solution.py:657
  185.8 34.6 %collective-permute-start.33 = (bf16[512,512]{1,0:T(8,128)(2,1)}, bf16[512,512]{1,0:T(8,128)(2,1)S(1)}, u32[]{:S(2)}, u32[]{:S(2)}) collective-permute-start(bf16[512,512]{1,0:T(8,128)(2,1)} %get-tuple-element.156), channel_id=1, source_target_pairs={{0,2},{1,3},{2,0},{3,1},{4,6},{5,7},{6,4},{7,5},{8,10},{9,11},{10,... | collective-permute-start | bytes 1572872 | tf_op jit(solution)/shard_map/ppermute | solution.py:657
  188.0 42.8 %collective-permute-start.34 = (bf16[512,512]{1,0:T(8,128)(2,1)}, bf16[512,512]{1,0:T(8,128)(2,1)S(1)}, u32[]{:S(2)}, u32[]{:S(2)}) collective-permute-start(bf16[512,512]{1,0:T(8,128)(2,1)} %get-tuple-element.157), channel_id=1, source_target_pairs={{0,3},{1,2},{2,1},{3,0},{4,7},{5,6},{6,5},{7,4},{8,11},{9,10},{10,... | collective-permute-start | bytes 1572872 | tf_op jit(solution)/shard_map/ppermute | solution.py:657
  211.8 35.8 %collective-permute-start.42 = (bf16[512,512]{1,0:T(8,128)(2,1)S(1)}, bf16[512,512]{1,0:T(8,128)(2,1)S(1)}, u32[]{:S(2)}, u32[]{:S(2)}) collective-permute-start(bf16[512,512]{1,0:T(8,128)(2,1)S(1)} %copy-done.43), channel_id=1, source_target_pairs={{0,5},{1,4},{2,7},{3,6},{4,1},{5,0},{6,3},{7,2},{8,13},{9,12},{10,... | collective-permute-start | bytes 1572872 | tf_op jit(solution)/shard_map/ppermute | solution.py:657
  213.2 93.3 %collective-permute-start.47 = (bf16[512,512]{1,0:T(8,128)(2,1)S(1)}, bf16[512,512]{1,0:T(8,128)(2,1)S(1)}, u32[]{:S(2)}, u32[]{:S(2)}) collective-permute-start(bf16[512,512]{1,0:T(8,128)(2,1)S(1)} %copy-done.46), channel_id=1, source_target_pairs={{0,6},{1,7},{2,4},{3,5},{4,2},{5,3},{6,0},{7,1},{8,14},{9,15},{10,... | collective-permute-start | bytes 1572872 | tf_op jit(solution)/shard_map/ppermute | solution.py:657
  230.7 62.3 %collective-permute-start.40 = (bf16[512,512]{1,0:T(8,128)(2,1)S(1)}, bf16[512,512]{1,0:T(8,128)(2,1)S(1)}, u32[]{:S(2)}, u32[]{:S(2)}) collective-permute-start(bf16[512,512]{1,0:T(8,128)(2,1)S(1)} %copy-done.70), channel_id=1, source_target_pairs={{0,5},{1,4},{2,7},{3,6},{4,1},{5,0},{6,3},{7,2},{8,13},{9,12},{10,... | collective-permute-start | bytes 1572872 | tf_op jit(solution)/shard_map/ppermute | solution.py:657
  246.8 59.8 %collective-permute-start.48 = (bf16[512,512]{1,0:T(8,128)(2,1)S(1)}, bf16[512,512]{1,0:T(8,128)(2,1)S(1)}, u32[]{:S(2)}, u32[]{:S(2)}) collective-permute-start(bf16[512,512]{1,0:T(8,128)(2,1)S(1)} %copy-done.49), channel_id=1, source_target_pairs={{0,7},{1,6},{2,5},{3,4},{4,3},{5,2},{6,1},{7,0},{8,15},{9,14},{10,... | collective-permute-start | bytes 1572872 | tf_op jit(solution)/shard_map/ppermute | solution.py:657
  247.6 59.0 %collective-permute-start.45 = (bf16[512,512]{1,0:T(8,128)(2,1)S(1)}, bf16[512,512]{1,0:T(8,128)(2,1)S(1)}, u32[]{:S(2)}, u32[]{:S(2)}) collective-permute-start(bf16[512,512]{1,0:T(8,128)(2,1)S(1)} %copy-done.64), channel_id=1, source_target_pairs={{0,6},{1,7},{2,4},{3,5},{4,2},{5,3},{6,0},{7,1},{8,14},{9,15},{10,... | collective-permute-start | bytes 1572872 | tf_op jit(solution)/shard_map/ppermute | solution.py:657
  249.2 57.4 %collective-permute-start.46 = (bf16[512,512]{1,0:T(8,128)(2,1)S(1)}, bf16[512,512]{1,0:T(8,128)(2,1)S(1)}, u32[]{:S(2)}, u32[]{:S(2)}) collective-permute-start(bf16[512,512]{1,0:T(8,128)(2,1)S(1)} %copy-done.62), channel_id=1, source_target_pairs={{0,7},{1,6},{2,5},{3,4},{4,3},{5,2},{6,1},{7,0},{8,15},{9,14},{10,... | collective-permute-start | bytes 1572872 | tf_op jit(solution)/shard_map/ppermute | solution.py:657
  349.6 265.6 %reduce-scatter.3.cloned.1.call-start = ((), (), s32[]{:S(2)}) async-start(), calls=%async_computation.2 | async-start | bytes 2621440 | tf_op jit(solution)/shard_map/reduce_scatter | solution.py:772
  352.5 35.3 %collective-permute-start.43 = (bf16[512,512]{1,0:T(8,128)(2,1)}, bf16[512,512]{1,0:T(8,128)(2,1)}, u32[]{:S(2)}, u32[]{:S(2)}) collective-permute-start(bf16[512,512]{1,0:T(8,128)(2,1)} %copy-done.74), channel_id=1, source_target_pairs={{0,4},{1,5},{2,6},{3,7},{4,0},{5,1},{6,2},{7,3},{8,12},{9,13},{10,... | collective-permute-start | bytes 1572872 | tf_op jit(solution)/shard_map/ppermute | solution.py:657
  353.9 45.1 %collective-permute-start.44 = (bf16[512,512]{1,0:T(8,128)(2,1)}, bf16[512,512]{1,0:T(8,128)(2,1)}, u32[]{:S(2)}, u32[]{:S(2)}) collective-permute-start(bf16[512,512]{1,0:T(8,128)(2,1)} %copy-done.73), channel_id=1, source_target_pairs={{0,5},{1,4},{2,7},{3,6},{4,1},{5,0},{6,3},{7,2},{8,13},{9,12},{10,... | collective-permute-start | bytes 1572872 | tf_op jit(solution)/shard_map/ppermute | solution.py:657
  354.3 44.6 %collective-permute-start.37 = (bf16[512,512]{1,0:T(8,128)(2,1)}, bf16[512,512]{1,0:T(8,128)(2,1)}, u32[]{:S(2)}, u32[]{:S(2)}) collective-permute-start(bf16[512,512]{1,0:T(8,128)(2,1)} %copy-done.56), channel_id=1, source_target_pairs={{0,2},{1,3},{2,0},{3,1},{4,6},{5,7},{6,4},{7,5},{8,10},{9,11},{10,... | collective-permute-start | bytes 1572872 | tf_op jit(solution)/shard_map/ppermute | solution.py:657
  366.7 32.3 %collective-permute-start.38 = (bf16[512,512]{1,0:T(8,128)(2,1)}, bf16[512,512]{1,0:T(8,128)(2,1)}, u32[]{:S(2)}, u32[]{:S(2)}) collective-permute-start(bf16[512,512]{1,0:T(8,128)(2,1)} %copy-done.55), channel_id=1, source_target_pairs={{0,3},{1,2},{2,1},{3,0},{4,7},{5,6},{6,5},{7,4},{8,11},{9,10},{10,... | collective-permute-start | bytes 1572872 | tf_op jit(solution)/shard_map/ppermute | solution.py:657
  412.8 48.7 %collective-permute-start.57 = (bf16[512,512]{1,0:T(8,128)(2,1)S(1)}, bf16[512,512]{1,0:T(8,128)(2,1)S(1)}, u32[]{:S(2)}, u32[]{:S(2)}) collective-permute-start(bf16[512,512]{1,0:T(8,128)(2,1)S(1)} %copy-done.60), channel_id=1, source_target_pairs={{0,7},{1,6},{2,5},{3,4},{4,3},{5,2},{6,1},{7,0},{8,15},{9,14},{10,... | collective-permute-start | bytes 1572872 | tf_op jit(solution)/shard_map/ppermute | solution.py:657
  414.8 48.0 %collective-permute-start.56 = (bf16[512,512]{1,0:T(8,128)(2,1)S(1)}, bf16[512,512]{1,0:T(8,128)(2,1)}, u32[]{:S(2)}, u32[]{:S(2)}) collective-permute-start(bf16[512,512]{1,0:T(8,128)(2,1)S(1)} %copy-done.58), channel_id=1, source_target_pairs={{0,6},{1,7},{2,4},{3,5},{4,2},{5,3},{6,0},{7,1},{8,14},{9,15},{10,... | collective-permute-start | bytes 1572872 | tf_op jit(solution)/shard_map/ppermute | solution.py:657
  415.4 48.4 %collective-permute-start.55 = (bf16[512,512]{1,0:T(8,128)(2,1)S(1)}, bf16[512,512]{1,0:T(8,128)(2,1)}, u32[]{:S(2)}, u32[]{:S(2)}) collective-permute-start(bf16[512,512]{1,0:T(8,128)(2,1)S(1)} %get-tuple-element.215), channel_id=1, source_target_pairs={{0,5},{1,4},{2,7},{3,6},{4,1},{5,0},{6,3},{7,2},{8,13},{9,12},{10,... | collective-permute-start | bytes 1572872 | tf_op jit(solution)/shard_map/ppermute | solution.py:657
  416.5 48.0 %collective-permute-start.54 = (bf16[512,512]{1,0:T(8,128)(2,1)S(1)}, bf16[512,512]{1,0:T(8,128)(2,1)}, u32[]{:S(2)}, u32[]{:S(2)}) collective-permute-start(bf16[512,512]{1,0:T(8,128)(2,1)S(1)} %get-tuple-element.212), channel_id=1, source_target_pairs={{0,4},{1,5},{2,6},{3,7},{4,0},{5,1},{6,2},{7,3},{8,12},{9,13},{10,... | collective-permute-start | bytes 1572872 | tf_op jit(solution)/shard_map/ppermute | solution.py:657
  461.4 69.6 %collective-permute-start.91 = (bf16[4,4,128,512]{3,2,1,0:T(8,128)(2,1)}, bf16[4,4,128,512]{3,2,1,0:T(8,128)(2,1)}, u32[]{:S(2)}, u32[]{:S(2)}) collective-permute-start(bf16[4,4,128,512]{3,2,1,0:T(8,128)(2,1)} %get-tuple-element.249), channel_id=1, source_target_pairs={{0,1},{1,0},{2,3},{3,2},{4,5},{5,4},{6,7},{7,6},{8,9},{9,8},{10,11... | collective-permute-start | bytes 6291464 | tf_op jit(solution)/shard_map/ppermute | solution.py:657
  462.3 41.1 %collective-permute-start.77 = (bf16[4,4,64,512]{3,2,1,0:T(8,128)(2,1)}, bf16[4,4,64,512]{3,2,1,0:T(8,128)(2,1)S(1)}, u32[]{:S(2)}, u32[]{:S(2)}) collective-permute-start(bf16[4,4,64,512]{3,2,1,0:T(8,128)(2,1)} %get-tuple-element.239), channel_id=1, source_target_pairs={{0,1},{1,0},{2,3},{3,2},{4,5},{5,4},{6,7},{7,6},{8,9},{9,8},{10,11... | collective-permute-start | bytes 3145736 | tf_op jit(solution)/shard_map/ppermute | solution.py:657
  491.1 36.4 %collective-permute-start.63 = (bf16[4,4,64,512]{3,2,1,0:T(8,128)(2,1)}, bf16[4,4,64,512]{3,2,1,0:T(8,128)(2,1)}, u32[]{:S(2)}, u32[]{:S(2)}) collective-permute-start(bf16[4,4,64,512]{3,2,1,0:T(8,128)(2,1)} %get-tuple-element.229), channel_id=1, source_target_pairs={{0,1},{1,0},{2,3},{3,2},{4,5},{5,4},{6,7},{7,6},{8,9},{9,8},{10,11... | collective-permute-start | bytes 3145736 | tf_op jit(solution)/shard_map/ppermute | solution.py:657
  535.9 41.8 %collective-permute-start.92 = (bf16[4,128,512]{2,1,0:T(8,128)(2,1)S(1)}, bf16[4,128,512]{2,1,0:T(8,128)(2,1)S(1)}, u32[]{:S(2)}, u32[]{:S(2)}) collective-permute-start(bf16[4,128,512]{2,1,0:T(8,128)(2,1)S(1)} %get-tuple-element.251), channel_id=1, source_target_pairs={{0,2},{1,3},{2,0},{3,1},{4,6},{5,7},{6,4},{7,5},{8,10},{9,11},{10,... | collective-permute-start | bytes 1572872 | tf_op jit(solution)/shard_map/ppermute | solution.py:657
  539.4 40.8 %collective-permute-start.93 = (bf16[4,128,512]{2,1,0:T(8,128)(2,1)}, bf16[4,128,512]{2,1,0:T(8,128)(2,1)S(1)}, u32[]{:S(2)}, u32[]{:S(2)}) collective-permute-start(bf16[4,128,512]{2,1,0:T(8,128)(2,1)} %get-tuple-element.252), channel_id=1, source_target_pairs={{0,4},{1,5},{2,6},{3,7},{4,0},{5,1},{6,2},{7,3},{8,12},{9,13},{10,... | collective-permute-start | bytes 1572872 | tf_op jit(solution)/shard_map/ppermute | solution.py:657
  542.5 37.8 %collective-permute-start.94 = (bf16[4,128,512]{2,1,0:T(8,128)(2,1)}, bf16[4,128,512]{2,1,0:T(8,128)(2,1)S(1)}, u32[]{:S(2)}, u32[]{:S(2)}) collective-permute-start(bf16[4,128,512]{2,1,0:T(8,128)(2,1)} %get-tuple-element.253), channel_id=1, source_target_pairs={{0,6},{1,7},{2,4},{3,5},{4,2},{5,3},{6,0},{7,1},{8,14},{9,15},{10,... | collective-permute-start | bytes 1572872 | tf_op jit(solution)/shard_map/ppermute | solution.py:657
  (199 other events, 2936.4 us)
Sparse Core Ops, SparseCore 0:
  9.6 66.7 all-gather.4
  78.0 44.0 all-gather.6
  349.7 46.1 reduce-scatter.4
  398.2 43.1 reduce-scatter.2

commit v2 on v1

v2 whole, which is shorter than its diff:
```python
import functools

import jax
import jax.numpy as jnp
from jax import lax
from jax.experimental import pallas as pl
from jax.experimental.pallas import tpu as pltpu
from jax.sharding import PartitionSpec as P

D = 512
FF = 2048
HEADS = 8
HEAD = D // HEADS
PACK = 1024
MOST_LEN = 64
ROWS = 256
QB = 128
KB = QB + 2 * MOST_LEN
EPS = 1e-05
BLOCKED = -1e30
BF = jnp.bfloat16
F32 = jnp.float32
GELU_C = 0.7978845608028654
GELU_A = 0.044715


COST = 4


def mm(left, right):
    return lax.dot_general(left, right, (((1,), (0,)), ((), ())), preferred_element_type=F32)


def mm_t(left, right):
    return lax.dot_general(left, right, (((1,), (1,)), ((), ())), preferred_element_type=F32)


def t_mm(left, right):
    return lax.dot_general(left, right, (((0,), (0,)), ((), ())), preferred_element_type=F32)


def unit_rows(hidden):
    centered = hidden - jnp.mean(hidden, axis=-1, keepdims=True)
    spread = jnp.mean(centered * centered, axis=-1, keepdims=True)
    scale = lax.rsqrt(spread + EPS)
    return centered * scale, scale


def unit_back(unit, scale, gain, grad):
    inner = grad * gain
    first = jnp.mean(inner, axis=-1, keepdims=True)
    second = jnp.mean(inner * unit, axis=-1, keepdims=True)
    return scale * (inner - first - unit * second)


def gelu_both(z):
    square = z * z
    half = 0.5 + 0.5 * jnp.tanh(z * (GELU_C + GELU_C * GELU_A * square))
    act = z * half
    return act, half + (act - act * half) * (2.0 * GELU_C + 6.0 * GELU_C * GELU_A * square)


def call(kernel, out_shape, *args, grid=None, in_specs=None, out_specs=None, scratch=(), mib=62, flops=0, moved=0,
         alias=None, pos=False):
    extra = {}
    if grid is not None and pos:
        extra["grid_spec"] = pltpu.PrefetchScalarGridSpec(
            num_scalar_prefetch=1, grid=grid, in_specs=in_specs, out_specs=out_specs, scratch_shapes=scratch
        )
    else:
        extra["scratch_shapes"] = scratch
        if grid is not None:
            extra.update(grid=grid, in_specs=in_specs, out_specs=out_specs)
        elif pos:
            held = pl.BlockSpec(memory_space=pltpu.VMEM)
            extra["in_specs"] = [pl.BlockSpec(memory_space=pltpu.SMEM)] + [held] * (len(args) - 1)
    if alias:
        extra["input_output_aliases"] = alias
    return pl.pallas_call(
        kernel,
        out_shape=out_shape,
        compiler_params=pltpu.CompilerParams(vmem_limit_bytes=mib << 20),
        cost_estimate=pl.CostEstimate(flops=flops // COST, bytes_accessed=moved // COST, transcendentals=0),
        **extra,
    )(*args)


def sds(shape, dtype):
    return jax.ShapeDtypeStruct(shape, dtype)


WIRE = 512


def piece_rows(split):
    dp, ex = split
    return D // (dp * ex)


def wired(split):
    dp, ex = split
    return piece_rows(split) % 16 == 0 and ex == 8


def near(split, pos_ref, j, k):
    return k * split[1] + jnp.bitwise_xor(pos_ref[0], j)


def send_rows(split, pos_ref, scr_ref, own_ref, core_ref, at, rows):
    dp, ex = split
    for j in range(ex):
        out = core_ref if j % 2 else own_ref
        for k in range(dp):
            start = pl.multiple_of(near(split, pos_ref, j, k) * rows, rows)
            out[j // 2, k, at : at + rows, :] = scr_ref[pl.ds(start, rows), :]


def wire_shapes(split, blocks):
    dp, ex = split
    shape = (ex // 2, dp, blocks * piece_rows(split), WIRE)
    return [sds(shape, BF), sds(shape, BF)]


WINDOW = 3 << 20


class Stage:
    def __init__(self, ins, outs, split_in, split_out, hold_in, hold_out, sem_in, sem_out, order):
        self.ins, self.outs = hold_in, hold_out
        self.split_in, self.split_out = split_in, split_out
        self.out_hbm, self.out_sem, self.sent = outs, sem_out, []
        self.got, self.begun, self.copies, self.bytes = set(), 0, {}, {}
        order = order or [(i, r) for i, parts in enumerate(split_in) for r in range(parts)]
        for n, (i, r) in enumerate(order):
            rows = self.rows(hold_in[i], split_in[i], r)
            self.copies[i, r] = pltpu.make_async_copy(ins[i].at[rows], hold_in[i].at[rows], sem_in.at[n])
            self.bytes[i, r] = hold_in[i].size * hold_in[i].dtype.itemsize // split_in[i]
        self.order = order
        self.ahead(0)

    def rows(self, ref, parts, r):
        size = ref.shape[0] // parts
        return pl.ds(r * size, size)

    def ahead(self, least):
        while self.begun < len(self.order):
            flying = sum(self.bytes[key] for key in self.order[: self.begun] if key not in self.got)
            if self.begun >= least and flying >= WINDOW:
                break
            self.copies[self.order[self.begun]].start()
            self.begun += 1

    def need(self, *which):
        for i in which:
            i, r = i if isinstance(i, tuple) else (i, None)
            for k in range(self.split_in[i]) if r is None else [r]:
                if (i, k) not in self.got:
                    self.ahead(self.order.index((i, k)) + 1)
                    self.copies[i, k].wait()
                    self.got.add((i, k))
                    self.ahead(0)

    def done(self, i, r=None):
        parts = self.split_out[i]
        for k in range(parts) if r is None else [r]:
            rows = self.rows(self.outs[i], parts, k)
            sem = self.out_sem.at[sum(self.split_out[:i]) + k]
            copy = pltpu.make_async_copy(self.outs[i].at[rows], self.out_hbm[i].at[rows], sem)
            copy.start()
            self.sent.append(copy)

    def finish(self):
        self.need(*self.order)
        for copy in self.sent:
            copy.wait()


def staged(body, outs, ins, small=(), small_outs=(), scratch=(), flops=0, moved=0, order=None):
    arrays, split_in = [x for x, _ in ins], [n for _, n in ins]
    shapes, split_out = [x for x, _ in outs], [n for _, n in outs]

    def kernel(*refs):
        at = 0
        groups = []
        for n in (len(small), len(arrays), len(small_outs), len(shapes), len(arrays), len(shapes), len(scratch), 2):
            groups.append(refs[at : at + n])
            at += n
        few, hbm_in, few_out, hbm_out, hold_in, hold_out, own, (sem_in, sem_out) = groups
        stage = Stage(hbm_in, hbm_out, split_in, split_out, hold_in, hold_out, sem_in, sem_out, order)
        body(stage, few, few_out, own)
        stage.finish()

    space = [pl.BlockSpec(memory_space=pltpu.SMEM if x.dtype == jnp.int32 else pltpu.VMEM) for x in small]
    got = pl.pallas_call(
        kernel,
        out_shape=list(small_outs) + shapes,
        in_specs=space + [pl.BlockSpec(memory_space=pl.ANY)] * len(arrays),
        out_specs=[pl.BlockSpec(memory_space=pltpu.VMEM)] * len(small_outs)
        + [pl.BlockSpec(memory_space=pl.ANY)] * len(shapes),
        scratch_shapes=[pltpu.VMEM(x.shape, x.dtype) for x in arrays + shapes]
        + list(scratch)
        + [pltpu.SemaphoreType.DMA((sum(split_in),)), pltpu.SemaphoreType.DMA((max(sum(split_out), 1),))],
        compiler_params=pltpu.CompilerParams(vmem_limit_bytes=62 << 20),
        cost_estimate=pl.CostEstimate(flops=flops // COST, bytes_accessed=moved // COST, transcendentals=0),
    )(*small, *arrays)
    return list(got)


def route_kernel(slots, sent_ref, pair_ref, tok_ref, slot_ref):
    t = lax.broadcasted_iota(jnp.int32, (PACK, 128), 0).astype(F32)
    start, end = sent_ref[0:1, :], sent_ref[1:2, :]
    member = (t >= start) & (t < end)

    def pick(value):
        return jnp.sum(jnp.where(member, value, 0.0), axis=1, keepdims=True)

    lane = lax.broadcasted_iota(jnp.int32, (PACK, 8), 1)
    out = jnp.where(lane == 0, pick(start), 0.0)
    out = jnp.where(lane == 1, pick(end), out)
    for k in range(2):
        base = sent_ref[2 + k : 3 + k, :]
        slot = pick(jnp.where(base >= 0, base - start + t + 1.0, 0.0)) - 1.0
        out = jnp.where(lane == 2 + k, slot, out)
    tok_ref[...] = out
    chunk = 512
    base, length, first = pair_ref[0:1, :], pair_ref[1:2, :], pair_ref[2:3, :]
    gate, task = pair_ref[3:4, :], pair_ref[4:5, :]
    for i in range(slots // chunk):
        s = lax.broadcasted_iota(jnp.int32, (chunk, 128), 0).astype(F32) + float(i * chunk)
        held = (base >= 0) & (s >= base) & (s < base + length)

        def take(value, held=held):
            return jnp.sum(jnp.where(held, value, 0.0), axis=1, keepdims=True)

        lane = lax.broadcasted_iota(jnp.int32, (chunk, 8), 1)
        out = jnp.where(lane == 0, take(first - base + s + 1.0) - 1.0, 0.0)
        out = jnp.where(lane == 1, take(gate), out)
        out = jnp.where(lane == 2, take(task + 1.0) - 1.0, out)
        slot_ref[i * chunk : (i + 1) * chunk, :] = out


def head_halves(block):
    low = lax.broadcasted_iota(jnp.int32, (1, 128), 1) < HEAD
    zero = jnp.zeros_like(block)
    return jnp.concatenate([jnp.where(low, block, zero), jnp.where(low, zero, block)], axis=0)


def merge_halves(stacked):
    low = lax.broadcasted_iota(jnp.int32, (1, 128), 1) < HEAD
    return jnp.where(low, stacked[:QB], stacked[QB:])


def key_start(i):
    return jnp.clip(i * QB - MOST_LEN, 0, PACK - KB)


def attention_kernel(norm_at, last, x_ref, np_ref, tok_ref, w_ref, *refs):
    if last:
        h_ref, a_ref, qkv_ref, ctx_ref, c_ref = refs
    else:
        h_ref, a_ref, qkv_ref, ctx_ref = refs
    gain, shift = np_ref[norm_at : norm_at + 1, :], np_ref[norm_at + 1 : norm_at + 2, :]
    for r in range(PACK // ROWS):
        rows = slice(r * ROWS, (r + 1) * ROWS)
        unit, _ = unit_rows(x_ref[rows, :].astype(F32))
        a = (unit * gain + shift).astype(BF)
        a_ref[rows, :] = a
        qkv_ref[rows, :] = mm(a, w_ref[:, 0 : 3 * D]).astype(BF)

    def block(i, carry):
        q0 = pl.multiple_of(i * QB, QB)
        k0 = pl.multiple_of(key_start(i), MOST_LEN)
        start, end = tok_ref[pl.ds(q0, QB), 0:1], tok_ref[pl.ds(q0, QB), 1:2]
        key = (lax.broadcasted_iota(jnp.int32, (QB, KB), 1) + k0).astype(F32)
        mask = (key >= start) & (key < end)
        mask = jnp.concatenate([mask, mask], axis=0)
        for pair in range(HEADS // 2):
            at = pair * 128
            q = head_halves(qkv_ref[pl.ds(q0, QB), at : at + 128] * BF(HEAD**-0.5))
            k = qkv_ref[pl.ds(k0, KB), D + at : D + at + 128]
            v = qkv_ref[pl.ds(k0, KB), 2 * D + at : 2 * D + at + 128]
            scores = jnp.where(mask, mm_t(q, k), BLOCKED)
            raised = jnp.exp(scores - jnp.max(scores, axis=1, keepdims=True))
            probs = (raised * (1.0 / jnp.sum(raised, axis=1, keepdims=True))).astype(BF)
            ctx_ref[pl.ds(q0, QB), at : at + 128] = merge_halves(mm(probs, v)).astype(BF)
        return carry

    lax.fori_loop(0, PACK // QB, block, 0)
    for r in range(PACK // ROWS):
        rows = slice(r * ROWS, (r + 1) * ROWS)
        h = x_ref[rows, :].astype(F32) + mm(ctx_ref[rows, :], w_ref[:, 3 * D : 4 * D])
        h_ref[rows, :] = h
        if last:
            unit, _ = unit_rows(h)
            c_ref[rows, :] = (unit * np_ref[6:7, :] + np_ref[7:8, :]).astype(BF)


def attention_forward(hidden, params, tok, weights, norm_at, last):
    outs = [sds((PACK, D), F32), sds((PACK, D), BF), sds((PACK, 3 * D), BF), sds((PACK, D), BF)]
    if last:
        outs.append(sds((PACK, D), BF))
    return call(
        functools.partial(attention_kernel, norm_at, last),
        outs, hidden, params, tok, weights,
        flops=6_000_000_000, moved=12 << 20, mib=40,
    )


def combine_grads(io, tok_ref, h_ref, cot_ref, blocks, np_ref, dx_ref, gn_ref, needs):
    for e, ref in enumerate(blocks):
        size = ref.shape[0] // 2
        io.need((needs[2 + e], e % 2))
        part = mm(slots_hot(tok_ref, size, e), ref[e % 2 * size : (e % 2 + 1) * size, :])
        dx_ref[...] = part if e == 0 else dx_ref[...] + part
    io.need(*needs[:2])
    dgain, dshift = jnp.zeros((1, D), F32), jnp.zeros((1, D), F32)
    for r in range(PACK // ROWS):
        rows = slice(r * ROWS, (r + 1) * ROWS)
        dnorm = dx_ref[rows, :]
        unit, scale = unit_rows(h_ref[rows, :])
        dgain += jnp.sum(dnorm * unit, axis=0, keepdims=True)
        dshift += jnp.sum(dnorm, axis=0, keepdims=True)
        dx_ref[rows, :] = cot_ref[rows, :].astype(F32) + unit_back(unit, scale, np_ref[6:7, :], dnorm)
    gn_ref[0:1, :] = dgain
    gn_ref[1:2, :] = dshift


def attention_core_back(io, dx_ref, dx_at, w_ref, w_at, tok_ref, qkv_ref, at_need, dctx_ref, dqkv_ref, acc_ref):
    io.need(w_at)
    for r in range(PACK // ROWS):
        rows = slice(r * ROWS, (r + 1) * ROWS)
        if dx_at is not None:
            io.need((dx_at, r))
        dctx_ref[rows, :] = mm_t(dx_ref[rows, :].astype(BF), w_ref[:, 3 * D : 4 * D]).astype(BF)
    acc_ref[...] = jnp.zeros_like(acc_ref)
    io.need(*at_need)

    def block(i, carry):
        q0 = pl.multiple_of(i * QB, QB)
        k0 = pl.multiple_of(key_start(i), MOST_LEN)
        start, end = tok_ref[pl.ds(k0, KB), 0:1], tok_ref[pl.ds(k0, KB), 1:2]
        query = (lax.broadcasted_iota(jnp.int32, (KB, QB), 1) + q0).astype(F32)
        mask = (query >= start) & (query < end)
        mask = jnp.concatenate([mask, mask], axis=1)
        for pair in range(HEADS // 2):
            at = pair * 128
            q = head_halves(qkv_ref[pl.ds(q0, QB), at : at + 128] * BF(HEAD**-0.5))
            k = qkv_ref[pl.ds(k0, KB), D + at : D + at + 128]
            v = qkv_ref[pl.ds(k0, KB), 2 * D + at : 2 * D + at + 128]
            g = head_halves(dctx_ref[pl.ds(q0, QB), at : at + 128])
            scores = jnp.where(mask, mm_t(k, q), BLOCKED)
            raised = jnp.exp(scores - jnp.max(scores, axis=0, keepdims=True))
            probs = raised * (1.0 / jnp.sum(raised, axis=0, keepdims=True))
            dprobs = mm_t(v, g)
            delta = jnp.sum(probs * dprobs, axis=0, keepdims=True)
            dscores = (probs * (dprobs - delta)).astype(BF)
            acc_ref[pl.ds(k0, KB), at : at + 128] += mm(dscores, q)
            acc_ref[pl.ds(k0, KB), D + at : D + at + 128] += mm(probs.astype(BF), g)
            dq = merge_halves(t_mm(dscores, k)) * (HEAD**-0.5)
            dqkv_ref[pl.ds(q0, QB), at : at + 128] = dq.astype(BF)
        return carry

    lax.fori_loop(0, PACK // QB, block, 0)
    dqkv_ref[:, D:] = acc_ref[...].astype(BF)


def attention_weight_back(split, pos_ref, a_ref, ctx_ref, dx_ref, dqkv_ref, grads, scr_ref):
    rows = piece_rows(split)
    for c in range(4):
        cols = slice(c * D, (c + 1) * D)
        if c < 3:
            grad = t_mm(a_ref[...], dqkv_ref[:, cols]).astype(BF)
        else:
            grad = t_mm(ctx_ref[...], dx_ref[...].astype(BF)).astype(BF)
        if wired(split):
            scr_ref[...] = grad
            send_rows(split, pos_ref, scr_ref, grads[0], grads[1], c * rows, rows)
        else:
            grads[0][:, cols] = grad


def first_back_kernel(split, norm_at, io, few, few_out, own):
    pos_ref, np_ref = few
    tok_ref, h_ref, cot_ref, w_ref, qkv_ref, a_ref, ctx_ref, x_ref = io.ins[:8]
    dx_ref, dctx_ref, dqkv_ref, acc_ref, scr_ref = own
    blocks = io.ins[8:]
    io.need(0)
    combine_grads(io, tok_ref, h_ref, cot_ref, blocks, np_ref, dx_ref, few_out[1], [1, 2] + list(range(8, 8 + len(blocks))))
    attention_core_back(io, dx_ref, None, w_ref, 3, tok_ref, qkv_ref, [4], dctx_ref, dqkv_ref, acc_ref)
    io.need(5, 6, 7)
    attention_weight_back(split, pos_ref, a_ref, ctx_ref, dx_ref, dqkv_ref, io.outs[1:], scr_ref)
    for n in range(1, len(io.outs)):
        io.done(n)
    norm_back_rows(norm_at, dx_ref, x_ref, dqkv_ref, np_ref, w_ref, io.outs[0], few_out[0], io)


def first_backward(pos, blocks, h, cotangent, hidden, saved, params, tok, weights, norm_at, split):
    a, qkv, ctx = saved
    grads = wire_shapes(split, 4) if wired(split) else [sds((D, 4 * D), BF)]
    ins = [(x, 1) for x in (tok, h, cotangent, weights, qkv, a, ctx, hidden)] + [(x, 2) for x in blocks]
    order = [(0, 0)] + [(8 + n, n % 2) for n in range(len(blocks))] + [(n, 0) for n in range(1, 8)]
    norm, norm_moe, out, *grads = staged(
        functools.partial(first_back_kernel, split, norm_at),
        [(sds((PACK, D), F32), 4)] + [(x, 1) for x in grads], ins, [pos, params], [sds((2, D), F32)] * 2,
        [pltpu.VMEM((PACK, D), F32), pltpu.VMEM((PACK, D), BF), pltpu.VMEM((PACK, 3 * D), BF),
         pltpu.VMEM((PACK, 2 * D), F32), pltpu.VMEM((D, D), BF)],
        flops=16_000_000_000, moved=20 << 20, order=order,
    )
    return norm, norm_moe, out, grads


def last_back_kernel(split, norm_at, io, few, few_out, own):
    pos_ref, np_ref, more = few[0], few[1], few[2:]
    dx_ref, w_ref, tok_ref, qkv_ref, a_ref, ctx_ref, x_ref = io.ins
    gn_ref, grads = few_out[0], io.outs[1:]
    dctx_ref, dqkv_ref, acc_ref, scr_ref, row_ref = own
    attention_core_back(io, dx_ref, 0, w_ref, 1, tok_ref, qkv_ref, [2, 3], dctx_ref, dqkv_ref, acc_ref)
    io.need(4, 5, 6)
    attention_weight_back(split, pos_ref, a_ref, ctx_ref, dx_ref, dqkv_ref, grads, scr_ref)
    norm_back_rows(norm_at, dx_ref, x_ref, dqkv_ref, np_ref, w_ref, io.outs[0], gn_ref, io)
    if wired(split):
        dp, ex = split
        rows, wide = piece_rows(split), D // dp
        for n, ref in enumerate((gn_ref,) + tuple(more[:-1])):
            for i in range(2):
                for d in range(dp):
                    row_ref[(2 * n + i) * dp + d : (2 * n + i) * dp + d + 1, :] = ref[i : i + 1, d * wide : (d + 1) * wide]
        first = lax.broadcasted_iota(jnp.int32, (16, WIRE), 0) == 0
        for j in range(ex):
            for k in range(dp):
                at = jnp.bitwise_xor(pos_ref[0], j) * dp + k
                table = jnp.zeros((1, 128), F32) if j else more[-1][0:1, :]
                row = jnp.concatenate(
                    [row_ref[pl.ds(at, 1), :], table, jnp.zeros((1, WIRE - wide - 128), F32)], axis=1
                )
                grads[j % 2][j // 2, k, 4 * rows : 4 * rows + 16, :] = jnp.where(first, row, 0.0).astype(BF)
    for n in range(1, len(io.outs)):
        io.done(n)


def last_backward(pos, dx, hidden, saved, params, tok, weights, norm_at, split, more):
    a, qkv, ctx = saved
    grads = wire_shapes(split, 5) if wired(split) else [sds((D, 4 * D), BF)]
    norm, out, *grads = staged(
        functools.partial(last_back_kernel, split, norm_at),
        [(sds((PACK, D), F32), 4)] + [(x, 1) for x in grads],
        [(dx, 4), (weights, 1), (tok, 1), (qkv, 1), (a, 1), (ctx, 1), (hidden, 1)], [pos, params, *more],
        [sds((2, D), F32)],
        [pltpu.VMEM((PACK, D), BF), pltpu.VMEM((PACK, 3 * D), BF), pltpu.VMEM((PACK, 2 * D), F32),
         pltpu.VMEM((D, D), BF), pltpu.VMEM((8 * split[0], D // split[0]), F32)],
        flops=14_000_000_000, moved=16 << 20,
        order=[(0, 0), (1, 0), (0, 1), (0, 2), (0, 3), (2, 0), (3, 0), (4, 0), (5, 0), (6, 0)],
    )
    return norm, out, grads


def feed_kernel(io, few, few_out, own):
    (np_ref,) = few
    x_ref, up_ref, down_ref = io.ins
    h_ref, n_ref, act_ref, slope_ref = io.outs
    gain, shift = np_ref[2:3, :], np_ref[3:4, :]
    for r in range(PACK // ROWS):
        rows = slice(r * ROWS, (r + 1) * ROWS)
        io.need((0, r))
        x = x_ref[rows, :]
        unit, _ = unit_rows(x)
        n = (unit * gain + shift).astype(BF)
        n_ref[rows, :] = n
        io.need(1)
        act, slope = gelu_both(mm(n, up_ref[...]))
        act = act.astype(BF)
        act_ref[rows, :] = act
        slope_ref[rows, :] = slope.astype(BF)
        io.need(2)
        h_ref[rows, :] = x + mm(act, down_ref[...])
        for i in range(4):
            io.done(i, r)


def feed_forward(hidden, params, up, down):
    return staged(
        feed_kernel,
        [(sds((PACK, D), F32), 4), (sds((PACK, D), BF), 4), (sds((PACK, FF), BF), 4), (sds((PACK, FF), BF), 4)],
        [(hidden, 4), (up, 1), (down, 1)], [params], flops=4_300_000_000, moved=17 << 20,
        order=[(0, 0), (1, 0), (2, 0), (0, 1), (0, 2), (0, 3)],
    )


def feed_back_kernel(split, io, few, few_out, own):
    wire = wired(split)
    pos_ref, np_ref = few
    dx_ref, down_ref, slope_ref, n_ref, act_ref, up_ref, x_ref = io.ins
    out_ref, grads = io.outs[0], io.outs[1:]
    dz_ref, dy_ref, scr_ref, tall_ref = own
    for r in range(PACK // ROWS):
        rows = slice(r * ROWS, (r + 1) * ROWS)
        io.need((0, r), 1, (2, r))
        dy = dx_ref[rows, :].astype(BF)
        dy_ref[rows, :] = dy
        dz_ref[rows, :] = (mm_t(dy, down_ref[...]) * slope_ref[rows, :].astype(F32)).astype(BF)
    io.need(3, 4)
    if wire:
        rows = piece_rows(split)
        for c in range(FF // D):
            scr_ref[...] = t_mm(n_ref[...], dz_ref[:, c * D : (c + 1) * D]).astype(BF)
            send_rows(split, pos_ref, scr_ref, *grads, c * rows, rows)
        for c in range(FF // D):
            tall_ref[c * D : (c + 1) * D, :] = t_mm(act_ref[:, c * D : (c + 1) * D], dy_ref[...]).astype(BF)
        send_rows(split, pos_ref, tall_ref, *grads, FF // D * rows, FF // D * rows)
    else:
        grads[0][...] = t_mm(n_ref[...], dz_ref[...]).astype(BF)
        grads[1][...] = t_mm(act_ref[...], dy_ref[...]).astype(BF)
    io.done(1)
    io.done(2)
    io.need(5, 6)
    norm_back_rows(2, dx_ref, x_ref, dz_ref, np_ref, up_ref, out_ref, few_out[0], io)


def feed_backward(pos, dx, hidden, saved, params, up, down, split):
    n, act, slope = saved
    grads = wire_shapes(split, 8) if wired(split) else [sds((D, FF), BF), sds((FF, D), BF)]
    norm, out, *grads = staged(
        functools.partial(feed_back_kernel, split),
        [(sds((PACK, D), F32), 4)] + [(x, 1) for x in grads],
        [(dx, 4), (down, 1), (slope, 4), (n, 1), (act, 1), (up, 1), (hidden, 1)], [pos, params], [sds((2, D), F32)],
        scratch=[pltpu.VMEM((PACK, FF), BF), pltpu.VMEM((PACK, D), BF), pltpu.VMEM((D, D), BF), pltpu.VMEM((FF, D), BF)],
        order=[(0, 0), (1, 0), (2, 0)] + [(i, r) for r in range(1, 4) for i in (0, 2)] + [(n, 0) for n in range(3, 7)],
        flops=8_600_000_000, moved=24 << 20,
    )
    return norm, out, grads


def norm_back_rows(norm_at, dx_ref, x_ref, grad_ref, np_ref, w_ref, out_ref, gn_ref, io, needs=()):
    gain = np_ref[norm_at : norm_at + 1, :]
    dgain, dshift = jnp.zeros((1, D), F32), jnp.zeros((1, D), F32)
    for r in range(PACK // ROWS):
        rows = slice(r * ROWS, (r + 1) * ROWS)
        for i in needs:
            io.need((i, r))
        dnorm = mm_t(grad_ref[rows, :], w_ref[:, : grad_ref.shape[1]])
        unit, scale = unit_rows(x_ref[rows, :].astype(F32))
        dgain += jnp.sum(dnorm * unit, axis=0, keepdims=True)
        dshift += jnp.sum(dnorm, axis=0, keepdims=True)
        out_ref[rows, :] = dx_ref[rows, :] + unit_back(unit, scale, gain, dnorm)
        io.done(0, r)
    gn_ref[0:1, :] = dgain
    gn_ref[1:2, :] = dshift


def assemble_kernel(split, blocks, tall, *refs):
    dp, ex = split
    rows = piece_rows(split)
    pos_ref, pieces, outs = refs[0], refs[1 : 1 + ex], refs[1 + ex :]
    for j in range(ex):
        for k in range(dp):
            at = lax.rem(pos_ref[1] + dp - k, dp) * ex + jnp.bitwise_xor(pos_ref[0], j)
            start = pl.multiple_of(at * rows, rows)
            for c in range(blocks):
                outs[0][pl.ds(start, rows), c * WIRE : (c + 1) * WIRE] = pieces[j][k, c * rows : (c + 1) * rows, :]
            if tall:
                high = blocks * rows
                start = pl.multiple_of(at * high, high)
                outs[1][pl.ds(start, high), :] = pieces[j][k, high : 2 * high, :]


def assemble(split, pos, pieces, tall):
    outs = [sds((D, 4 * D), BF)] + ([sds((FF, D), BF)] if tall else [])
    return call(
        functools.partial(assemble_kernel, split, 4, tall), outs, pos, *pieces,
        pos=True, flops=1_000_000, moved=4 << 20, mib=24,
    )


def assemble_norm_kernel(split, *refs):
    dp, ex = split
    rows = piece_rows(split)
    pos_ref, pieces, (w_ref, np_ref, scr_ref) = refs[0], refs[1 : 1 + ex], refs[1 + ex :]
    for j in range(ex):
        for k in range(dp):
            at = lax.rem(pos_ref[1] + dp - k, dp) * ex + jnp.bitwise_xor(pos_ref[0], j)
            start = pl.multiple_of(at * rows, rows)
            for c in range(4):
                w_ref[pl.ds(start, rows), c * WIRE : (c + 1) * WIRE] = pieces[j][k, c * rows : (c + 1) * rows, :]
            scr_ref[pl.ds(start, rows), :] = pieces[j][k, 4 * rows : 5 * rows, 0:128].astype(F32)
    np_ref[...] = jnp.transpose(scr_ref[...])[:8]


def add_core_kernel(near, io, few, few_out, own):
    mine_ref, got_ref = io.ins
    for j in range(mine_ref.shape[0]):
        io.need((0, j), (1, j))
        total = (mine_ref[j].astype(F32) + got_ref[j].astype(F32)).astype(BF)
        if near:
            io.outs[j][...] = total
            io.done(j)
        else:
            io.outs[0][jnp.bitwise_xor(few[0][0] // 2, j)] = total
    if not near:
        io.done(0)


def add_near_kernel(lists, pos_ref, *refs):
    ins, outs = refs[: sum(lists)], refs[sum(lists) :]
    dp = len(outs)
    for k, out in enumerate(outs):
        at = lax.rem(pos_ref[1] + k, dp)
        first, top = 0, 0
        for n in lists:
            parts = ins[first : first + n]
            first += n
            parts = [parts[0].at[i] for i in range(parts[0].shape[0])] if n == 1 else parts
            total = parts[0][at].astype(F32)
            for part in parts[1:]:
                total = total + part[at].astype(F32)
            out[top : top + total.shape[0], :] = total.astype(BF)
            top += total.shape[0]


def add_turn_kernel(*refs):
    total = refs[0][...].astype(F32)
    for ref in refs[1:-1]:
        total = total + ref[...].astype(F32)
    refs[-1][...] = total.astype(BF)


def spread_kernel(split, *refs):
    dp, ex = split
    rows = piece_rows(split)
    pos_ref, last_ref, early_ref, qkv_ref, attn_ref, up_ref, down_ref, gn_ref, table_ref = refs

    def put(n, start, piece):
        for c in range(3):
            qkv_ref[n, pl.ds(start, rows), c * D : (c + 1) * D] = piece[c * rows : (c + 1) * rows]
        attn_ref[n, pl.ds(start, rows), :] = piece[3 * rows : 4 * rows]

    for j in range(ex):
        start, high = j * rows, j * 4 * rows
        piece = early_ref[j].astype(F32)
        for c in range(4):
            up_ref[pl.ds(start, rows), c * D : (c + 1) * D] = piece[c * rows : (c + 1) * rows]
        down_ref[pl.ds(high, 4 * rows), :] = piece[4 * rows : 8 * rows]
        put(1, start, piece[8 * rows :])
        piece = last_ref[j].astype(F32)
        put(0, j * rows, piece)
        gn_ref[j : j + 1, :] = piece[4 * rows : 4 * rows + 1, 0 : D // dp]
        table_ref[j : j + 1, :] = piece[4 * rows : 4 * rows + 1, D // dp : D // dp + 128]


def gather_kernel(io, few, few_out, own):
    src_ref, slot_ref = io.ins
    pairs = len(io.outs)
    size = io.outs[0].shape[0] // 2
    tokens = lax.broadcasted_iota(jnp.int32, (size, PACK), 1).astype(F32)
    io.need(0)
    for n in range(2 * pairs):
        io.need((1, n))
        hot = jnp.where(slot_ref[n * size : (n + 1) * size, 0:1] == tokens, 1.0, 0.0).astype(BF)
        io.outs[n // 2][n % 2 * size : (n % 2 + 1) * size, :] = mm(hot, src_ref[...]).astype(BF)
        io.done(n // 2, n % 2)


def gather_rows(slot, source, experts):
    size = slot.shape[0] // experts
    return staged(
        gather_kernel, [(sds((2 * size, D), BF), 2)] * (experts // 2), [(source, 1), (slot, experts)],
        flops=2 * slot.shape[0] * PACK * D, moved=6 << 20,
    )


def gather_near_kernel(at, io, few, few_out, own):
    (pair_ref,) = few
    size = io.outs[0].shape[0] // len(io.ins)
    tokens = lax.broadcasted_iota(jnp.int32, (size, PACK), 1).astype(F32)
    lane = lax.broadcasted_iota(jnp.int32, (size, 8), 1)
    for n, source in enumerate(io.ins):
        one = 8 * (at + n)
        base, length, first, gate, task = [pair_ref[one + i : one + i + 1, :] for i in range(5)]
        s = lax.broadcasted_iota(jnp.int32, (size, 128), 0).astype(F32) + float((at + n) * size)
        held = (base >= 0) & (s >= base) & (s < base + length)

        def take(value, held=held):
            return jnp.sum(jnp.where(held, value, 0.0), axis=1, keepdims=True)

        gate, task = take(gate), take(task + 1.0) - 1.0
        hot = jnp.where(take(first - base + s + 1.0) - 1.0 == tokens, 1.0, 0.0).astype(BF)
        io.need(n)
        rows = slice(n * size, (n + 1) * size)
        io.outs[0][rows, :] = (mm(hot, source[...]) * gate).astype(BF)
        io.outs[1][rows, :] = jnp.where(lane == 0, gate, jnp.where(lane == 1, task, 0.0))
        io.done(0, n)
        io.done(1, n)


def gather_near(pairs, sources, size, at):
    count = len(sources)
    return staged(
        functools.partial(gather_near_kernel, at),
        [(sds((count * size, D), BF), count), (sds((count * size, 8), F32), count)], [(x, 1) for x in sources], [pairs],
        flops=2 * count * size * PACK * D, moved=4 << 20,
    )


def slots_hot(tok_ref, size, n):
    at = lax.broadcasted_iota(jnp.int32, (PACK, size), 1).astype(F32) + float(n * size)
    return jnp.where((tok_ref[:, 2:3] == at) | (tok_ref[:, 3:4] == at), 1.0, 0.0).astype(BF)


def whole(shape):
    return pl.BlockSpec(shape, lambda e: (0,) * len(shape))


def combine_out_kernel(experts, io, few, few_out, own):
    pos_ref = few[0]
    tok_ref, slot_ref, rows_ref, h_ref = io.ins
    acc_ref, size = own[0], rows_ref.shape[0] // experts
    io.need(0, 1, 2)
    for e in range(experts):
        start = pl.multiple_of(jnp.bitwise_xor(pos_ref[0], e) * size, size)
        rows = rows_ref[pl.ds(start, size), :].astype(F32)
        part = mm(slots_hot(tok_ref, size, e), (rows * slot_ref[e * size : (e + 1) * size, 1:2]).astype(BF))
        acc_ref[...] = part if e == 0 else acc_ref[...] + part
    for r in range(PACK // ROWS):
        rows = slice(r * ROWS, (r + 1) * ROWS)
        io.need((3, r))
        io.outs[0][rows, :] = (h_ref[rows, :] + acc_ref[rows, :]).astype(BF)
        io.done(0, r)


def combine_out(pos, tok, slot, rows, hidden, experts):
    return staged(
        functools.partial(combine_out_kernel, experts), [(sds((PACK, D), BF), 4)],
        [(tok, 1), (slot, 1), (rows, 1), (hidden, 4)], [pos], scratch=[pltpu.VMEM((PACK, D), F32)],
        flops=2 * 4096 * PACK * D, moved=14 << 20,
    )[0]


def expert_kernel(count, steps, *refs):
    bufs = refs[1 : 1 + count]
    dout_in, slot_ref, up_ref, down_ref = refs[1 + count : 5 + count]
    dbufs = refs[-count // 2 - 6 : -6]
    table_ref, out_ref, act_ref, du_ref, buf_ref, dout_ref = refs[-6:]
    i = pl.program_id(0)

    @pl.when(i == 0)
    def _():
        table_ref[...] = jnp.zeros_like(table_ref)

    def work(n):
        buf, dout = bufs[n][...], dout_in[...]
        buf_ref[...] = buf
        dout_ref[...] = dout
        z, dact = mm(buf, up_ref[...]), mm_t(dout, down_ref[...])
        act, slope = gelu_both(z)
        act = act.astype(BF)
        act_ref[...] = act
        out = mm(act, down_ref[...]).astype(BF)
        du = (dact * slope).astype(BF)
        du_ref[...] = du
        dbufs[n // 2][...] = mm_t(du, up_ref[...]).astype(BF)
        out_ref[...] = out
        gate, task = slot_ref[:, 0:1], slot_ref[:, 1:2]
        dgate = jnp.sum(out.astype(F32) * dout.astype(F32), axis=1, keepdims=True)
        dgate = jnp.where(task >= 0, dgate / jnp.where(task >= 0, gate, 1.0), 0.0)
        tasks = lax.broadcasted_iota(jnp.int32, (buf.shape[0], 128), 1).astype(F32)
        table_ref[0:1, :] += jnp.sum(jnp.where(tasks == task, dgate, 0.0), axis=0, keepdims=True)

    for n in range(count):
        pl.when(i // steps == n)(functools.partial(work, n))


def expert_rows(pos, bufs, dout, slot, up, down, total, at, held):
    rows = bufs[0].shape[0] // 2
    count = len(bufs)
    size = min(256, rows)
    steps = rows // size
    blocks = [
        pl.BlockSpec((size, D), lambda i, p, n=n: (jnp.clip(i - n * steps, 0, steps - 1) + n % 2 * steps, 0))
        for n in range(count)
    ]
    pairs = [
        pl.BlockSpec((size, D), lambda i, p, n=n: (jnp.clip(i - 2 * n * steps, 0, 2 * steps - 1), 0))
        for n in range(count // 2)
    ]

    def there(i, p):
        return (jnp.bitwise_xor(p[0], at + i // steps) * steps + lax.rem(i, steps), 0)

    def fixed(shape):
        return pl.BlockSpec(shape, lambda i, p: (0, 0), pipeline_mode=pl.Buffered(1))

    first = at * steps

    def tile(cols, first=first):
        return pl.BlockSpec((size, cols), lambda i, p: (i + first, 0))

    alias = {count + 5 + n: count // 2 + 1 + n for n in range(5)} if held else None
    outs = call(
        functools.partial(expert_kernel, count, steps),
        [sds((2 * rows, D), BF)] * (count // 2) + [sds((8, 128), F32)]
        + [sds((total, cols), BF) for cols in (D, FF, FF, D, D)],
        pos, *bufs, dout, slot, up, down, *held,
        grid=(count * steps,), pos=True,
        in_specs=blocks + [tile(D, 0), tile(8, 0), fixed((D, FF)), fixed((FF, D))]
        + [pl.BlockSpec(memory_space=pl.ANY)] * len(held),
        out_specs=pairs + [pl.BlockSpec((8, 128), lambda i, p: (0, 0)), pl.BlockSpec((size, D), there)]
        + [tile(FF), tile(FF), tile(D), tile(D)],
        alias=alias,
        flops=8 * rows * count * D * FF, moved=count * rows * 13 << 10,
    )
    return outs[: count // 2], outs[count // 2], outs[count // 2 + 1 :]


def expert_grad_kernel(steps, act_ref, du_ref, buf_ref, dout_ref, gup_ref, gdown_ref, up_acc, down_acc):
    i = pl.program_id(0)

    @pl.when(i == 0)
    def _():
        up_acc[...] = jnp.zeros_like(up_acc)
        down_acc[...] = jnp.zeros_like(down_acc)

    up_acc[...] += t_mm(buf_ref[...], du_ref[...])
    down_acc[...] += t_mm(act_ref[...], dout_ref[...])

    @pl.when(i == steps - 1)
    def _():
        gup_ref[...] = up_acc[...].astype(BF)
        gdown_ref[...] = down_acc[...].astype(BF)


def expert_grads(act, du, buf, dout):
    rows = buf.shape[0]
    size = 1024
    tile = lambda cols: pl.BlockSpec((size, cols), lambda i: (i, 0))
    return call(
        functools.partial(expert_grad_kernel, rows // size),
        [sds((D, FF), BF), sds((FF, D), BF)], act, du, buf, dout,
        grid=(rows // size,),
        in_specs=[tile(FF), tile(FF), tile(D), tile(D)],
        out_specs=[whole((D, FF)), whole((FF, D))],
        scratch=[pltpu.VMEM((D, FF), F32), pltpu.VMEM((FF, D), F32)],
        flops=4 * rows * D * FF, moved=44 << 20, mib=62,
    )


def route(lengths, task_ids, task_experts, capacity, task_logits, cap_slots, rel):
    sentences = lengths.shape[1]
    experts = capacity.shape[0]
    tasks = task_experts.shape[0]
    lens, ids = lengths.reshape(-1), task_ids.reshape(-1)
    ends = jnp.cumsum(lens)
    starts = ends - lens
    table = jnp.take_along_axis(task_logits, task_experts, axis=1)
    gates = jax.nn.softmax(table, axis=-1)
    hot = ids[:, None] == lax.broadcasted_iota(jnp.int32, (1, tasks), 1)
    expert = jnp.sum(jnp.where(hot[:, :, None], task_experts[None], 0), axis=1)
    gate = jnp.sum(jnp.where(hot[:, :, None], gates[None], 0.0), axis=1)
    pair_expert = expert.reshape(-1)
    pair_len = jnp.repeat(lens, 2)
    expert_hot = (pair_expert[:, None] == lax.broadcasted_iota(jnp.int32, (1, experts), 1)).astype(jnp.int32)
    running = jnp.cumsum(expert_hot * pair_len[:, None], axis=0)
    filled = jnp.sum(running * expert_hot, axis=1)
    limits = jnp.sum(expert_hot * capacity[None, :], axis=1)
    base = jnp.where(filled <= limits, jnp.bitwise_xor(pair_expert, rel) * cap_slots + filled - pair_len, -1)
    base_two = base.reshape(sentences, 2)

    def lanes(rows):
        rows = jnp.stack([row.astype(F32) for row in rows])
        return jnp.pad(rows, ((0, 8 - rows.shape[0]), (0, 128 - rows.shape[1])))

    sent = lanes([starts, ends, base_two[:, 0], base_two[:, 1]])
    pair = lanes([base, pair_len, jnp.repeat(starts, 2), gate.reshape(-1), jnp.repeat(ids, 2)])
    slots = experts * cap_slots
    tok, slot = call(
        functools.partial(route_kernel, slots),
        [sds((PACK, 8), F32), sds((slots, 8), F32)], sent, pair,
        flops=1_000_000, moved=3 << 20, mib=24,
    )
    return tok, slot, pair, gates


EXPERT = ("xy", "core")
BOTH = ("dp", "xy", "core")


def flip(rows, j, ex):
    return lax.ppermute(rows, EXPERT, [(i, i ^ j) for i in range(ex)])


def turn(rows, k, dp):
    return lax.ppermute(rows, "dp", [(i, (i + k) % dp) for i in range(dp)])


def tie(value, *after):
    return lax.optimization_barrier((value,) + after)[0]


def send_even(here, ex):
    return [here] + [flip(here, j, ex) for j in range(2, ex, 2)]


def send_core(even, ex):
    got = []
    for one in even:
        got += [one, flip(one, 1, ex)]
    return got


def add_core(pos, own, got, near=False):
    parts = own.shape[0]
    outs = [(sds(own.shape[1:], BF), 1)] * parts if near else [(sds(own.shape, BF), parts)]
    got = staged(
        functools.partial(add_core_kernel, near), outs, [(own, parts), (got, parts)], [pos],
        order=[(i, j) for j in range(parts) for i in range(2)], flops=1_000_000, moved=own.size * 6,
    )
    return got if near else got[0]


def add_near(pos, *lists):
    lists = [one if isinstance(one, list) else [one] for one in lists]
    rows = sum(one[0].shape[-2] for one in lists)
    dp = lists[0][0].shape[-3]
    return call(
        functools.partial(add_near_kernel, [len(one) for one in lists]), [sds((rows, WIRE), BF)] * dp,
        pos, *sum(lists, []), pos=True, flops=1_000_000, moved=rows << 14,
    )


def send_near(sums, ex):
    return [sums[0]] + [flip(sums[j], 2 * j, ex) for j in range(1, ex // 2)]


def send_turn(sums, dp):
    return [sums[0]] + [turn(sums[k], k, dp) for k in range(1, dp)]


def add_turn(got):
    return call(add_turn_kernel, sds(got[0].shape, BF), *got, flops=1_000_000, moved=got[0].size * 10, mib=62)


def swap(parts, axis):
    return lax.all_to_all(parts, axis, split_axis=0, concat_axis=0, tiled=True)


def local(n_dp, n_ex, hidden_in, lengths, task_ids, task_experts, capacity, task_logits, norm_params,
          w_qkv, w_attn, w_up, w_down, expert_up, expert_down, cotangent):
    experts = capacity.shape[0]
    cap_slots = max(4 * hidden_in.shape[0] // experts, 2 * MOST_LEN)
    slots = experts * cap_slots
    me, here = lax.axis_index(EXPERT), lax.axis_index("dp")
    pos = jnp.stack([me, here]).astype(jnp.int32)
    split = (n_dp, n_ex)
    wire = wired(split)

    def mine(shard):
        rows = shard.shape[0] // n_ex
        return lax.dynamic_slice_in_dim(shard, me * rows, rows, 0)

    def exchange(pair, j):
        return flip(pair, j, n_ex) if j else pair

    tok, slot, pair, gates = route(lengths, task_ids, task_experts, capacity, task_logits, cap_slots, me)
    if wire:
        rows = piece_rows(split)

        def blocks(wide):
            return [wide[:, c * WIRE : (c + 1) * WIRE] for c in range(wide.shape[1] // WIRE)]

        norms = jnp.pad(mine(norm_params), ((0, 0), (0, WIRE - 8)))
        qkv, attn = mine(w_qkv), mine(w_attn)
        piece = blocks(qkv[:, 0]) + [attn[:, 0], norms] + blocks(mine(w_up)) + [mine(w_down)]
        piece = jnp.concatenate(piece + blocks(qkv[:, 1]) + [attn[:, 1]])
        parts = [piece] + [turn(piece, k, n_dp) for k in range(1, n_dp)]
        expert_up, expert_down = tie(expert_up, *parts[1:]), tie(expert_down, *parts[1:])
        zero, feed, one = [
            jnp.stack([part[lo * rows : hi * rows] for part in parts]) for lo, hi in ((0, 5), (5, 13), (13, 17))
        ]
        cots = [cotangent, flip(cotangent, 2, n_ex), flip(cotangent, 4, n_ex)]
        zero = send_even(tie(zero, *cots[1:]), n_ex)
        pairs = pair
        j = 1
        while j < n_ex:
            pairs = jnp.concatenate([pairs, flip(pairs, j, n_ex)])
            j *= 2
        zero = send_core([tie(part, tok, pairs) for part in zero], n_ex)
        feed = send_even(tie(feed, *zero[1:]), n_ex)
        groups = [(0, 2), (2, 6), (6, 8)]

        def gather_group(lo, hi):
            sources = sum([[cots[j], flip(cots[j], 1, n_ex)] for j in range(lo // 2, hi // 2)], [])
            return gather_near(pairs, sources, cap_slots, lo)

        near = [gather_group(*group) for group in groups[:2]]
        attn_zero, params = call(
            functools.partial(assemble_norm_kernel, split), [sds((D, 4 * D), BF), sds((8, D), F32)], pos, *zero,
            scratch=[pltpu.VMEM((D, 128), F32)], pos=True, flops=1_000_000, moved=4 << 20, mib=24,
        )
        fwd = tie(hidden_in, *sum(near, []))
        h1, *saved_zero = attention_forward(fwd, params, tok, attn_zero, 0, False)
        one = send_even(tie(one, h1, *feed[1:]), n_ex)
        feed = send_core([tie(part, h1) for part in feed], n_ex)
        up, down = assemble(split, pos, feed, True)
        h2, *saved_feed = feed_forward(h1, params, up, down)
        one = [tie(part, h2) for part in one]
        cots.append(flip(tie(cotangent, *one[1:]), 6, n_ex))
        one = send_core(one, n_ex)
        attn_one = assemble(split, pos, one, False)[0]
    else:

        def gather_all(shard):
            return lax.all_gather(mine(shard), BOTH, axis=0, tiled=True)

        params = lax.all_gather(norm_params, "dp", axis=0, tiled=True).astype(F32).T
        attn_zero = gather_all(jnp.concatenate([w_qkv[:, 0], w_attn[:, 0]], axis=1))
        up, down = gather_all(w_up), gather_all(w_down)
        attn_one = gather_all(jnp.concatenate([w_qkv[:, 1], w_attn[:, 1]], axis=1))
        h1, *saved_zero = attention_forward(hidden_in, params, tok, attn_zero, 0, False)
        h2, *saved_feed = feed_forward(h1, params, up, down)
        pairs = pair
        j = 1
        while j < n_ex:
            pairs = jnp.concatenate([pairs, flip(pairs, j, n_ex)])
            j *= 2
        groups = [(j, j + 4) for j in range(0, n_ex, 4)]
        cots = [cotangent] + [flip(cotangent, j, n_ex) for j in range(1, n_ex)]
        near = [gather_near(pairs, cots[lo:hi], cap_slots, lo) for lo, hi in groups]
    up_expert = lax.all_gather(expert_up[0], "dp", axis=0, tiled=True)
    down_expert = lax.all_gather(expert_down[0], "dp", axis=0, tiled=True)
    h3, *saved_one, c = attention_forward(h2, params, tok, attn_one, 4, True)
    if wire:
        c = tie(c, cots[-1])
    sent = gather_rows(slot, c, experts)
    if wire:
        near.append(gather_group(*groups[2]))
    sums, held, table = [], (), 0.0
    bufs = {j: exchange(sent[j // 2], j) for j in range(0, groups[-1][0], 2)}
    for n, ((lo, hi), (dout, slot_near)) in enumerate(zip(groups, near)):
        if n == 1:
            for j in range(groups[-1][0], n_ex, 2):
                bufs[j] = exchange(tie(sent[j // 2], *[bufs[i] for i in range(lo, hi, 2)], *sums[:1]), j)
        for j in range(lo, hi, 2):
            bufs[j + 1] = flip(tie(bufs[j], *sums[-1:]), 1, n_ex)
        back, part, held = expert_rows(
            pos, [bufs[j] for j in range(lo, hi)], dout, slot_near, up_expert, down_expert, slots, lo, held
        )
        sums += back
        table = table + part
    out, *held = held
    back = [exchange(pair, 2 * j) for j, pair in enumerate(sums)]
    early_back = len(back) - (groups[-1][1] - groups[-1][0]) // 2
    far = [flip(tie(pair, sums[-1]), 1, n_ex) for pair in back[:early_back]]
    held = [tie(one, *far) for one in held]
    gup_expert, gdown_expert = expert_grads(*held)
    far += [flip(tie(pair, gup_expert), 1, n_ex) for pair in back[early_back:]]
    dbuf_home = sum([list(both) for both in zip(back, far)], [])
    out_home = swap(tie(out, *back, gup_expert).reshape(experts, cap_slots, D), EXPERT).reshape(-1, D)
    gn_one, gn_moe, dx, g_one = first_backward(
        pos, dbuf_home, h3, cotangent, h2, saved_one, params, tok, attn_one, 4, split
    )
    expert_up_sum = lax.psum_scatter(tie(gup_expert, gn_moe), "dp", scatter_dimension=0, tiled=True).astype(F32)
    expert_down_sum = lax.psum_scatter(tie(gdown_expert, gn_moe), "dp", scatter_dimension=0, tiled=True).astype(F32)
    if wire:
        got_one = flip(g_one[1], 1, n_ex)
    gn_feed, dx, g_feed = feed_backward(pos, dx, h1, saved_feed, params, up, down, split)
    if wire:
        got_one = add_core(pos, g_one[0], tie(got_one, gn_feed), True)
        got_feed = flip(tie(g_feed[1], out_home), 1, n_ex)
        sum_feed = add_core(pos, g_feed[0], tie(got_feed, *got_one))
        got_one = send_near(got_one, n_ex)
        dx = tie(dx, sum_feed)
        got_feed = swap(sum_feed, "xy")
    gn_zero, grad_in, g_zero = last_backward(
        pos, dx, hidden_in, saved_zero, params, tok, attn_zero, 0, split, (gn_feed, gn_one, gn_moe, table)
    )
    if wire:
        early = add_near(pos, tie(got_feed, gn_zero), got_one)
        got_zero = flip(tie(g_zero[1], early[0]), 1, n_ex)
        early = send_turn(early, n_dp)
        sum_zero = add_core(pos, g_zero[0], got_zero)
        h3 = tie(h3, sum_zero)
        sum_zero = swap(sum_zero, "xy")
    hidden_out = combine_out(pos, tok, slot, out_home, h3, experts)
    if wire:
        sum_zero = tie(sum_zero, hidden_out)
        early = lax.all_gather(add_turn([tie(one, sum_zero) for one in early]), EXPERT, axis=0)
        sum_zero = add_near(pos, tie(sum_zero, hidden_out, expert_up_sum, expert_down_sum))
        sum_zero = add_turn(send_turn(sum_zero, n_dp))
        last = lax.all_gather(sum_zero, EXPERT, axis=0)
        rows = D // n_dp
        grad_qkv, grad_attn, grad_up, grad_down, gn, sums = call(
            functools.partial(spread_kernel, split),
            [sds((2, rows, 3 * D), F32), sds((2, rows, D), F32), sds((rows, FF), F32), sds((FF // n_dp, D), F32),
             sds((8, rows), F32), sds((experts, 128), F32)],
            pos, last, early,
            pos=True, flops=1_000_000, moved=7 << 20, mib=32,
        )
        grad_qkv, grad_attn, gn = grad_qkv.transpose(1, 0, 2), grad_attn.transpose(1, 0, 2), gn.T
    else:
        small = jnp.concatenate([gn_zero, gn_feed, gn_one, gn_moe], axis=0)
        table = lax.dynamic_update_slice_in_dim(jnp.zeros((experts, 128), F32), table[:1], me, 0)
        small = jnp.concatenate([small, jnp.pad(table, ((0, 0), (0, D - 128)))], axis=0)
        small = lax.psum(small, BOTH)
        gn = lax.dynamic_slice_in_dim(small[:8], here * (D // n_dp), D // n_dp, 1).T
        sums = small[8:]

        def reduce_all(grad):
            rows = grad.shape[0] // (n_dp * n_ex)
            grad = grad.reshape(n_dp, n_ex, rows, -1).transpose(1, 0, 2, 3).reshape(grad.shape)
            part = lax.psum_scatter(grad, EXPERT, scatter_dimension=0, tiled=True)
            part = lax.psum_scatter(part, "dp", scatter_dimension=0, tiled=True)
            return lax.all_gather(part, EXPERT, axis=0, tiled=True).astype(F32)

        g_one, grad_up, grad_down, g_zero = [reduce_all(g) for g in (*g_one, *g_feed, *g_zero)]
        grad_qkv = jnp.stack([g_zero[:, : 3 * D], g_one[:, : 3 * D]], axis=1)
        grad_attn = jnp.stack([g_zero[:, 3 * D :], g_one[:, 3 * D :]], axis=1)
    sums = sums[:, : task_logits.shape[0]].T
    hot = task_experts[:, :, None] == lax.broadcasted_iota(jnp.int32, (1, 1, experts), 2)
    pair_sum = jnp.sum(jnp.where(hot, sums[:, None, :], 0.0), axis=2)
    lean = gates[:, 0] * gates[:, 1] * (pair_sum[:, 0] - pair_sum[:, 1])
    grad_logits = jnp.where(hot[:, 0], lean[:, None], 0.0) - jnp.where(hot[:, 1], lean[:, None], 0.0)
    return (
        hidden_out, grad_in, grad_logits, gn, grad_qkv, grad_attn, grad_up, grad_down,
        expert_up_sum[None], expert_down_sum[None],
    )


def solution(mesh):
    n_dp, n_ex = mesh.shape["dp"], mesh.shape["expert"]
    mesh = jax.sharding.Mesh(mesh.devices.reshape(n_dp, n_ex // 2, 2), BOTH)
    token = P(BOTH, None)
    expert = P(EXPERT, "dp", None)
    in_specs = (
        token, token, token, P(), P(), P(), P("dp", None), P("dp", None, None), P("dp", None, None),
        P("dp", None), P("dp", None), expert, expert, token,
    )
    out_specs = (
        token, token, P(), P("dp", None), P("dp", None, None), P("dp", None, None), P("dp", None), P("dp", None),
        expert, expert,
    )
    step = functools.partial(local, n_dp, n_ex)
    return jax.shard_map(step, mesh=mesh, in_specs=in_specs, out_specs=out_specs, check_vma=False)
```

time: 628 us -> 494 us (0.79)
  waiting for transfers between devices: 198 us -> 61.3 us
  Pallas kernels: 229 us -> 262 us
  starting transfers between devices: 101 us -> 69.7 us
  local copies, waits for them, and re-layouts: 72.9 us -> 54.8 us
  blocking collectives: 0 us -> 12.2 us
    ppermute x87 -> x51, waiting for transfers between devices: 152 us -> 42.6 us  [flip(): return lax.ppermute(rows, EXPERT, [(i, i ^ j) for i in range(ex)])]
    ppermute x87 -> x51, starting transfers between devices: 77.5 us -> 37.4 us  [flip(): return lax.ppermute(rows, EXPERT, [(i, i ^ j) for i in range(ex)])]
    pallas_call x29 -> x27, Pallas kernels: 229 us -> 262 us  [the longest x12 133 us: staged(): pl.pallas_call(kernel, out_shape=list(small_outs) + shapes, in_specs=spac...]
    ppermute x18 -> x9, waiting for transfers between devices: 45.2 us -> 17.2 us  [turn(): return lax.ppermute(rows, 'dp', [(i, (i + k) % dp) for i in range(dp)])]
    unnamed x257 -> x161, local copies, waits for them, and re-layouts: 64.3 us -> 44.2 us
    all_to_all x0 -> x3, starting transfers between devices: none -> 13 us  [swap(): return lax.all_to_all(parts, axis, split_axis=0, concat_axis=0, tiled=True)]
    all_gather x0 -> x1, blocking collectives: none -> 12.2 us  [local(): last = lax.all_gather(sum_zero, EXPERT, axis=0)]
    ppermute x18 -> x9, starting transfers between devices: 23.3 us -> 18.3 us  [turn(): return lax.ppermute(rows, 'dp', [(i, (i + k) % dp) for i in range(dp)])]
  transfers between devices with their start and end apart: 109 -> 68, of which waited for: 32 -> 30; matrix products, arithmetic and copies ran while one was open for 3% -> 3% of each run, Pallas kernels for 30% -> 54%
where the time goes in v2:
time: 494 us; the launch traced here: 484 us
  Pallas kernels  262 us (53%)
  starting transfers between devices  69.7 us (14%)
  waiting for transfers between devices  61.3 us (12%)
  local copies, waits for them, and re-layouts  54.8 us (11%)
  between operations  15.4 us (3%)
  blocking collectives  12.2 us (2%)
  other arithmetic  8.55 us (2%)
    pallas_call x12, Pallas kernels, staged(): pl.pallas_call(kernel, out_shape=list(small_outs) + shapes, in_specs=spac...  133 us
    pallas_call x15, Pallas kernels, call(): pl.pallas_call(kernel, out_shape=out_shape, compiler_params=pltpu.Compile...  129 us
    unnamed x161, local copies, waits for them, and re-layouts  44.2 us
    ppermute x51, waiting for transfers between devices, flip(): return lax.ppermute(rows, EXPERT, [(i, i ^ j) for i in range(ex)])  42.6 us
    ppermute x51, starting transfers between devices, flip(): return lax.ppermute(rows, EXPERT, [(i, i ^ j) for i in range(ex)])  37.4 us
    ppermute x9, starting transfers between devices, turn(): return lax.ppermute(rows, 'dp', [(i, (i + k) % dp) for i in range(dp)])  18.3 us
    ppermute x9, waiting for transfers between devices, turn(): return lax.ppermute(rows, 'dp', [(i, (i + k) % dp) for i in range(dp)])  17.2 us
    all_to_all x3, starting transfers between devices, swap(): return lax.all_to_all(parts, axis, split_axis=0, concat_axis=0, tiled=True)  13 us
  transfers between devices with their start and end apart: 68, of which 30 were waited for; matrix products, arithmetic and copies ran while one was open for 3% of the time, Pallas kernels for 54%

profile of v2, /device:TPU:0, one launch (start us, length us, event | category | flops | bytes accessed | tf_op | source)
XLA Modules:
  0.0 484.4 jit_solution(17537384338491980377)
XLA Ops:
  14.8 5.1 %collective-permute-start.2 = (bf16[272,512]{1,0:T(8,128)(2,1)S(1)}, bf16[272,512]{1,0:T(8,128)(2,1)S(1)}, u32[]{:S(2)}, u32[]{:S(2)}) collective-permute-start(bf16[272,512]{1,0:T(8,128)(2,1)S(1)} %get-tuple-element.312), channel_id=1, source_target_pairs={{0,24},{8,0},{16,8},{24,16},{1,25},{9,1},{17,9},{25,17},{2,26},{10... | collective-permute-start | bytes 835592 | tf_op jit(solution)/shard_map/ppermute | solution.py:890
  30.6 13.0 %collective-permute-done.1 = bf16[272,512]{1,0:T(8,128)(2,1)S(1)} collective-permute-done((bf16[272,512]{1,0:T(8,128)(2,1)S(1)}, bf16[272,512]{1,0:T(8,128)(2,1)S(1)}, u32[]{:S(2)}, u32[]{:S(2)}) %collective-permute-start.1) | collective-permute-done | bytes 278560 | tf_op jit(solution)/shard_map/ppermute | solution.py:890
  55.9 7.4 %collective-permute-done.7 = f32[32,128]{1,0:T(8,128)S(1)} collective-permute-done((f32[32,128]{1,0:T(8,128)S(1)}, f32[32,128]{1,0:T(8,128)S(1)}, u32[]{:S(2)}, u32[]{:S(2)}) %collective-permute-start.7) | collective-permute-done | bytes 16416 | tf_op jit(solution)/shard_map/ppermute | solution.py:886
  76.6 4.6 shard_map.215
  90.2 6.6 %shard_map.216 = (bf16[2048,512]{1,0:T(8,128)(2,1)}, f32[2048,8]{1,0:T(8,128)}) custom-call(f32[64,128]{1,0:T(8,128)} %pad_maximum_fusion.3.refs_0_, bf16[1024,512]{1,0:T(8,128)(2,1)} %collective-permute-done.3.refs_1_, bf16[1024,512]{1,0:T(8,128)(2,1)} %collective-permute-done.16.refs_2_, bf16[1024,512]{1,0:T(8,128)(2,1)} %collective-permute-done.4.refs_3_, ...), custom_call_target="tpu_custom_call" | custom-call | flops 536870912 | bytes 1048576 | tf_op jit(solution)/shard_map/pallas_call | solution.py:194
  99.9 12.1 %shard_map.217 = (f32[1024,512]{1,0:T(8,128)S(1)}, bf16[1024,512]{1,0:T(8,128)(2,1)S(1)}, bf16[1024,1536]{1,0:T(8,128)(2,1)S(1)}, bf16[1024,512]{1,0:T(8,128)(2,1)S(1)}) custom-call(bf16[1024,512]{1,0:T(8,128)(2,1)S(1)} %copy-done.34, f32[8,512]{1,0:T(8,128)S(1)} %get-tuple-element.147.np_ref.refs_0_.refs_1_, ...), custom_call_target="tpu_custom_call" | custom-call | flops 1500000000 | bytes 3145728 | tf_op jit(solution)/shard_map/pallas_call | solution.py:79
  124.3 13.3 %shard_map.219 = (f32[1024,512]{1,0:T(8,128)}, bf16[1024,512]{1,0:T(8,128)(2,1)}, bf16[1024,2048]{1,0:T(8,128)(2,1)}, bf16[1024,2048]{1,0:T(8,128)(2,1)}) custom-call(f32[8,512]{1,0:T(8,128)} %copy-done.28, f32[1024,512]{1,0:T(8,128)} %copy-done.2, bf16[512,2048]{1,0:T(8,128)(2,1)} %copy-done.3, bf16[2048,512]{1,0:T(8,128)(2,1)} %copy-done.4), custom_call_target="tpu_custom_call" | custom-call | flops 1075000064 | bytes 4456448 | tf_op jit(solution)/shard_map/pallas_call | solution.py:194
  144.8 12.6 %shard_map.221 = (f32[1024,512]{1,0:T(8,128)S(1)}, bf16[1024,512]{1,0:T(8,128)(2,1)S(1)}, bf16[1024,1536]{1,0:T(8,128)(2,1)S(1)}, bf16[1024,512]{1,0:T(8,128)(2,1)S(1)}, bf16[1024,512]{1,0:T(8,128)(2,1)S(1)}) custom-call(f32[1024,512]{1,0:T(8,128)S(1)} %copy-done.10, f32[8,512]{1,0:T(8,128)S(1)} %copy-done.29, ...), custom_call_target="tpu_custom_call" | custom-call | flops 1500000000 | bytes 3145728 | tf_op jit(solution)/shard_map/pallas_call | solution.py:79
  164.7 8.2 %shard_map.222 = (bf16[1024,512]{1,0:T(8,128)(2,1)}, bf16[1024,512]{1,0:T(8,128)(2,1)}, bf16[1024,512]{1,0:T(8,128)(2,1)}, bf16[1024,512]{1,0:T(8,128)(2,1)}) custom-call(bf16[1024,512]{1,0:T(8,128)(2,1)} %copy-done.35, f32[4096,8]{1,0:T(8,128)} %copy-done.8), custom_call_target="tpu_custom_call" | custom-call | flops 1073741824 | bytes 1572864 | tf_op jit(solution)/shard_map/pallas_call | solution.py:194
  176.0 16.5 %shard_map.223 = (bf16[1024,512]{1,0:T(8,128)(2,1)}, f32[8,128]{1,0:T(8,128)}, bf16[4096,512]{1,0:T(8,128)(2,1)}, bf16[4096,2048]{1,0:T(8,128)(2,1)}, bf16[4096,...) custom-call(s32[2]{0:T(128)} %copy-done.30, bf16[1024,512]{1,0:T(8,128)(2,1)} %get-tuple-element.174.refs_1_, ...), custom_call_target="tpu_custom_call" | custom-call | flops 2147483648 | bytes 3407872 | tf_op jit(solution)/shard_map/pallas_call | solution.py:79
  192.5 6.3 %collective-permute-done.33.refs_1_ = bf16[1024,512]{1,0:T(8,128)(2,1)S(1)} collective-permute-done((bf16[1024,512]{1,0:T(8,128)(2,1)}, bf16[1024,512]{1,0:T(8,128)(2,1)S(1)}, u32[]{:S(2)}, u32[]{:S(2)}) %collective-permute-start.33) | collective-permute-done | bytes 1048608 | tf_op jit(solution)/shard_map/ppermute | solution.py:886
  204.2 29.4 %shard_map.224 = (bf16[1024,512]{1,0:T(8,128)(2,1)}, bf16[1024,512]{1,0:T(8,128)(2,1)}, f32[8,128]{1,0:T(8,128)}, bf16[4096,512]{1,0:T(8,128)(2,1)}, bf16[4096,2...) custom-call(s32[2]{0:T(128)} %copy-done.30, ...), custom_call_target="tpu_custom_call", output_to_operand_aliasing={{3}: (9, {}), {4}: (10, {}), {5}: (11, {}), {6}: (12, {}), ... | custom-call | flops 4294967296 | bytes 6815744 | tf_op jit(solution)/shard_map/pallas_call | solution.py:79
  236.6 4.6 shard_map.225
  242.2 16.6 %shard_map.226 = (bf16[1024,512]{1,0:T(8,128)(2,1)}, f32[8,128]{1,0:T(8,128)}, bf16[4096,512]{1,0:T(8,128)(2,1)}, bf16[4096,2048]{1,0:T(8,128)(2,1)}, bf16[4096,...) custom-call(s32[2]{0:T(128)} %copy-done.30, ...), custom_call_target="tpu_custom_call", output_to_operand_aliasing={{2}: (7, {}), {3}: (8, {}), {4}: (9, {}), {5}: (10, {}), {6... | custom-call | flops 2147483648 | bytes 3407872 | tf_op jit(solution)/shard_map/pallas_call | solution.py:79
  264.8 25.3 %shard_map.227 = (bf16[512,2048]{1,0:T(8,128)(2,1)}, bf16[2048,512]{1,0:T(8,128)(2,1)}) custom-call(bf16[4096,2048]{1,0:T(8,128)(2,1)} %get-tuple-element.202.act_ref, bf16[4096,2048]{1,0:T(8,128)(2,1)} %get-tuple-element.204.du_ref, bf16[4096,512]{1,0:T(8,128)(2,1)} %get-tuple-element.206.buf_ref, bf16[4096,512]{1,0:T(8,128)(2,1)} %get-tuple-element.208.dout_ref), custom_call_target="tpu_custom_call" | custom-call | flops 4294967296 | bytes 11534336 | tf_op jit(solution)/shard_map/pallas_call | solution.py:79
  290.3 4.6 all-to-all-start
  296.3 31.4 %shard_map.228 = (f32[2,512]{1,0:T(2,128)}, f32[2,512]{1,0:T(2,128)}, f32[1024,512]{1,0:T(8,128)}, bf16[4,4,64,512]{3,2,1,0:T(8,128)(2,1)}, bf16[4,4,64,512]{3,2,1,0:T(8,128)(2,1)}) custom-call(s32[2]{0:T(128)} %copy-done.30, f32[8,512]{1,0:T(8,128)} %copy-done.28, f32[1024,8]{1,0:T(8,128)} %copy-done.9, f32[1024,512]{1,0:T(8,128)} %copy-done.5, ...), custom_call_target="tpu_custom_call" | custom-call | flops 4000000000 | bytes 5242880 | tf_op jit(solution)/shard_map/pallas_call | solution.py:194
  328.0 17.1 %shard_map.229 = (f32[2,512]{1,0:T(2,128)}, f32[1024,512]{1,0:T(8,128)}, bf16[4,4,128,512]{3,2,1,0:T(8,128)(2,1)}, bf16[4,4,128,512]{3,2,1,0:T(8,128)(2,1)}) custom-call(s32[2]{0:T(128)} %copy-done.30, f32[8,512]{1,0:T(8,128)} %copy-done.28, f32[1024,512]{1,0:T(8,128)} %get-tuple-element.216.refs_2_, bf16[2048,512]{1,0:T(8,128)(2,1)} %copy-done.4, ...), custom_call_target="tpu_custom_call" | custom-call | flops 2150000128 | bytes 6291456 | tf_op jit(solution)/shard_map/pallas_call | solution.py:194
  345.7 5.3 %collective-permute-done.49.refs_2_ = bf16[4,4,64,512]{3,2,1,0:T(8,128)(2,1)S(1)} collective-permute-done((bf16[4,4,64,512]{3,2,1,0:T(8,128)(2,1)}, bf16[4,4,64,512]{3,2,1,0:T(8,128)(2,1)S(1)}, u32[]{:S(2)}, u32[]{:S(2)}) %collective-permute-start.49) | collective-permute-done | bytes 1048608 | tf_op jit(solution)/shard_map/ppermute | solution.py:886
  355.1 4.6 shard_map.231
  359.8 4.9 %all-to-all-start.1 = ((bf16[4,4,128,512]{3,2,1,0:T(8,128)(2,1)}), bf16[4,4,128,512]{3,2,1,0:T(8,128)(2,1)}, u32[]{:S(2)}, u32[]{:S(2)}) async-start(bf16[4,4,128,512]{3,2,1,0:T(8,128)(2,1)} %shard_map.231), calls=%async_computation.1 | async-start | bytes 4194304 | tf_op jit(solution)/shard_map/all_to_all | solution.py:941
  368.8 26.0 %shard_map.232 = (f32[2,512]{1,0:T(2,128)}, f32[1024,512]{1,0:T(8,128)}, bf16[4,4,80,512]{3,2,1,0:T(8,128)(2,1)}, bf16[4,4,80,512]{3,2,1,0:T(8,128)(2,1)}) custom-call(s32[2]{0:T(128)} %copy-done.30, f32[8,512]{1,0:T(8,128)} %copy-done.28, f32[2,512]{1,0:T(2,128)} %get-tuple-element.220.refs_2_, f32[2,512]{1,0:T(2,128)} %get-tuple-element.221.refs_3_, ...), custom_call_target="tpu_custom_call" | custom-call | flops 3500000000 | bytes 4194304 | tf_op jit(solution)/shard_map/pallas_call | solution.py:194
  396.4 5.9 %collective-permute-done.52.refs_4_ = bf16[4,64,512]{2,1,0:T(8,128)(2,1)S(1)} collective-permute-done((bf16[4,64,512]{2,1,0:T(8,128)(2,1)S(1)}, bf16[4,64,512]{2,1,0:T(8,128)(2,1)S(1)}, u32[]{:S(2)}, u32[]{:S(2)}) %collective-permute-start.52) | collective-permute-done | bytes 262176 | tf_op jit(solution)/shard_map/ppermute | solution.py:886
  403.1 3.1 shard_map.233
  406.1 3.2 collective-permute-done.53.refs_2_
  410.4 3.6 shard_map.234
  414.1 3.6 all-to-all-start.2
  420.4 3.1 collective-permute-start.59
  423.5 10.1 %shard_map.235 = bf16[1024,512]{1,0:T(8,128)(2,1)} custom-call(s32[2]{0:T(128)} %copy-done.30, f32[1024,8]{1,0:T(8,128)} %copy-done.9, f32[4096,8]{1,0:T(8,128)} %copy-done.8, bf16[4096,512]{1,0:T(8,128)(2,1)} %bitcast.29.refs_3_, f32[1024,512]{1,0:T(8,128)} %copy-done.5), custom_call_target="tpu_custom_call" | custom-call | flops 1073741824 | bytes 3670016 | tf_op jit(solution)/shard_map/pallas_call | solution.py:194
  442.9 3.2 collective-permute-start.54
  446.1 3.1 collective-permute-start.55
  457.3 12.2 %all-gather.2 = bf16[640,512]{1,0:T(8,128)(2,1)S(1)} all-gather(bf16[80,512]{1,0:T(8,128)(2,1)} %shard_map.237), channel_id=4, replica_groups=mesh['dp'=4,'xy'=4,'core'=2] {'xy','core'}, dimensions={0}, use_global_device_ids=true | all-gather | bytes 737280 | tf_op jit(solution)/shard_map/all_gather | solution.py:1087
  (376 shorter events, 142.5 us)
Async XLA Ops:
  7.2 168.7 %all-gather.8.cloned.1.call-start = ((), (), s32[]{:S(2)}) async-start(), calls=%async_computation.7 | async-start | bytes 2621440 | tf_op jit(solution)/shard_map/all_gather | solution.py:1026
  19.9 23.7 %collective-permute-start.1 = (bf16[272,512]{1,0:T(8,128)(2,1)S(1)}, bf16[272,512]{1,0:T(8,128)(2,1)S(1)}, u32[]{:S(2)}, u32[]{:S(2)}) collective-permute-start(bf16[272,512]{1,0:T(8,128)(2,1)S(1)} %get-tuple-element.312), channel_id=1, source_target_pairs={{0,16},{8,24},{16,0},{24,8},{1,17},{9,25},{17,1},{25,9},{2,18},{10... | collective-permute-start | bytes 835592 | tf_op jit(solution)/shard_map/ppermute | solution.py:890
  19.9 23.7 %collective-permute-start = (bf16[272,512]{1,0:T(8,128)(2,1)S(1)}, bf16[272,512]{1,0:T(8,128)(2,1)S(1)}, u32[]{:S(2)}, u32[]{:S(2)}) collective-permute-start(bf16[272,512]{1,0:T(8,128)(2,1)S(1)} %get-tuple-element.312), channel_id=1, source_target_pairs={{0,8},{8,16},{16,24},{24,0},{1,9},{9,17},{17,25},{25,1},{2,10},{10... | collective-permute-start | bytes 835592 | tf_op jit(solution)/shard_map/ppermute | solution.py:890
  20.9 26.0 %collective-permute-start.3 = (bf16[1024,512]{1,0:T(8,128)(2,1)}, bf16[1024,512]{1,0:T(8,128)(2,1)}, u32[]{:S(2)}, u32[]{:S(2)}) collective-permute-start(bf16[1024,512]{1,0:T(8,128)(2,1)} %refs_4_.1), channel_id=1, source_target_pairs={{0,2},{1,3},{2,0},{3,1},{4,6},{5,7},{6,4},{7,5},{8,10},{9,11},{10,... | collective-permute-start | bytes 3145736 | tf_op jit(solution)/shard_map/ppermute | solution.py:886
  22.4 24.5 %collective-permute-start.4 = (bf16[1024,512]{1,0:T(8,128)(2,1)}, bf16[1024,512]{1,0:T(8,128)(2,1)}, u32[]{:S(2)}, u32[]{:S(2)}) collective-permute-start(bf16[1024,512]{1,0:T(8,128)(2,1)} %refs_4_.1), channel_id=1, source_target_pairs={{0,4},{1,5},{2,6},{3,7},{4,0},{5,1},{6,2},{7,3},{8,12},{9,13},{10,... | collective-permute-start | bytes 3145736 | tf_op jit(solution)/shard_map/ppermute | solution.py:886
  30.5 44.4 %collective-permute-start.15 = (bf16[1024,512]{1,0:T(8,128)(2,1)}, bf16[1024,512]{1,0:T(8,128)(2,1)}, u32[]{:S(2)}, u32[]{:S(2)}) collective-permute-start(bf16[1024,512]{1,0:T(8,128)(2,1)} %refs_4_.1), channel_id=1, source_target_pairs={{0,1},{1,0},{2,3},{3,2},{4,5},{5,4},{6,7},{7,6},{8,9},{9,8},{10,11... | collective-permute-start | bytes 3145736 | tf_op jit(solution)/shard_map/ppermute | solution.py:886
  43.7 132.3 %all-gather.10.cloned.1.call-start = ((), (), s32[]{:S(2)}) async-start(), calls=%async_computation.8 | async-start | bytes 2621440 | tf_op jit(solution)/shard_map/all_gather | solution.py:1027
  63.9 26.4 %collective-permute-start.16 = (bf16[1024,512]{1,0:T(8,128)(2,1)}, bf16[1024,512]{1,0:T(8,128)(2,1)}, u32[]{:S(2)}, u32[]{:S(2)}) collective-permute-start(bf16[1024,512]{1,0:T(8,128)(2,1)} %collective-permute-done.3.refs_1_), channel_id=1, source_target_pairs={{0,1},{1,0},{2,3},{3,2},{4,5},{5,4},{6,7},{7,6},{8,9},{9,8},{10,11... | collective-permute-start | bytes 3145736 | tf_op jit(solution)/shard_map/ppermute | solution.py:886
  64.4 25.8 %collective-permute-start.17 = (bf16[1024,512]{1,0:T(8,128)(2,1)}, bf16[1024,512]{1,0:T(8,128)(2,1)}, u32[]{:S(2)}, u32[]{:S(2)}) collective-permute-start(bf16[1024,512]{1,0:T(8,128)(2,1)} %collective-permute-done.4.refs_3_), channel_id=1, source_target_pairs={{0,1},{1,0},{2,3},{3,2},{4,5},{5,4},{6,7},{7,6},{8,9},{9,8},{10,11... | collective-permute-start | bytes 3145736 | tf_op jit(solution)/shard_map/ppermute | solution.py:886
  71.0 42.7 %collective-permute-start.19 = (bf16[4,128,512]{2,1,0:T(8,128)(2,1)S(1)}, bf16[4,128,512]{2,1,0:T(8,128)(2,1)S(1)}, u32[]{:S(2)}, u32[]{:S(2)}) collective-permute-start(bf16[4,128,512]{2,1,0:T(8,128)(2,1)S(1)} %pad_maximum_fusion.refs_1_), channel_id=1, source_target_pairs={{0,2},{1,3},{2,0},{3,1},{4,6},{5,7},{6,4},{7,5},{8,10},{9,11},{10,... | collective-permute-start | bytes 1572872 | tf_op jit(solution)/shard_map/ppermute | solution.py:886
  73.4 40.8 %collective-permute-start.21 = (bf16[4,128,512]{2,1,0:T(8,128)(2,1)S(1)}, bf16[4,128,512]{2,1,0:T(8,128)(2,1)}, u32[]{:S(2)}, u32[]{:S(2)}) collective-permute-start(bf16[4,128,512]{2,1,0:T(8,128)(2,1)S(1)} %pad_maximum_fusion.refs_1_), channel_id=1, source_target_pairs={{0,4},{1,5},{2,6},{3,7},{4,0},{5,1},{6,2},{7,3},{8,12},{9,13},{10,... | collective-permute-start | bytes 1572872 | tf_op jit(solution)/shard_map/ppermute | solution.py:886
  75.0 39.3 %collective-permute-start.23 = (bf16[4,128,512]{2,1,0:T(8,128)(2,1)S(1)}, bf16[4,128,512]{2,1,0:T(8,128)(2,1)}, u32[]{:S(2)}, u32[]{:S(2)}) collective-permute-start(bf16[4,128,512]{2,1,0:T(8,128)(2,1)S(1)} %pad_maximum_fusion.refs_1_), channel_id=1, source_target_pairs={{0,6},{1,7},{2,4},{3,5},{4,2},{5,3},{6,0},{7,1},{8,14},{9,15},{10,... | collective-permute-start | bytes 1572872 | tf_op jit(solution)/shard_map/ppermute | solution.py:886
  116.5 21.1 %collective-permute-start.26 = (bf16[4,64,512]{2,1,0:T(8,128)(2,1)S(1)}, bf16[4,64,512]{2,1,0:T(8,128)(2,1)}, u32[]{:S(2)}, u32[]{:S(2)}) collective-permute-start(bf16[4,64,512]{2,1,0:T(8,128)(2,1)S(1)} %pad_maximum_fusion.2.refs_1_), channel_id=1, source_target_pairs={{0,2},{1,3},{2,0},{3,1},{4,6},{5,7},{6,4},{7,5},{8,10},{9,11},{10,... | collective-permute-start | bytes 786440 | tf_op jit(solution)/shard_map/ppermute | solution.py:886
  118.5 19.1 %collective-permute-start.28 = (bf16[4,64,512]{2,1,0:T(8,128)(2,1)S(1)}, bf16[4,64,512]{2,1,0:T(8,128)(2,1)}, u32[]{:S(2)}, u32[]{:S(2)}) collective-permute-start(bf16[4,64,512]{2,1,0:T(8,128)(2,1)S(1)} %pad_maximum_fusion.2.refs_1_), channel_id=1, source_target_pairs={{0,4},{1,5},{2,6},{3,7},{4,0},{5,1},{6,2},{7,3},{8,12},{9,13},{10,... | collective-permute-start | bytes 786440 | tf_op jit(solution)/shard_map/ppermute | solution.py:886
  120.1 17.6 %collective-permute-start.30 = (bf16[4,64,512]{2,1,0:T(8,128)(2,1)S(1)}, bf16[4,64,512]{2,1,0:T(8,128)(2,1)}, u32[]{:S(2)}, u32[]{:S(2)}) collective-permute-start(bf16[4,64,512]{2,1,0:T(8,128)(2,1)S(1)} %pad_maximum_fusion.2.refs_1_), channel_id=1, source_target_pairs={{0,6},{1,7},{2,4},{3,5},{4,2},{5,3},{6,0},{7,1},{8,14},{9,15},{10,... | collective-permute-start | bytes 786440 | tf_op jit(solution)/shard_map/ppermute | solution.py:886
  137.7 26.0 %collective-permute-start.32 = (bf16[1024,512]{1,0:T(8,128)(2,1)}, bf16[1024,512]{1,0:T(8,128)(2,1)S(1)}, u32[]{:S(2)}, u32[]{:S(2)}) collective-permute-start(bf16[1024,512]{1,0:T(8,128)(2,1)} %refs_4_.1), channel_id=1, source_target_pairs={{0,6},{1,7},{2,4},{3,5},{4,2},{5,3},{6,0},{7,1},{8,14},{9,15},{10,... | collective-permute-start | bytes 3145736 | tf_op jit(solution)/shard_map/ppermute | solution.py:886
  173.0 25.8 %collective-permute-start.33 = (bf16[1024,512]{1,0:T(8,128)(2,1)}, bf16[1024,512]{1,0:T(8,128)(2,1)S(1)}, u32[]{:S(2)}, u32[]{:S(2)}) collective-permute-start(bf16[1024,512]{1,0:T(8,128)(2,1)} %get-tuple-element.172), channel_id=1, source_target_pairs={{0,2},{1,3},{2,0},{3,1},{4,6},{5,7},{6,4},{7,5},{8,10},{9,11},{10,... | collective-permute-start | bytes 3145736 | tf_op jit(solution)/shard_map/ppermute | solution.py:886
  174.4 25.5 %collective-permute-start.34 = (bf16[1024,512]{1,0:T(8,128)(2,1)}, bf16[1024,512]{1,0:T(8,128)(2,1)}, u32[]{:S(2)}, u32[]{:S(2)}) collective-permute-start(bf16[1024,512]{1,0:T(8,128)(2,1)} %get-tuple-element.173), channel_id=1, source_target_pairs={{0,4},{1,5},{2,6},{3,7},{4,0},{5,1},{6,2},{7,3},{8,12},{9,13},{10,... | collective-permute-start | bytes 3145736 | tf_op jit(solution)/shard_map/ppermute | solution.py:886
  200.0 33.6 %collective-permute-start.36 = (bf16[1024,512]{1,0:T(8,128)(2,1)}, bf16[1024,512]{1,0:T(8,128)(2,1)}, u32[]{:S(2)}, u32[]{:S(2)}) collective-permute-start(bf16[1024,512]{1,0:T(8,128)(2,1)} %get-tuple-element.178), channel_id=1, source_target_pairs={{0,6},{1,7},{2,4},{3,5},{4,2},{5,3},{6,0},{7,1},{8,14},{9,15},{10,... | collective-permute-start | bytes 3145736 | tf_op jit(solution)/shard_map/ppermute | solution.py:886
  201.6 35.0 %collective-permute-start.40 = (bf16[1024,512]{1,0:T(8,128)(2,1)}, bf16[1024,512]{1,0:T(8,128)(2,1)}, u32[]{:S(2)}, u32[]{:S(2)}) collective-permute-start(bf16[1024,512]{1,0:T(8,128)(2,1)} %copy-done.46), channel_id=1, source_target_pairs={{0,1},{1,0},{2,3},{3,2},{4,5},{5,4},{6,7},{7,6},{8,9},{9,8},{10,11... | collective-permute-start | bytes 3145736 | tf_op jit(solution)/shard_map/ppermute | solution.py:886
  233.8 25.8 %collective-permute-start.41 = (bf16[1024,512]{1,0:T(8,128)(2,1)}, bf16[1024,512]{1,0:T(8,128)(2,1)}, u32[]{:S(2)}, u32[]{:S(2)}) collective-permute-start(bf16[1024,512]{1,0:T(8,128)(2,1)} %get-tuple-element.196), channel_id=1, source_target_pairs={{0,2},{1,3},{2,0},{3,1},{4,6},{5,7},{6,4},{7,5},{8,10},{9,11},{10,... | collective-permute-start | bytes 3145736 | tf_op jit(solution)/shard_map/ppermute | solution.py:886
  235.1 25.5 %collective-permute-start.42 = (bf16[1024,512]{1,0:T(8,128)(2,1)}, bf16[1024,512]{1,0:T(8,128)(2,1)}, u32[]{:S(2)}, u32[]{:S(2)}) collective-permute-start(bf16[1024,512]{1,0:T(8,128)(2,1)} %get-tuple-element.186), channel_id=1, source_target_pairs={{0,4},{1,5},{2,6},{3,7},{4,0},{5,1},{6,2},{7,3},{8,12},{9,13},{10,... | collective-permute-start | bytes 3145736 | tf_op jit(solution)/shard_map/ppermute | solution.py:886
  260.6 29.5 %collective-permute-start.43 = (bf16[1024,512]{1,0:T(8,128)(2,1)}, bf16[1024,512]{1,0:T(8,128)(2,1)}, u32[]{:S(2)}, u32[]{:S(2)}) collective-permute-start(bf16[1024,512]{1,0:T(8,128)(2,1)} %get-tuple-element.197), channel_id=1, source_target_pairs={{0,6},{1,7},{2,4},{3,5},{4,2},{5,3},{6,0},{7,1},{8,14},{9,15},{10,... | collective-permute-start | bytes 3145736 | tf_op jit(solution)/shard_map/ppermute | solution.py:886
  290.3 54.8 %all-to-all-start = ((bf16[8,512,512]{2,1,0:T(8,128)(2,1)}), bf16[8,512,512]{2,1,0:T(8,128)(2,1)}, u32[]{:S(2)}, u32[]{:S(2)}) async-start(bf16[8,512,512]{2,1,0:T(8,128)(2,1)} %bitcast.93), calls=%async_computation | async-start | bytes 8388608 | tf_op jit(solution)/shard_map/all_to_all | solution.py:941
  294.9 143.8 %reduce-scatter.3.cloned.1.call-start = ((), (), s32[]{:S(2)}) async-start(), calls=%async_computation.5 | async-start | bytes 2621440 | tf_op jit(solution)/shard_map/reduce_scatter | solution.py:1059
  327.7 121.5 %reduce-scatter.5.cloned.1.call-start = ((), (), s32[]{:S(2)}) async-start(), calls=%async_computation.6 | async-start | bytes 2621440 | tf_op jit(solution)/shard_map/reduce_scatter | solution.py:1060
  359.8 35.0 %all-to-all-start.1 = ((bf16[4,4,128,512]{3,2,1,0:T(8,128)(2,1)}), bf16[4,4,128,512]{3,2,1,0:T(8,128)(2,1)}, u32[]{:S(2)}, u32[]{:S(2)}) async-start(bf16[4,4,128,512]{3,2,1,0:T(8,128)(2,1)} %shard_map.231), calls=%async_computation.1 | async-start | bytes 4194304 | tf_op jit(solution)/shard_map/all_to_all | solution.py:941
  365.3 31.2 %collective-permute-start.50 = (bf16[4,64,512]{2,1,0:T(8,128)(2,1)S(1)}, bf16[4,64,512]{2,1,0:T(8,128)(2,1)S(1)}, u32[]{:S(2)}, u32[]{:S(2)}) collective-permute-start(bf16[4,64,512]{2,1,0:T(8,128)(2,1)S(1)} %copy-done.71), channel_id=1, source_target_pairs={{0,2},{1,3},{2,0},{3,1},{4,6},{5,7},{6,4},{7,5},{8,10},{9,11},{10,... | collective-permute-start | bytes 786440 | tf_op jit(solution)/shard_map/ppermute | solution.py:886
  367.3 29.2 %collective-permute-start.51 = (bf16[4,64,512]{2,1,0:T(8,128)(2,1)S(1)}, bf16[4,64,512]{2,1,0:T(8,128)(2,1)S(1)}, u32[]{:S(2)}, u32[]{:S(2)}) collective-permute-start(bf16[4,64,512]{2,1,0:T(8,128)(2,1)S(1)} %copy-done.70), channel_id=1, source_target_pairs={{0,4},{1,5},{2,6},{3,7},{4,0},{5,1},{6,2},{7,3},{8,12},{9,13},{10,... | collective-permute-start | bytes 786440 | tf_op jit(solution)/shard_map/ppermute | solution.py:886
  368.7 33.6 %collective-permute-start.52 = (bf16[4,64,512]{2,1,0:T(8,128)(2,1)S(1)}, bf16[4,64,512]{2,1,0:T(8,128)(2,1)S(1)}, u32[]{:S(2)}, u32[]{:S(2)}) collective-permute-start(bf16[4,64,512]{2,1,0:T(8,128)(2,1)S(1)} %copy-done.69), channel_id=1, source_target_pairs={{0,6},{1,7},{2,4},{3,5},{4,2},{5,3},{6,0},{7,1},{8,14},{9,15},{10,... | collective-permute-start | bytes 786440 | tf_op jit(solution)/shard_map/ppermute | solution.py:886
  414.1 20.5 %all-to-all-start.2 = ((bf16[4,4,80,512]{3,2,1,0:T(8,128)(2,1)}), bf16[4,4,80,512]{3,2,1,0:T(8,128)(2,1)S(1)}, u32[]{:S(2)}, u32[]{:S(2)}) async-start(bf16[4,4,80,512]{3,2,1,0:T(8,128)(2,1)} %shard_map.234), calls=%async_computation.2 | async-start | bytes 2621440 | tf_op jit(solution)/shard_map/all_to_all | solution.py:941
  417.6 52.2 %all-gather.12.cloned.1.call-start = ((), (), s32[]{:S(2)}) async-start(), calls=%async_computation.9 | async-start | bytes 1769472 | tf_op jit(solution)/shard_map/all_gather | solution.py:1084
  (108 other events, 845.6 us)
Sparse Core Ops, SparseCore 0:
  43.8 46.3 all-gather.7
  91.8 44.6 all-gather.9
  327.9 44.5 reduce-scatter.2
  374.7 43.1 reduce-scatter.4
  438.7 31.0 all-gather.11

commit v3 on v2

--- a/solution.py
+++ b/solution.py
@@ -121,13 +121,13 @@
     return [sds(shape, BF), sds(shape, BF)]
 
 
-WINDOW = 3 << 20
+WINDOW = 12 << 20
 
 
 class Stage:
-    def __init__(self, ins, outs, split_in, split_out, hold_in, hold_out, sem_in, sem_out, order):
+    def __init__(self, ins, outs, split_in, split_out, hold_in, hold_out, sem_in, sem_out, order, axes):
         self.ins, self.outs = hold_in, hold_out
-        self.split_in, self.split_out = split_in, split_out
+        self.split_in, self.split_out, self.axes = split_in, split_out, axes
         self.out_hbm, self.out_sem, self.sent = outs, sem_out, []
         self.got, self.begun, self.copies, self.bytes = set(), 0, {}, {}
         order = order or [(i, r) for i, parts in enumerate(split_in) for r in range(parts)]
@@ -138,9 +138,9 @@
         self.order = order
         self.ahead(0)
 
-    def rows(self, ref, parts, r):
-        size = ref.shape[0] // parts
-        return pl.ds(r * size, size)
+    def rows(self, ref, parts, r, axis=0):
+        size = ref.shape[axis] // parts
+        return (slice(None),) * axis + (pl.ds(r * size, size),)
 
     def ahead(self, least):
         while self.begun < len(self.order):
@@ -163,7 +163,7 @@
     def done(self, i, r=None):
         parts = self.split_out[i]
         for k in range(parts) if r is None else [r]:
-            rows = self.rows(self.outs[i], parts, k)
+            rows = self.rows(self.outs[i], parts, k, self.axes[i])
             sem = self.out_sem.at[sum(self.split_out[:i]) + k]
             copy = pltpu.make_async_copy(self.outs[i].at[rows], self.out_hbm[i].at[rows], sem)
             copy.start()
@@ -175,9 +175,10 @@
             copy.wait()
 
 
-def staged(body, outs, ins, small=(), small_outs=(), scratch=(), flops=0, moved=0, order=None):
+def staged(body, outs, ins, small=(), small_outs=(), scratch=(), flops=0, moved=0, order=None, mib=62):
     arrays, split_in = [x for x, _ in ins], [n for _, n in ins]
-    shapes, split_out = [x for x, _ in outs], [n for _, n in outs]
+    shapes, split_out = [x[0] for x in outs], [x[1] for x in outs]
+    axes = [x[2] if len(x) > 2 else 0 for x in outs]
 
     def kernel(*refs):
         at = 0
@@ -186,7 +187,7 @@
             groups.append(refs[at : at + n])
             at += n
         few, hbm_in, few_out, hbm_out, hold_in, hold_out, own, (sem_in, sem_out) = groups
-        stage = Stage(hbm_in, hbm_out, split_in, split_out, hold_in, hold_out, sem_in, sem_out, order)
+        stage = Stage(hbm_in, hbm_out, split_in, split_out, hold_in, hold_out, sem_in, sem_out, order, axes)
         body(stage, few, few_out, own)
         stage.finish()
 
@@ -200,7 +201,7 @@
         scratch_shapes=[pltpu.VMEM(x.shape, x.dtype) for x in arrays + shapes]
         + list(scratch)
         + [pltpu.SemaphoreType.DMA((sum(split_in),)), pltpu.SemaphoreType.DMA((max(sum(split_out), 1),))],
-        compiler_params=pltpu.CompilerParams(vmem_limit_bytes=62 << 20),
+        compiler_params=pltpu.CompilerParams(vmem_limit_bytes=mib << 20),
         cost_estimate=pl.CostEstimate(flops=flops // COST, bytes_accessed=moved // COST, transcendentals=0),
     )(*small, *arrays)
     return list(got)
@@ -274,18 +275,18 @@
         key = (lax.broadcasted_iota(jnp.int32, (QB, KB), 1) + k0).astype(F32)
         mask = (key >= start) & (key < end)
         mask = jnp.concatenate([mask, mask], axis=0)
-        for pair in range(HEADS // 2):
-            at = pair * 128
-            q = head_halves(qkv_ref[pl.ds(q0, QB), at : at + 128] * BF(HEAD**-0.5))
-            k = qkv_ref[pl.ds(k0, KB), D + at : D + at + 128]
-            v = qkv_ref[pl.ds(k0, KB), 2 * D + at : 2 * D + at + 128]
-            scores = jnp.where(mask, mm_t(q, k), BLOCKED)
-            raised = jnp.exp(scores - jnp.max(scores, axis=1, keepdims=True))
-            probs = (raised * (1.0 / jnp.sum(raised, axis=1, keepdims=True))).astype(BF)
-            ctx_ref[pl.ds(q0, QB), at : at + 128] = merge_halves(mm(probs, v)).astype(BF)
+        at = [pair * 128 for pair in range(HEADS // 2)]
+        q = [head_halves(qkv_ref[pl.ds(q0, QB), a : a + 128] * BF(HEAD**-0.5)) for a in at]
+        k = [qkv_ref[pl.ds(k0, KB), D + a : D + a + 128] for a in at]
+        v = [qkv_ref[pl.ds(k0, KB), 2 * D + a : 2 * D + a + 128] for a in at]
+        scores = [jnp.where(mask, mm_t(x, y), BLOCKED) for x, y in zip(q, k)]
+        raised = [jnp.exp(x - jnp.max(x, axis=1, keepdims=True)) for x in scores]
+        probs = [(x * (1.0 / jnp.sum(x, axis=1, keepdims=True))).astype(BF) for x in raised]
+        ctx = [merge_halves(mm(x, y)).astype(BF) for x, y in zip(probs, v)]
+        ctx_ref[pl.ds(q0, QB), :] = jnp.concatenate(ctx, axis=1)
         return carry
 
-    lax.fori_loop(0, PACK // QB, block, 0)
+    lax.fori_loop(0, PACK // QB, block, 0, unroll=4)
     for r in range(PACK // ROWS):
         rows = slice(r * ROWS, (r + 1) * ROWS)
         h = x_ref[rows, :].astype(F32) + mm(ctx_ref[rows, :], w_ref[:, 3 * D : 4 * D])
@@ -342,29 +343,33 @@
         query = (lax.broadcasted_iota(jnp.int32, (KB, QB), 1) + q0).astype(F32)
         mask = (query >= start) & (query < end)
         mask = jnp.concatenate([mask, mask], axis=1)
-        for pair in range(HEADS // 2):
-            at = pair * 128
-            q = head_halves(qkv_ref[pl.ds(q0, QB), at : at + 128] * BF(HEAD**-0.5))
-            k = qkv_ref[pl.ds(k0, KB), D + at : D + at + 128]
-            v = qkv_ref[pl.ds(k0, KB), 2 * D + at : 2 * D + at + 128]
-            g = head_halves(dctx_ref[pl.ds(q0, QB), at : at + 128])
-            scores = jnp.where(mask, mm_t(k, q), BLOCKED)
-            raised = jnp.exp(scores - jnp.max(scores, axis=0, keepdims=True))
-            probs = raised * (1.0 / jnp.sum(raised, axis=0, keepdims=True))
-            dprobs = mm_t(v, g)
-            delta = jnp.sum(probs * dprobs, axis=0, keepdims=True)
-            dscores = (probs * (dprobs - delta)).astype(BF)
-            acc_ref[pl.ds(k0, KB), at : at + 128] += mm(dscores, q)
-            acc_ref[pl.ds(k0, KB), D + at : D + at + 128] += mm(probs.astype(BF), g)
-            dq = merge_halves(t_mm(dscores, k)) * (HEAD**-0.5)
-            dqkv_ref[pl.ds(q0, QB), at : at + 128] = dq.astype(BF)
+        at = [pair * 128 for pair in range(HEADS // 2)]
+        q = [head_halves(qkv_ref[pl.ds(q0, QB), a : a + 128] * BF(HEAD**-0.5)) for a in at]
+        k = [qkv_ref[pl.ds(k0, KB), D + a : D + a + 128] for a in at]
+        v = [qkv_ref[pl.ds(k0, KB), 2 * D + a : 2 * D + a + 128] for a in at]
+        g = [head_halves(dctx_ref[pl.ds(q0, QB), a : a + 128]) for a in at]
+        scores = [jnp.where(mask, mm_t(x, y), BLOCKED) for x, y in zip(k, q)]
+        dprobs = [mm_t(x, y) for x, y in zip(v, g)]
+        raised = [jnp.exp(x - jnp.max(x, axis=0, keepdims=True)) for x in scores]
+        probs = [x * (1.0 / jnp.sum(x, axis=0, keepdims=True)) for x in raised]
+        delta = [jnp.sum(x * y, axis=0, keepdims=True) for x, y in zip(probs, dprobs)]
+        dscores = [(x * (y - z)).astype(BF) for x, y, z in zip(probs, dprobs, delta)]
+        dq = [(merge_halves(t_mm(x, y)) * (HEAD**-0.5)).astype(BF) for x, y in zip(dscores, k)]
+        dk = [mm(x, y) for x, y in zip(dscores, q)]
+        dv = [mm(x.astype(BF), y) for x, y in zip(probs, g)]
+        dqkv_ref[pl.ds(q0, QB), 0:D] = jnp.concatenate(dq, axis=1)
+        acc_ref[pl.ds(k0, KB), :] += jnp.concatenate(dk + dv, axis=1)
         return carry
 
-    lax.fori_loop(0, PACK // QB, block, 0)
+    lax.fori_loop(0, PACK // QB, block, 0, unroll=2)
     dqkv_ref[:, D:] = acc_ref[...].astype(BF)
 
 
-def attention_weight_back(split, pos_ref, a_ref, ctx_ref, dx_ref, dqkv_ref, grads, scr_ref):
+def wire_outs(split, blocks):
+    return [(x, blocks, 2) for x in wire_shapes(split, blocks)]
+
+
+def attention_weight_back(io, split, pos_ref, a_ref, ctx_ref, dx_ref, dqkv_ref, grads, scr_ref):
     rows = piece_rows(split)
     for c in range(4):
         cols = slice(c * D, (c + 1) * D)
@@ -375,6 +380,8 @@
         if wired(split):
             scr_ref[...] = grad
             send_rows(split, pos_ref, scr_ref, grads[0], grads[1], c * rows, rows)
+            io.done(1, c)
+            io.done(2, c)
         else:
             grads[0][:, cols] = grad
 
@@ -388,20 +395,20 @@
     combine_grads(io, tok_ref, h_ref, cot_ref, blocks, np_ref, dx_ref, few_out[1], [1, 2] + list(range(8, 8 + len(blocks))))
     attention_core_back(io, dx_ref, None, w_ref, 3, tok_ref, qkv_ref, [4], dctx_ref, dqkv_ref, acc_ref)
     io.need(5, 6, 7)
-    attention_weight_back(split, pos_ref, a_ref, ctx_ref, dx_ref, dqkv_ref, io.outs[1:], scr_ref)
-    for n in range(1, len(io.outs)):
-        io.done(n)
+    attention_weight_back(io, split, pos_ref, a_ref, ctx_ref, dx_ref, dqkv_ref, io.outs[1:], scr_ref)
+    if not wired(split):
+        io.done(1)
     norm_back_rows(norm_at, dx_ref, x_ref, dqkv_ref, np_ref, w_ref, io.outs[0], few_out[0], io)
 
 
 def first_backward(pos, blocks, h, cotangent, hidden, saved, params, tok, weights, norm_at, split):
     a, qkv, ctx = saved
-    grads = wire_shapes(split, 4) if wired(split) else [sds((D, 4 * D), BF)]
+    grads = wire_outs(split, 4) if wired(split) else [(sds((D, 4 * D), BF), 1)]
     ins = [(x, 1) for x in (tok, h, cotangent, weights, qkv, a, ctx, hidden)] + [(x, 2) for x in blocks]
     order = [(0, 0)] + [(8 + n, n % 2) for n in range(len(blocks))] + [(n, 0) for n in range(1, 8)]
     norm, norm_moe, out, *grads = staged(
         functools.partial(first_back_kernel, split, norm_at),
-        [(sds((PACK, D), F32), 4)] + [(x, 1) for x in grads], ins, [pos, params], [sds((2, D), F32)] * 2,
+        [(sds((PACK, D), F32), 4)] + grads, ins, [pos, params], [sds((2, D), F32)] * 2,
         [pltpu.VMEM((PACK, D), F32), pltpu.VMEM((PACK, D), BF), pltpu.VMEM((PACK, 3 * D), BF),
          pltpu.VMEM((PACK, 2 * D), F32), pltpu.VMEM((D, D), BF)],
         flops=16_000_000_000, moved=20 << 20, order=order,
@@ -416,7 +423,7 @@
     dctx_ref, dqkv_ref, acc_ref, scr_ref, row_ref = own
     attention_core_back(io, dx_ref, 0, w_ref, 1, tok_ref, qkv_ref, [2, 3], dctx_ref, dqkv_ref, acc_ref)
     io.need(4, 5, 6)
-    attention_weight_back(split, pos_ref, a_ref, ctx_ref, dx_ref, dqkv_ref, grads, scr_ref)
+    attention_weight_back(io, split, pos_ref, a_ref, ctx_ref, dx_ref, dqkv_ref, grads, scr_ref)
     norm_back_rows(norm_at, dx_ref, x_ref, dqkv_ref, np_ref, w_ref, io.outs[0], gn_ref, io)
     if wired(split):
         dp, ex = split
@@ -434,16 +441,19 @@
                     [row_ref[pl.ds(at, 1), :], table, jnp.zeros((1, WIRE - wide - 128), F32)], axis=1
                 )
                 grads[j % 2][j // 2, k, 4 * rows : 4 * rows + 16, :] = jnp.where(first, row, 0.0).astype(BF)
-    for n in range(1, len(io.outs)):
-        io.done(n)
+    if wired(split):
+        io.done(1, 4)
+        io.done(2, 4)
+    else:
+        io.done(1)
 
 
 def last_backward(pos, dx, hidden, saved, params, tok, weights, norm_at, split, more):
     a, qkv, ctx = saved
-    grads = wire_shapes(split, 5) if wired(split) else [sds((D, 4 * D), BF)]
+    grads = wire_outs(split, 5) if wired(split) else [(sds((D, 4 * D), BF), 1)]
     norm, out, *grads = staged(
         functools.partial(last_back_kernel, split, norm_at),
-        [(sds((PACK, D), F32), 4)] + [(x, 1) for x in grads],
+        [(sds((PACK, D), F32), 4)] + grads,
         [(dx, 4), (weights, 1), (tok, 1), (qkv, 1), (a, 1), (ctx, 1), (hidden, 1)], [pos, params, *more],
         [sds((2, D), F32)],
         [pltpu.VMEM((PACK, D), BF), pltpu.VMEM((PACK, 3 * D), BF), pltpu.VMEM((PACK, 2 * D), F32),
@@ -481,7 +491,7 @@
     return staged(
         feed_kernel,
         [(sds((PACK, D), F32), 4), (sds((PACK, D), BF), 4), (sds((PACK, FF), BF), 4), (sds((PACK, FF), BF), 4)],
-        [(hidden, 4), (up, 1), (down, 1)], [params], flops=4_300_000_000, moved=17 << 20,
+        [(hidden, 4), (up, 1), (down, 1)], [params], flops=4_300_000_000, moved=17 << 20, mib=36,
         order=[(0, 0), (1, 0), (2, 0), (0, 1), (0, 2), (0, 3)],
     )
 
@@ -504,24 +514,29 @@
         for c in range(FF // D):
             scr_ref[...] = t_mm(n_ref[...], dz_ref[:, c * D : (c + 1) * D]).astype(BF)
             send_rows(split, pos_ref, scr_ref, *grads, c * rows, rows)
+            io.done(1, c)
+            io.done(2, c)
         for c in range(FF // D):
             tall_ref[c * D : (c + 1) * D, :] = t_mm(act_ref[:, c * D : (c + 1) * D], dy_ref[...]).astype(BF)
         send_rows(split, pos_ref, tall_ref, *grads, FF // D * rows, FF // D * rows)
+        for c in range(FF // D):
+            io.done(1, FF // D + c)
+            io.done(2, FF // D + c)
     else:
         grads[0][...] = t_mm(n_ref[...], dz_ref[...]).astype(BF)
         grads[1][...] = t_mm(act_ref[...], dy_ref[...]).astype(BF)
-    io.done(1)
-    io.done(2)
+        io.done(1)
+        io.done(2)
     io.need(5, 6)
     norm_back_rows(2, dx_ref, x_ref, dz_ref, np_ref, up_ref, out_ref, few_out[0], io)
 
 
 def feed_backward(pos, dx, hidden, saved, params, up, down, split):
     n, act, slope = saved
-    grads = wire_shapes(split, 8) if wired(split) else [sds((D, FF), BF), sds((FF, D), BF)]
+    grads = wire_outs(split, 8) if wired(split) else [(sds((D, FF), BF), 1), (sds((FF, D), BF), 1)]
     norm, out, *grads = staged(
         functools.partial(feed_back_kernel, split),
-        [(sds((PACK, D), F32), 4)] + [(x, 1) for x in grads],
+        [(sds((PACK, D), F32), 4)] + grads,
         [(dx, 4), (down, 1), (slope, 4), (n, 1), (act, 1), (up, 1), (hidden, 1)], [pos, params], [sds((2, D), F32)],
         scratch=[pltpu.VMEM((PACK, FF), BF), pltpu.VMEM((PACK, D), BF), pltpu.VMEM((D, D), BF), pltpu.VMEM((FF, D), BF)],
         order=[(0, 0), (1, 0), (2, 0)] + [(i, r) for r in range(1, 4) for i in (0, 2)] + [(n, 0) for n in range(3, 7)],
@@ -663,7 +678,7 @@
     size = slot.shape[0] // experts
     return staged(
         gather_kernel, [(sds((2 * size, D), BF), 2)] * (experts // 2), [(source, 1), (slot, experts)],
-        flops=2 * slot.shape[0] * PACK * D, moved=6 << 20,
+        flops=2 * slot.shape[0] * PACK * D, moved=6 << 20, mib=24,
     )
 
 
@@ -696,7 +711,7 @@
     return staged(
         functools.partial(gather_near_kernel, at),
         [(sds((count * size, D), BF), count), (sds((count * size, 8), F32), count)], [(x, 1) for x in sources], [pairs],
-        flops=2 * count * size * PACK * D, moved=4 << 20,
+        flops=2 * count * size * PACK * D, moved=4 << 20, mib=20,
     )
 
 
@@ -985,11 +1000,11 @@
         feed = send_even(tie(feed, *zero[1:]), n_ex)
         groups = [(0, 2), (2, 6), (6, 8)]
 
-        def gather_group(lo, hi):
+        def gather_group(lo, hi, pairs):
             sources = sum([[cots[j], flip(cots[j], 1, n_ex)] for j in range(lo // 2, hi // 2)], [])
             return gather_near(pairs, sources, cap_slots, lo)
 
-        near = [gather_group(*group) for group in groups[:2]]
+        near = [gather_group(*group, pairs) for group in groups[:2]]
         attn_zero, params = call(
             functools.partial(assemble_norm_kernel, split), [sds((D, 4 * D), BF), sds((8, D), F32)], pos, *zero,
             scratch=[pltpu.VMEM((D, 128), F32)], pos=True, flops=1_000_000, moved=4 << 20, mib=24,
@@ -1026,19 +1041,20 @@
     up_expert = lax.all_gather(expert_up[0], "dp", axis=0, tiled=True)
     down_expert = lax.all_gather(expert_down[0], "dp", axis=0, tiled=True)
     h3, *saved_one, c = attention_forward(h2, params, tok, attn_one, 4, True)
+    sent = gather_rows(slot, c, experts)
+    sums, held, table = [], (), 0.0
     if wire:
-        c = tie(c, cots[-1])
-    sent = gather_rows(slot, c, experts)
-    if wire:
-        near.append(gather_group(*groups[2]))
-    sums, held, table = [], (), 0.0
+        sent = [tie(pair, cots[-1]) for pair in sent]
     bufs = {j: exchange(sent[j // 2], j) for j in range(0, groups[-1][0], 2)}
-    for n, ((lo, hi), (dout, slot_near)) in enumerate(zip(groups, near)):
+    for n, (lo, hi) in enumerate(groups):
+        if wire and n == 1:
+            near.append(gather_group(*groups[2], tie(pairs, sums[0])))
+        dout, slot_near = near[n]
         if n == 1:
             for j in range(groups[-1][0], n_ex, 2):
                 bufs[j] = exchange(tie(sent[j // 2], *[bufs[i] for i in range(lo, hi, 2)], *sums[:1]), j)
         for j in range(lo, hi, 2):
-            bufs[j + 1] = flip(tie(bufs[j], *sums[-1:]), 1, n_ex)
+            bufs[j + 1] = flip(tie(bufs[j], *sums[-1:], *near[-1]), 1, n_ex)
         back, part, held = expert_rows(
             pos, [bufs[j] for j in range(lo, hi)], dout, slot_near, up_expert, down_expert, slots, lo, held
         )
@@ -1046,11 +1062,8 @@
         table = table + part
     out, *held = held
     back = [exchange(pair, 2 * j) for j, pair in enumerate(sums)]
-    early_back = len(back) - (groups[-1][1] - groups[-1][0]) // 2
-    far = [flip(tie(pair, sums[-1]), 1, n_ex) for pair in back[:early_back]]
-    held = [tie(one, *far) for one in held]
     gup_expert, gdown_expert = expert_grads(*held)
-    far += [flip(tie(pair, gup_expert), 1, n_ex) for pair in back[early_back:]]
+    far = [flip(tie(pair, gup_expert), 1, n_ex) for pair in back]
     dbuf_home = sum([list(both) for both in zip(back, far)], [])
     out_home = swap(tie(out, *back, gup_expert).reshape(experts, cap_slots, D), EXPERT).reshape(-1, D)
     gn_one, gn_moe, dx, g_one = first_backward(
@@ -1059,13 +1072,13 @@
     expert_up_sum = lax.psum_scatter(tie(gup_expert, gn_moe), "dp", scatter_dimension=0, tiled=True).astype(F32)
     expert_down_sum = lax.psum_scatter(tie(gdown_expert, gn_moe), "dp", scatter_dimension=0, tiled=True).astype(F32)
     if wire:
-        got_one = flip(g_one[1], 1, n_ex)
+        got_one = add_core(pos, g_one[0], flip(g_one[1], 1, n_ex), True)
+        dx = tie(dx, got_one[0])
+        got_one = send_near(got_one, n_ex)
     gn_feed, dx, g_feed = feed_backward(pos, dx, h1, saved_feed, params, up, down, split)
     if wire:
-        got_one = add_core(pos, g_one[0], tie(got_one, gn_feed), True)
-        got_feed = flip(tie(g_feed[1], out_home), 1, n_ex)
-        sum_feed = add_core(pos, g_feed[0], tie(got_feed, *got_one))
-        got_one = send_near(got_one, n_ex)
+        got_feed = flip(tie(g_feed[1], out_home, *got_one[1:]), 1, n_ex)
+        sum_feed = add_core(pos, g_feed[0], got_feed)
         dx = tie(dx, sum_feed)
         got_feed = swap(sum_feed, "xy")
     gn_zero, grad_in, g_zero = last_backward(
@@ -1073,7 +1086,7 @@
     )
     if wire:
         early = add_near(pos, tie(got_feed, gn_zero), got_one)
-        got_zero = flip(tie(g_zero[1], early[0]), 1, n_ex)
+        got_zero = tie(flip(g_zero[1], 1, n_ex), early[0])
         early = send_turn(early, n_dp)
         sum_zero = add_core(pos, g_zero[0], got_zero)
         h3 = tie(h3, sum_zero)
@@ -1082,8 +1095,8 @@
     if wire:
         sum_zero = tie(sum_zero, hidden_out)
         early = lax.all_gather(add_turn([tie(one, sum_zero) for one in early]), EXPERT, axis=0)
-        sum_zero = add_near(pos, tie(sum_zero, hidden_out, expert_up_sum, expert_down_sum))
-        sum_zero = add_turn(send_turn(sum_zero, n_dp))
+        sum_zero = send_turn(add_near(pos, tie(sum_zero, hidden_out)), n_dp)
+        sum_zero = add_turn([tie(part, expert_up_sum, expert_down_sum) for part in sum_zero])
         last = lax.all_gather(sum_zero, EXPERT, axis=0)
         rows = D // n_dp
         grad_qkv, grad_attn, grad_up, grad_down, gn, sums = call(

time: 494 us -> 450 us (0.911)
  Pallas kernels: 262 us -> 236 us
  waiting for transfers between devices: 61.3 us -> 52.2 us
  local copies, waits for them, and re-layouts: 54.8 us -> 48.7 us
    pallas_call x12, Pallas kernels: 133 us -> 116 us  [staged(): pl.pallas_call(kernel, out_shape=list(small_outs) + shapes, in_specs=spac...]
    ppermute x51, waiting for transfers between devices: 42.6 us -> 27.2 us  [flip(): return lax.ppermute(rows, EXPERT, [(i, i ^ j) for i in range(ex)])]
    pallas_call x15, Pallas kernels: 129 us -> 120 us  [call(): pl.pallas_call(kernel, out_shape=out_shape, compiler_params=pltpu.Compile...]
    unnamed x161 -> x165, local copies, waits for them, and re-layouts: 44.2 us -> 36.6 us
  transfers between devices with their start and end apart: 68 -> 68, of which waited for: 30 -> 27; matrix products, arithmetic and copies ran while one was open for 3% -> 4% of each run, Pallas kernels for 54% -> 53%
where the time goes in v3:
time: 450 us; the launch traced here: 443 us
  Pallas kernels  236 us (52%)
  starting transfers between devices  70 us (16%)
  waiting for transfers between devices  52.2 us (12%)
  local copies, waits for them, and re-layouts  48.7 us (11%)
  between operations  15.2 us (3%)
  blocking collectives  12.2 us (3%)
  other arithmetic  8.9 us (2%)
    pallas_call x15, Pallas kernels, call(): pl.pallas_call(kernel, out_shape=out_shape, compiler_params=pltpu.Compile...  120 us
    pallas_call x12, Pallas kernels, staged(): pl.pallas_call(kernel, out_shape=list(small_outs) + shapes, in_specs=spac...  116 us
    ppermute x51, starting transfers between devices, flip(): return lax.ppermute(rows, EXPERT, [(i, i ^ j) for i in range(ex)])  38.2 us
    unnamed x165, local copies, waits for them, and re-layouts  36.6 us
    ppermute x51, waiting for transfers between devices, flip(): return lax.ppermute(rows, EXPERT, [(i, i ^ j) for i in range(ex)])  27.2 us
    ppermute x9, waiting for transfers between devices, turn(): return lax.ppermute(rows, 'dp', [(i, (i + k) % dp) for i in range(dp)])  20 us
    ppermute x9, starting transfers between devices, turn(): return lax.ppermute(rows, 'dp', [(i, (i + k) % dp) for i in range(dp)])  18.2 us
    all_to_all x3, starting transfers between devices, swap(): return lax.all_to_all(parts, axis, split_axis=0, concat_axis=0, tiled=True)  13 us
  transfers between devices with their start and end apart: 68, of which 27 were waited for; matrix products, arithmetic and copies ran while one was open for 4% of the time, Pallas kernels for 53%

profile of v3, /device:TPU:0, one launch (start us, length us, event | category | flops | bytes accessed | tf_op | source)
XLA Modules:
  0.0 443.3 jit_solution(16502922880667220795)
XLA Ops:
  15.4 5.0 %collective-permute-start.2 = (bf16[272,512]{1,0:T(8,128)(2,1)S(1)}, bf16[272,512]{1,0:T(8,128)(2,1)S(1)}, u32[]{:S(2)}, u32[]{:S(2)}) collective-permute-start(bf16[272,512]{1,0:T(8,128)(2,1)S(1)} %get-tuple-element.320), channel_id=1, source_target_pairs={{0,24},{8,0},{16,8},{24,16},{1,25},{9,1},{17,9},{25,17},{2,26},{10... | collective-permute-start | bytes 835592 | tf_op jit(solution)/shard_map/ppermute | solution.py:905
  31.2 13.0 %collective-permute-done.1 = bf16[272,512]{1,0:T(8,128)(2,1)S(1)} collective-permute-done((bf16[272,512]{1,0:T(8,128)(2,1)S(1)}, bf16[272,512]{1,0:T(8,128)(2,1)S(1)}, u32[]{:S(2)}, u32[]{:S(2)}) %collective-permute-start.1) | collective-permute-done | bytes 278560 | tf_op jit(solution)/shard_map/ppermute | solution.py:905
  56.3 7.3 %collective-permute-done.7 = f32[32,128]{1,0:T(8,128)S(1)} collective-permute-done((f32[32,128]{1,0:T(8,128)S(1)}, f32[32,128]{1,0:T(8,128)S(1)}, u32[]{:S(2)}, u32[]{:S(2)}) %collective-permute-start.7) | collective-permute-done | bytes 16416 | tf_op jit(solution)/shard_map/ppermute | solution.py:901
  81.9 6.8 %shard_map.216 = (bf16[2048,512]{1,0:T(8,128)(2,1)S(1)}, f32[2048,8]{1,0:T(8,128)S(1)}) custom-call(f32[64,128]{1,0:T(8,128)S(1)} %pad_maximum_fusion.3.refs_0_, bf16[1024,512]{1,0:T(8,128)(2,1)} %collective-permute-done.3.refs_1_, bf16[1024,512]{1,0:T(8,128)(2,1)} %collective-permute-done.16.refs_2_, bf16[1024,512]{1,0:T(8,128)(2,1)} %collective-permute-done.4.refs_3_, ...), custom_call_target="tpu_custom_call" | custom-call | flops 536870912 | bytes 1048576 | tf_op jit(solution)/shard_map/pallas_call | solution.py:195
  91.0 7.6 %shard_map.217 = (f32[1024,512]{1,0:T(8,128)S(1)}, bf16[1024,512]{1,0:T(8,128)(2,1)S(1)}, bf16[1024,1536]{1,0:T(8,128)(2,1)S(1)}, bf16[1024,512]{1,0:T(8,128)(2,1)S(1)}) custom-call(bf16[1024,512]{1,0:T(8,128)(2,1)S(1)} %copy-done.39, f32[8,512]{1,0:T(8,128)S(1)} %get-tuple-element.151.np_ref.refs_0_.refs_1_, ...), custom_call_target="tpu_custom_call" | custom-call | flops 1500000000 | bytes 3145728 | tf_op jit(solution)/shard_map/pallas_call | solution.py:79
  108.3 10.7 %shard_map.219 = (f32[1024,512]{1,0:T(8,128)S(1)}, bf16[1024,512]{1,0:T(8,128)(2,1)S(1)}, bf16[1024,2048]{1,0:T(8,128)(2,1)S(1)}, bf16[1024,2048]{1,0:T(8,128)(2,1)S(1)}) custom-call(f32[8,512]{1,0:T(8,128)S(1)} %get-tuple-element.151.np_ref.refs_0_.refs_1_, f32[1024,512]{1,0:T(8,128)S(1)} %get-tuple-element.158.refs_1_.refs_8_, ...), custom_call_target="tpu_custom_call" | custom-call | flops 1075000064 | bytes 4456448 | tf_op jit(solution)/shard_map/pallas_call | solution.py:195
  124.0 3.0 collective-permute-start.32
  130.3 7.7 %shard_map.221 = (f32[1024,512]{1,0:T(8,128)S(1)}, bf16[1024,512]{1,0:T(8,128)(2,1)S(1)}, bf16[1024,1536]{1,0:T(8,128)(2,1)S(1)}, bf16[1024,512]{1,0:T(8,128)(2,1)S(1)}, bf16[1024,512]{1,0:T(8,128)(2,1)S(1)}) custom-call(f32[1024,512]{1,0:T(8,128)S(1)} %get-tuple-element.166.x_ref.refs_9_, f32[8,512]{1,0:T(8,128)S(1)} %get-tuple-element.151.np_ref.refs_0_.refs_1_, ...), custom_call_target="tpu_custom_call" | custom-call | flops 1500000000 | bytes 3145728 | tf_op jit(solution)/shard_map/pallas_call | solution.py:79
  141.4 7.3 %shard_map.222 = (bf16[1024,512]{1,0:T(8,128)(2,1)S(1)}, bf16[1024,512]{1,0:T(8,128)(2,1)}, bf16[1024,512]{1,0:T(8,128)(2,1)}, bf16[1024,512]{1,0:T(8,128)(2,1)}) custom-call(bf16[1024,512]{1,0:T(8,128)(2,1)S(1)} %get-tuple-element.172.refs_0_, f32[4096,8]{1,0:T(8,128)S(1)} %copy-done.12), custom_call_target="tpu_custom_call" | custom-call | flops 1073741824 | bytes 1572864 | tf_op jit(solution)/shard_map/pallas_call | solution.py:195
  153.4 16.7 %shard_map.223 = (bf16[1024,512]{1,0:T(8,128)(2,1)}, f32[8,128]{1,0:T(8,128)}, bf16[4096,512]{1,0:T(8,128)(2,1)}, bf16[4096,2048]{1,0:T(8,128)(2,1)}, bf16[4096,...) custom-call(s32[2]{0:T(128)} %copy-done.36, bf16[1024,512]{1,0:T(8,128)(2,1)} %copy-done.41, ...), custom_call_target="tpu_custom_call" | custom-call | flops 2147483648 | bytes 3407872 | tf_op jit(solution)/shard_map/pallas_call | solution.py:79
  170.1 3.4 shard_map.224
  180.3 29.3 %shard_map.225 = (bf16[1024,512]{1,0:T(8,128)(2,1)}, bf16[1024,512]{1,0:T(8,128)(2,1)}, f32[8,128]{1,0:T(8,128)}, bf16[4096,512]{1,0:T(8,128)(2,1)}, bf16[4096,2...) custom-call(s32[2]{0:T(128)} %copy-done.36, ...), custom_call_target="tpu_custom_call", output_to_operand_aliasing={{3}: (9, {}), {4}: (10, {}), {5}: (11, {}), {6}: (12, {}), ... | custom-call | flops 4294967296 | bytes 6815744 | tf_op jit(solution)/shard_map/pallas_call | solution.py:79
  213.6 17.0 %shard_map.226 = (bf16[1024,512]{1,0:T(8,128)(2,1)}, f32[8,128]{1,0:T(8,128)}, bf16[4096,512]{1,0:T(8,128)(2,1)}, bf16[4096,2048]{1,0:T(8,128)(2,1)}, bf16[4096,...) custom-call(s32[2]{0:T(128)} %copy-done.36, ...), custom_call_target="tpu_custom_call", output_to_operand_aliasing={{2}: (7, {}), {3}: (8, {}), {4}: (9, {}), {5}: (10, {}), {6... | custom-call | flops 2147483648 | bytes 3407872 | tf_op jit(solution)/shard_map/pallas_call | solution.py:79
  232.9 25.2 %shard_map.227 = (bf16[512,2048]{1,0:T(8,128)(2,1)}, bf16[2048,512]{1,0:T(8,128)(2,1)}) custom-call(bf16[4096,2048]{1,0:T(8,128)(2,1)} %get-tuple-element.207.act_ref, bf16[4096,2048]{1,0:T(8,128)(2,1)} %get-tuple-element.208.du_ref, bf16[4096,512]{1,0:T(8,128)(2,1)} %get-tuple-element.209.buf_ref, bf16[4096,512]{1,0:T(8,128)(2,1)} %get-tuple-element.210.dout_ref), custom_call_target="tpu_custom_call" | custom-call | flops 4294967296 | bytes 11534336 | tf_op jit(solution)/shard_map/pallas_call | solution.py:79
  259.2 4.6 %all-to-all-start = ((bf16[8,512,512]{2,1,0:T(8,128)(2,1)}), bf16[8,512,512]{2,1,0:T(8,128)(2,1)}, u32[]{:S(2)}, u32[]{:S(2)}) async-start(bf16[8,512,512]{2,1,0:T(8,128)(2,1)} %bitcast.93), calls=%async_computation | async-start | bytes 8388608 | tf_op jit(solution)/shard_map/all_to_all | solution.py:956
  265.6 27.6 %shard_map.228 = (f32[2,512]{1,0:T(2,128)}, f32[2,512]{1,0:T(2,128)}, f32[1024,512]{1,0:T(8,128)}, bf16[4,4,64,512]{3,2,1,0:T(8,128)(2,1)}, bf16[4,4,64,512]{3,2,1,0:T(8,128)(2,1)}) custom-call(s32[2]{0:T(128)} %copy-done.36, f32[8,512]{1,0:T(8,128)} %copy-done.35, f32[1024,8]{1,0:T(8,128)} %copy-done.14, f32[1024,512]{1,0:T(8,128)} %copy-done.5, ...), custom_call_target="tpu_custom_call" | custom-call | flops 4000000000 | bytes 5242880 | tf_op jit(solution)/shard_map/pallas_call | solution.py:195
  298.1 3.3 shard_map.229
  305.0 15.3 %shard_map.230 = (f32[2,512]{1,0:T(2,128)}, f32[1024,512]{1,0:T(8,128)}, bf16[4,4,128,512]{3,2,1,0:T(8,128)(2,1)}, bf16[4,4,128,512]{3,2,1,0:T(8,128)(2,1)}) custom-call(s32[2]{0:T(128)} %copy-done.36, f32[8,512]{1,0:T(8,128)} %copy-done.35, f32[1024,512]{1,0:T(8,128)} %get-tuple-element.225.refs_2_, bf16[2048,512]{1,0:T(8,128)(2,1)} %copy-done.4, ...), custom_call_target="tpu_custom_call" | custom-call | flops 2150000128 | bytes 6291456 | tf_op jit(solution)/shard_map/pallas_call | solution.py:195
  320.4 3.7 collective-permute-done.51.refs_4_
  324.8 3.8 collective-permute-done.52.refs_2_
  328.6 4.4 shard_map.231
  333.0 4.9 %all-to-all-start.1 = ((bf16[4,4,128,512]{3,2,1,0:T(8,128)(2,1)}), bf16[4,4,128,512]{3,2,1,0:T(8,128)(2,1)}, u32[]{:S(2)}, u32[]{:S(2)}) async-start(bf16[4,4,128,512]{3,2,1,0:T(8,128)(2,1)} %shard_map.231), calls=%async_computation.1 | async-start | bytes 4194304 | tf_op jit(solution)/shard_map/all_to_all | solution.py:956
  337.9 21.2 %shard_map.232 = (f32[2,512]{1,0:T(2,128)}, f32[1024,512]{1,0:T(8,128)}, bf16[4,4,80,512]{3,2,1,0:T(8,128)(2,1)}, bf16[4,4,80,512]{3,2,1,0:T(8,128)(2,1)}) custom-call(s32[2]{0:T(128)} %copy-done.36, f32[8,512]{1,0:T(8,128)} %copy-done.35, f32[2,512]{1,0:T(2,128)} %get-tuple-element.229.refs_2_, f32[2,512]{1,0:T(2,128)} %get-tuple-element.230.refs_3_, ...), custom_call_target="tpu_custom_call" | custom-call | flops 3500000000 | bytes 4194304 | tf_op jit(solution)/shard_map/pallas_call | solution.py:195
  359.3 4.1 all-to-all-done.1.refs_0_
  363.4 3.0 shard_map.233
  367.5 3.6 shard_map.234
  371.1 3.6 all-to-all-start.2
  377.7 3.0 collective-permute-start.59
  380.7 9.9 %shard_map.235 = bf16[1024,512]{1,0:T(8,128)(2,1)} custom-call(s32[2]{0:T(128)} %copy-done.36, f32[1024,8]{1,0:T(8,128)} %copy-done.14, f32[4096,8]{1,0:T(8,128)} %copy-done.11, bf16[4096,512]{1,0:T(8,128)(2,1)} %bitcast.29.refs_3_, f32[1024,512]{1,0:T(8,128)} %copy-done.5), custom_call_target="tpu_custom_call" | custom-call | flops 1073741824 | bytes 3670016 | tf_op jit(solution)/shard_map/pallas_call | solution.py:195
  390.9 3.7 collective-permute-done.58.refs_2_
  402.2 3.8 collective-permute-start.54
  416.5 12.2 %all-gather.2 = bf16[640,512]{1,0:T(8,128)(2,1)S(1)} all-gather(bf16[80,512]{1,0:T(8,128)(2,1)} %shard_map.237), channel_id=4, replica_groups=mesh['dp'=4,'xy'=4,'core'=2] {'xy','core'}, dimensions={0}, use_global_device_ids=true | all-gather | bytes 737280 | tf_op jit(solution)/shard_map/all_gather | solution.py:1100
  (380 shorter events, 132.4 us)
Async XLA Ops:
  7.2 146.0 %all-gather.8.cloned.1.call-start = ((), (), s32[]{:S(2)}) async-start(), calls=%async_computation.7 | async-start | bytes 2621440 | tf_op jit(solution)/shard_map/all_gather | solution.py:1041
  20.5 23.7 %collective-permute-start.1 = (bf16[272,512]{1,0:T(8,128)(2,1)S(1)}, bf16[272,512]{1,0:T(8,128)(2,1)S(1)}, u32[]{:S(2)}, u32[]{:S(2)}) collective-permute-start(bf16[272,512]{1,0:T(8,128)(2,1)S(1)} %get-tuple-element.320), channel_id=1, source_target_pairs={{0,16},{8,24},{16,0},{24,8},{1,17},{9,25},{17,1},{25,9},{2,18},{10... | collective-permute-start | bytes 835592 | tf_op jit(solution)/shard_map/ppermute | solution.py:905
  20.5 23.7 %collective-permute-start = (bf16[272,512]{1,0:T(8,128)(2,1)S(1)}, bf16[272,512]{1,0:T(8,128)(2,1)S(1)}, u32[]{:S(2)}, u32[]{:S(2)}) collective-permute-start(bf16[272,512]{1,0:T(8,128)(2,1)S(1)} %get-tuple-element.320), channel_id=1, source_target_pairs={{0,8},{8,16},{16,24},{24,0},{1,9},{9,17},{17,25},{25,1},{2,10},{10... | collective-permute-start | bytes 835592 | tf_op jit(solution)/shard_map/ppermute | solution.py:905
  21.5 25.9 %collective-permute-start.3 = (bf16[1024,512]{1,0:T(8,128)(2,1)}, bf16[1024,512]{1,0:T(8,128)(2,1)}, u32[]{:S(2)}, u32[]{:S(2)}) collective-permute-start(bf16[1024,512]{1,0:T(8,128)(2,1)} %refs_4_.1), channel_id=1, source_target_pairs={{0,2},{1,3},{2,0},{3,1},{4,6},{5,7},{6,4},{7,5},{8,10},{9,11},{10,... | collective-permute-start | bytes 3145736 | tf_op jit(solution)/shard_map/ppermute | solution.py:901
  23.0 24.4 %collective-permute-start.4 = (bf16[1024,512]{1,0:T(8,128)(2,1)}, bf16[1024,512]{1,0:T(8,128)(2,1)}, u32[]{:S(2)}, u32[]{:S(2)}) collective-permute-start(bf16[1024,512]{1,0:T(8,128)(2,1)} %refs_4_.1), channel_id=1, source_target_pairs={{0,4},{1,5},{2,6},{3,7},{4,0},{5,1},{6,2},{7,3},{8,12},{9,13},{10,... | collective-permute-start | bytes 3145736 | tf_op jit(solution)/shard_map/ppermute | solution.py:901
  31.1 44.8 %collective-permute-start.15 = (bf16[1024,512]{1,0:T(8,128)(2,1)S(1)}, bf16[1024,512]{1,0:T(8,128)(2,1)}, u32[]{:S(2)}, u32[]{:S(2)}) collective-permute-start(bf16[1024,512]{1,0:T(8,128)(2,1)S(1)} %copy-done.9), channel_id=1, source_target_pairs={{0,1},{1,0},{2,3},{3,2},{4,5},{5,4},{6,7},{7,6},{8,9},{9,8},{10,11... | collective-permute-start | bytes 3145736 | tf_op jit(solution)/shard_map/ppermute | solution.py:901
  44.2 109.0 %all-gather.10.cloned.1.call-start = ((), (), s32[]{:S(2)}) async-start(), calls=%async_computation.8 | async-start | bytes 2621440 | tf_op jit(solution)/shard_map/all_gather | solution.py:1042
  63.7 18.2 %collective-permute-start.16 = (bf16[1024,512]{1,0:T(8,128)(2,1)}, bf16[1024,512]{1,0:T(8,128)(2,1)}, u32[]{:S(2)}, u32[]{:S(2)}) collective-permute-start(bf16[1024,512]{1,0:T(8,128)(2,1)} %collective-permute-done.3.refs_1_), channel_id=1, source_target_pairs={{0,1},{1,0},{2,3},{3,2},{4,5},{5,4},{6,7},{7,6},{8,9},{9,8},{10,11... | collective-permute-start | bytes 3145736 | tf_op jit(solution)/shard_map/ppermute | solution.py:901
  64.2 17.7 %collective-permute-start.17 = (bf16[1024,512]{1,0:T(8,128)(2,1)}, bf16[1024,512]{1,0:T(8,128)(2,1)}, u32[]{:S(2)}, u32[]{:S(2)}) collective-permute-start(bf16[1024,512]{1,0:T(8,128)(2,1)} %collective-permute-done.4.refs_3_), channel_id=1, source_target_pairs={{0,1},{1,0},{2,3},{3,2},{4,5},{5,4},{6,7},{7,6},{8,9},{9,8},{10,11... | collective-permute-start | bytes 3145736 | tf_op jit(solution)/shard_map/ppermute | solution.py:901
  72.0 28.3 %collective-permute-start.19 = (bf16[4,128,512]{2,1,0:T(8,128)(2,1)S(1)}, bf16[4,128,512]{2,1,0:T(8,128)(2,1)S(1)}, u32[]{:S(2)}, u32[]{:S(2)}) collective-permute-start(bf16[4,128,512]{2,1,0:T(8,128)(2,1)S(1)} %pad_maximum_fusion.refs_1_), channel_id=1, source_target_pairs={{0,2},{1,3},{2,0},{3,1},{4,6},{5,7},{6,4},{7,5},{8,10},{9,11},{10,... | collective-permute-start | bytes 1572872 | tf_op jit(solution)/shard_map/ppermute | solution.py:901
  74.4 26.4 %collective-permute-start.21 = (bf16[4,128,512]{2,1,0:T(8,128)(2,1)S(1)}, bf16[4,128,512]{2,1,0:T(8,128)(2,1)}, u32[]{:S(2)}, u32[]{:S(2)}) collective-permute-start(bf16[4,128,512]{2,1,0:T(8,128)(2,1)S(1)} %pad_maximum_fusion.refs_1_), channel_id=1, source_target_pairs={{0,4},{1,5},{2,6},{3,7},{4,0},{5,1},{6,2},{7,3},{8,12},{9,13},{10,... | collective-permute-start | bytes 1572872 | tf_op jit(solution)/shard_map/ppermute | solution.py:901
  75.9 25.0 %collective-permute-start.23 = (bf16[4,128,512]{2,1,0:T(8,128)(2,1)S(1)}, bf16[4,128,512]{2,1,0:T(8,128)(2,1)}, u32[]{:S(2)}, u32[]{:S(2)}) collective-permute-start(bf16[4,128,512]{2,1,0:T(8,128)(2,1)S(1)} %pad_maximum_fusion.refs_1_), channel_id=1, source_target_pairs={{0,6},{1,7},{2,4},{3,5},{4,2},{5,3},{6,0},{7,1},{8,14},{9,15},{10,... | collective-permute-start | bytes 1572872 | tf_op jit(solution)/shard_map/ppermute | solution.py:901
  103.1 20.8 %collective-permute-start.26 = (bf16[4,64,512]{2,1,0:T(8,128)(2,1)S(1)}, bf16[4,64,512]{2,1,0:T(8,128)(2,1)S(1)}, u32[]{:S(2)}, u32[]{:S(2)}) collective-permute-start(bf16[4,64,512]{2,1,0:T(8,128)(2,1)S(1)} %pad_maximum_fusion.2.refs_1_), channel_id=1, source_target_pairs={{0,2},{1,3},{2,0},{3,1},{4,6},{5,7},{6,4},{7,5},{8,10},{9,11},{10,... | collective-permute-start | bytes 786440 | tf_op jit(solution)/shard_map/ppermute | solution.py:901
  105.1 18.8 %collective-permute-start.28 = (bf16[4,64,512]{2,1,0:T(8,128)(2,1)S(1)}, bf16[4,64,512]{2,1,0:T(8,128)(2,1)S(1)}, u32[]{:S(2)}, u32[]{:S(2)}) collective-permute-start(bf16[4,64,512]{2,1,0:T(8,128)(2,1)S(1)} %pad_maximum_fusion.2.refs_1_), channel_id=1, source_target_pairs={{0,4},{1,5},{2,6},{3,7},{4,0},{5,1},{6,2},{7,3},{8,12},{9,13},{10,... | collective-permute-start | bytes 786440 | tf_op jit(solution)/shard_map/ppermute | solution.py:901
  124.0 25.9 %collective-permute-start.32 = (bf16[1024,512]{1,0:T(8,128)(2,1)S(1)}, bf16[1024,512]{1,0:T(8,128)(2,1)}, u32[]{:S(2)}, u32[]{:S(2)}) collective-permute-start(bf16[1024,512]{1,0:T(8,128)(2,1)S(1)} %copy-done.9), channel_id=1, source_target_pairs={{0,6},{1,7},{2,4},{3,5},{4,2},{5,3},{6,0},{7,1},{8,14},{9,15},{10,... | collective-permute-start | bytes 3145736 | tf_op jit(solution)/shard_map/ppermute | solution.py:901
  149.8 20.3 %collective-permute-start.37 = (bf16[1024,512]{1,0:T(8,128)(2,1)}, bf16[1024,512]{1,0:T(8,128)(2,1)S(1)}, u32[]{:S(2)}, u32[]{:S(2)}) collective-permute-start(bf16[1024,512]{1,0:T(8,128)(2,1)} %collective-permute-done.32.refs_1_), channel_id=1, source_target_pairs={{0,1},{1,0},{2,3},{3,2},{4,5},{5,4},{6,7},{7,6},{8,9},{9,8},{10,11... | collective-permute-start | bytes 3145736 | tf_op jit(solution)/shard_map/ppermute | solution.py:901
  150.3 25.4 %collective-permute-start.33 = (bf16[1024,512]{1,0:T(8,128)(2,1)}, bf16[1024,512]{1,0:T(8,128)(2,1)}, u32[]{:S(2)}, u32[]{:S(2)}) collective-permute-start(bf16[1024,512]{1,0:T(8,128)(2,1)} %get-tuple-element.177), channel_id=1, source_target_pairs={{0,2},{1,3},{2,0},{3,1},{4,6},{5,7},{6,4},{7,5},{8,10},{9,11},{10,... | collective-permute-start | bytes 3145736 | tf_op jit(solution)/shard_map/ppermute | solution.py:901
  151.7 25.2 %collective-permute-start.34 = (bf16[1024,512]{1,0:T(8,128)(2,1)}, bf16[1024,512]{1,0:T(8,128)(2,1)}, u32[]{:S(2)}, u32[]{:S(2)}) collective-permute-start(bf16[1024,512]{1,0:T(8,128)(2,1)} %get-tuple-element.179), channel_id=1, source_target_pairs={{0,4},{1,5},{2,6},{3,7},{4,0},{5,1},{6,2},{7,3},{8,12},{9,13},{10,... | collective-permute-start | bytes 3145736 | tf_op jit(solution)/shard_map/ppermute | solution.py:901
  176.9 32.7 %collective-permute-start.36 = (bf16[1024,512]{1,0:T(8,128)(2,1)}, bf16[1024,512]{1,0:T(8,128)(2,1)}, u32[]{:S(2)}, u32[]{:S(2)}) collective-permute-start(bf16[1024,512]{1,0:T(8,128)(2,1)} %get-tuple-element.186), channel_id=1, source_target_pairs={{0,6},{1,7},{2,4},{3,5},{4,2},{5,3},{6,0},{7,1},{8,14},{9,15},{10,... | collective-permute-start | bytes 3145736 | tf_op jit(solution)/shard_map/ppermute | solution.py:901
  209.8 48.8 %collective-permute-start.42 = (bf16[1024,512]{1,0:T(8,128)(2,1)}, bf16[1024,512]{1,0:T(8,128)(2,1)}, u32[]{:S(2)}, u32[]{:S(2)}) collective-permute-start(bf16[1024,512]{1,0:T(8,128)(2,1)} %get-tuple-element.197), channel_id=1, source_target_pairs={{0,4},{1,5},{2,6},{3,7},{4,0},{5,1},{6,2},{7,3},{8,12},{9,13},{10,... | collective-permute-start | bytes 3145736 | tf_op jit(solution)/shard_map/ppermute | solution.py:901
  211.2 47.0 %collective-permute-start.41 = (bf16[1024,512]{1,0:T(8,128)(2,1)}, bf16[1024,512]{1,0:T(8,128)(2,1)}, u32[]{:S(2)}, u32[]{:S(2)}) collective-permute-start(bf16[1024,512]{1,0:T(8,128)(2,1)} %get-tuple-element.205), channel_id=1, source_target_pairs={{0,2},{1,3},{2,0},{3,1},{4,6},{5,7},{6,4},{7,5},{8,10},{9,11},{10,... | collective-permute-start | bytes 3145736 | tf_op jit(solution)/shard_map/ppermute | solution.py:901
  230.7 28.5 %collective-permute-start.43 = (bf16[1024,512]{1,0:T(8,128)(2,1)}, bf16[1024,512]{1,0:T(8,128)(2,1)}, u32[]{:S(2)}, u32[]{:S(2)}) collective-permute-start(bf16[1024,512]{1,0:T(8,128)(2,1)} %get-tuple-element.206), channel_id=1, source_target_pairs={{0,6},{1,7},{2,4},{3,5},{4,2},{5,3},{6,0},{7,1},{8,14},{9,15},{10,... | collective-permute-start | bytes 3145736 | tf_op jit(solution)/shard_map/ppermute | solution.py:901
  259.2 64.9 %all-to-all-start = ((bf16[8,512,512]{2,1,0:T(8,128)(2,1)}), bf16[8,512,512]{2,1,0:T(8,128)(2,1)}, u32[]{:S(2)}, u32[]{:S(2)}) async-start(bf16[8,512,512]{2,1,0:T(8,128)(2,1)} %bitcast.93), calls=%async_computation | async-start | bytes 8388608 | tf_op jit(solution)/shard_map/all_to_all | solution.py:956
  263.8 134.2 %reduce-scatter.3.cloned.1.call-start = ((), (), s32[]{:S(2)}) async-start(), calls=%async_computation.5 | async-start | bytes 2621440 | tf_op jit(solution)/shard_map/reduce_scatter | solution.py:1072
  293.2 115.2 %reduce-scatter.5.cloned.1.call-start = ((), (), s32[]{:S(2)}) async-start(), calls=%async_computation.6 | async-start | bytes 2621440 | tf_op jit(solution)/shard_map/reduce_scatter | solution.py:1073
  301.4 18.9 %collective-permute-start.49 = (bf16[4,64,512]{2,1,0:T(8,128)(2,1)}, bf16[4,64,512]{2,1,0:T(8,128)(2,1)S(1)}, u32[]{:S(2)}, u32[]{:S(2)}) collective-permute-start(bf16[4,64,512]{2,1,0:T(8,128)(2,1)} %get-tuple-element.238), channel_id=1, source_target_pairs={{0,2},{1,3},{2,0},{3,1},{4,6},{5,7},{6,4},{7,5},{8,10},{9,11},{10,... | collective-permute-start | bytes 786440 | tf_op jit(solution)/shard_map/ppermute | solution.py:901
  302.6 17.8 %collective-permute-start.50 = (bf16[4,64,512]{2,1,0:T(8,128)(2,1)}, bf16[4,64,512]{2,1,0:T(8,128)(2,1)S(1)}, u32[]{:S(2)}, u32[]{:S(2)}) collective-permute-start(bf16[4,64,512]{2,1,0:T(8,128)(2,1)} %get-tuple-element.239), channel_id=1, source_target_pairs={{0,4},{1,5},{2,6},{3,7},{4,0},{5,1},{6,2},{7,3},{8,12},{9,13},{10,... | collective-permute-start | bytes 786440 | tf_op jit(solution)/shard_map/ppermute | solution.py:901
  304.1 20.0 %collective-permute-start.51 = (bf16[4,64,512]{2,1,0:T(8,128)(2,1)}, bf16[4,64,512]{2,1,0:T(8,128)(2,1)S(1)}, u32[]{:S(2)}, u32[]{:S(2)}) collective-permute-start(bf16[4,64,512]{2,1,0:T(8,128)(2,1)} %get-tuple-element.240), channel_id=1, source_target_pairs={{0,6},{1,7},{2,4},{3,5},{4,2},{5,3},{6,0},{7,1},{8,14},{9,15},{10,... | collective-permute-start | bytes 786440 | tf_op jit(solution)/shard_map/ppermute | solution.py:901
  333.0 30.4 %all-to-all-start.1 = ((bf16[4,4,128,512]{3,2,1,0:T(8,128)(2,1)}), bf16[4,4,128,512]{3,2,1,0:T(8,128)(2,1)}, u32[]{:S(2)}, u32[]{:S(2)}) async-start(bf16[4,4,128,512]{3,2,1,0:T(8,128)(2,1)} %shard_map.231), calls=%async_computation.1 | async-start | bytes 4194304 | tf_op jit(solution)/shard_map/all_to_all | solution.py:956
  371.1 19.7 %all-to-all-start.2 = ((bf16[4,4,80,512]{3,2,1,0:T(8,128)(2,1)}), bf16[4,4,80,512]{3,2,1,0:T(8,128)(2,1)S(1)}, u32[]{:S(2)}, u32[]{:S(2)}) async-start(bf16[4,4,80,512]{3,2,1,0:T(8,128)(2,1)} %shard_map.234), calls=%async_computation.2 | async-start | bytes 2621440 | tf_op jit(solution)/shard_map/all_to_all | solution.py:956
  374.7 54.4 %all-gather.12.cloned.1.call-start = ((), (), s32[]{:S(2)}) async-start(), calls=%async_computation.9 | async-start | bytes 1769472 | tf_op jit(solution)/shard_map/all_gather | solution.py:1097
  375.7 18.9 %collective-permute-start.58 = (bf16[192,512]{1,0:T(8,128)(2,1)}, bf16[192,512]{1,0:T(8,128)(2,1)S(1)}, u32[]{:S(2)}, u32[]{:S(2)}) collective-permute-start(bf16[192,512]{1,0:T(8,128)(2,1)} %get-tuple-element.268), channel_id=1, source_target_pairs={{0,16},{8,24},{16,0},{24,8},{1,17},{9,25},{17,1},{25,9},{2,18},{10... | collective-permute-start | bytes 589832 | tf_op jit(solution)/shard_map/ppermute | solution.py:905
  (110 other events, 843.9 us)
Sparse Core Ops, SparseCore 0:
  44.3 46.3 all-gather.7
  92.3 44.6 all-gather.9
  293.4 44.0 reduce-scatter.2
  339.7 45.5 reduce-scatter.4
  398.1 30.9 all-gather.11

commit v4 on v3

--- a/solution.py
+++ b/solution.py
@@ -24,7 +24,7 @@
 GELU_A = 0.044715
 
 
-COST = 4
+COST = 2
 
 
 def mm(left, right):
@@ -257,7 +257,8 @@
 
 def attention_kernel(norm_at, last, x_ref, np_ref, tok_ref, w_ref, *refs):
     if last:
-        h_ref, a_ref, qkv_ref, ctx_ref, c_ref = refs
+        slot_ref, h_ref, a_ref, qkv_ref, ctx_ref = refs[:5]
+        pair_refs, c_ref = refs[5:-1], refs[-1]
     else:
         h_ref, a_ref, qkv_ref, ctx_ref = refs
     gain, shift = np_ref[norm_at : norm_at + 1, :], np_ref[norm_at + 1 : norm_at + 2, :]
@@ -294,15 +295,24 @@
         if last:
             unit, _ = unit_rows(h)
             c_ref[rows, :] = (unit * np_ref[6:7, :] + np_ref[7:8, :]).astype(BF)
-
-
-def attention_forward(hidden, params, tok, weights, norm_at, last):
+    if last:
+        size = pair_refs[0].shape[0] // 2
+        tokens = lax.broadcasted_iota(jnp.int32, (size, PACK), 1).astype(F32)
+        for n in range(2 * len(pair_refs)):
+            hot = jnp.where(slot_ref[n * size : (n + 1) * size, 0:1] == tokens, 1.0, 0.0).astype(BF)
+            pair_refs[n // 2][n % 2 * size : (n % 2 + 1) * size, :] = mm(hot, c_ref[...]).astype(BF)
+
+
+def attention_forward(hidden, params, tok, weights, norm_at, slot=None, experts=0):
+    last = slot is not None
     outs = [sds((PACK, D), F32), sds((PACK, D), BF), sds((PACK, 3 * D), BF), sds((PACK, D), BF)]
+    more, scratch = (), ()
     if last:
-        outs.append(sds((PACK, D), BF))
+        outs += [sds((2 * slot.shape[0] // experts, D), BF)] * (experts // 2)
+        more, scratch = (slot,), [pltpu.VMEM((PACK, D), BF)]
     return call(
         functools.partial(attention_kernel, norm_at, last),
-        outs, hidden, params, tok, weights,
+        outs, hidden, params, tok, weights, *more, scratch=scratch,
         flops=6_000_000_000, moved=12 << 20, mib=40,
     )
 
@@ -645,8 +655,8 @@
 
     def put(n, start, piece):
         for c in range(3):
-            qkv_ref[n, pl.ds(start, rows), c * D : (c + 1) * D] = piece[c * rows : (c + 1) * rows]
-        attn_ref[n, pl.ds(start, rows), :] = piece[3 * rows : 4 * rows]
+            qkv_ref[pl.ds(start, rows), n, c * D : (c + 1) * D] = piece[c * rows : (c + 1) * rows]
+        attn_ref[pl.ds(start, rows), n, :] = piece[3 * rows : 4 * rows]
 
     for j in range(ex):
         start, high = j * rows, j * 4 * rows
@@ -659,27 +669,6 @@
         put(0, j * rows, piece)
         gn_ref[j : j + 1, :] = piece[4 * rows : 4 * rows + 1, 0 : D // dp]
         table_ref[j : j + 1, :] = piece[4 * rows : 4 * rows + 1, D // dp : D // dp + 128]
-
-
-def gather_kernel(io, few, few_out, own):
-    src_ref, slot_ref = io.ins
-    pairs = len(io.outs)
-    size = io.outs[0].shape[0] // 2
-    tokens = lax.broadcasted_iota(jnp.int32, (size, PACK), 1).astype(F32)
-    io.need(0)
-    for n in range(2 * pairs):
-        io.need((1, n))
-        hot = jnp.where(slot_ref[n * size : (n + 1) * size, 0:1] == tokens, 1.0, 0.0).astype(BF)
-        io.outs[n // 2][n % 2 * size : (n % 2 + 1) * size, :] = mm(hot, src_ref[...]).astype(BF)
-        io.done(n // 2, n % 2)
-
-
-def gather_rows(slot, source, experts):
-    size = slot.shape[0] // experts
-    return staged(
-        gather_kernel, [(sds((2 * size, D), BF), 2)] * (experts // 2), [(source, 1), (slot, experts)],
-        flops=2 * slot.shape[0] * PACK * D, moved=6 << 20, mib=24,
-    )
 
 
 def gather_near_kernel(at, io, few, few_out, own):
@@ -996,8 +985,8 @@
         while j < n_ex:
             pairs = jnp.concatenate([pairs, flip(pairs, j, n_ex)])
             j *= 2
+        feed = send_even(tie(feed, *zero[1:]), n_ex)
         zero = send_core([tie(part, tok, pairs) for part in zero], n_ex)
-        feed = send_even(tie(feed, *zero[1:]), n_ex)
         groups = [(0, 2), (2, 6), (6, 8)]
 
         def gather_group(lo, hi, pairs):
@@ -1010,7 +999,7 @@
             scratch=[pltpu.VMEM((D, 128), F32)], pos=True, flops=1_000_000, moved=4 << 20, mib=24,
         )
         fwd = tie(hidden_in, *sum(near, []))
-        h1, *saved_zero = attention_forward(fwd, params, tok, attn_zero, 0, False)
+        h1, *saved_zero = attention_forward(fwd, params, tok, attn_zero, 0)
         one = send_even(tie(one, h1, *feed[1:]), n_ex)
         feed = send_core([tie(part, h1) for part in feed], n_ex)
         up, down = assemble(split, pos, feed, True)
@@ -1028,7 +1017,7 @@
         attn_zero = gather_all(jnp.concatenate([w_qkv[:, 0], w_attn[:, 0]], axis=1))
         up, down = gather_all(w_up), gather_all(w_down)
         attn_one = gather_all(jnp.concatenate([w_qkv[:, 1], w_attn[:, 1]], axis=1))
-        h1, *saved_zero = attention_forward(hidden_in, params, tok, attn_zero, 0, False)
+        h1, *saved_zero = attention_forward(hidden_in, params, tok, attn_zero, 0)
         h2, *saved_feed = feed_forward(h1, params, up, down)
         pairs = pair
         j = 1
@@ -1040,8 +1029,8 @@
         near = [gather_near(pairs, cots[lo:hi], cap_slots, lo) for lo, hi in groups]
     up_expert = lax.all_gather(expert_up[0], "dp", axis=0, tiled=True)
     down_expert = lax.all_gather(expert_down[0], "dp", axis=0, tiled=True)
-    h3, *saved_one, c = attention_forward(h2, params, tok, attn_one, 4, True)
-    sent = gather_rows(slot, c, experts)
+    h3, *saved_one = attention_forward(h2, params, tok, attn_one, 4, slot, experts)
+    saved_one, sent = saved_one[:3], saved_one[3:]
     sums, held, table = [], (), 0.0
     if wire:
         sent = [tie(pair, cots[-1]) for pair in sent]
@@ -1069,8 +1058,8 @@
     gn_one, gn_moe, dx, g_one = first_backward(
         pos, dbuf_home, h3, cotangent, h2, saved_one, params, tok, attn_one, 4, split
     )
-    expert_up_sum = lax.psum_scatter(tie(gup_expert, gn_moe), "dp", scatter_dimension=0, tiled=True).astype(F32)
-    expert_down_sum = lax.psum_scatter(tie(gdown_expert, gn_moe), "dp", scatter_dimension=0, tiled=True).astype(F32)
+    expert_up_sum = lax.psum_scatter(tie(gup_expert, gn_moe), "dp", scatter_dimension=0, tiled=True)
+    expert_down_sum = lax.psum_scatter(tie(gdown_expert, gn_moe), "dp", scatter_dimension=0, tiled=True)
     if wire:
         got_one = add_core(pos, g_one[0], flip(g_one[1], 1, n_ex), True)
         dx = tie(dx, got_one[0])
@@ -1085,28 +1074,29 @@
         pos, dx, hidden_in, saved_zero, params, tok, attn_zero, 0, split, (gn_feed, gn_one, gn_moe, table)
     )
     if wire:
-        early = add_near(pos, tie(got_feed, gn_zero), got_one)
-        got_zero = tie(flip(g_zero[1], 1, n_ex), early[0])
-        early = send_turn(early, n_dp)
-        sum_zero = add_core(pos, g_zero[0], got_zero)
+        sum_zero = add_core(pos, g_zero[0], flip(g_zero[1], 1, n_ex))
+        early = add_near(pos, tie(got_feed, sum_zero), got_one)
         h3 = tie(h3, sum_zero)
         sum_zero = swap(sum_zero, "xy")
+        early = send_turn(early, n_dp)
     hidden_out = combine_out(pos, tok, slot, out_home, h3, experts)
     if wire:
-        sum_zero = tie(sum_zero, hidden_out)
-        early = lax.all_gather(add_turn([tie(one, sum_zero) for one in early]), EXPERT, axis=0)
-        sum_zero = send_turn(add_near(pos, tie(sum_zero, hidden_out)), n_dp)
+        sum_zero = add_near(pos, tie(sum_zero, hidden_out))
+        early = lax.all_gather(add_turn([tie(one, sum_zero[0]) for one in early]), EXPERT, axis=0)
+        expert_up_sum, expert_down_sum = tie(expert_up_sum, sum_zero[0]), tie(expert_down_sum, sum_zero[0])
+        expert_up_sum, expert_down_sum = expert_up_sum.astype(F32), expert_down_sum.astype(F32)
+        sum_zero = send_turn(sum_zero, n_dp)
         sum_zero = add_turn([tie(part, expert_up_sum, expert_down_sum) for part in sum_zero])
         last = lax.all_gather(sum_zero, EXPERT, axis=0)
         rows = D // n_dp
         grad_qkv, grad_attn, grad_up, grad_down, gn, sums = call(
             functools.partial(spread_kernel, split),
-            [sds((2, rows, 3 * D), F32), sds((2, rows, D), F32), sds((rows, FF), F32), sds((FF // n_dp, D), F32),
+            [sds((rows, 2, 3 * D), F32), sds((rows, 2, D), F32), sds((rows, FF), F32), sds((FF // n_dp, D), F32),
              sds((8, rows), F32), sds((experts, 128), F32)],
             pos, last, early,
             pos=True, flops=1_000_000, moved=7 << 20, mib=32,
         )
-        grad_qkv, grad_attn, gn = grad_qkv.transpose(1, 0, 2), grad_attn.transpose(1, 0, 2), gn.T
+        gn = gn.T
     else:
         small = jnp.concatenate([gn_zero, gn_feed, gn_one, gn_moe], axis=0)
         table = lax.dynamic_update_slice_in_dim(jnp.zeros((experts, 128), F32), table[:1], me, 0)
@@ -1132,7 +1122,7 @@
     grad_logits = jnp.where(hot[:, 0], lean[:, None], 0.0) - jnp.where(hot[:, 1], lean[:, None], 0.0)
     return (
         hidden_out, grad_in, grad_logits, gn, grad_qkv, grad_attn, grad_up, grad_down,
-        expert_up_sum[None], expert_down_sum[None],
+        expert_up_sum.astype(F32)[None], expert_down_sum.astype(F32)[None],
     )
 
 

time: 450 us -> 443 us (0.984)
  local copies, waits for them, and re-layouts: 48.7 us -> 43.4 us
    pallas_call x15, Pallas kernels: 120 us -> 128 us  [call(): pl.pallas_call(kernel, out_shape=out_shape, compiler_params=pltpu.Compile...]
    pallas_call x12 -> x11, Pallas kernels: 116 us -> 109 us  [staged(): pl.pallas_call(kernel, out_shape=list(small_outs) + shapes, in_specs=spac...]
    unnamed x165 -> x135, local copies, waits for them, and re-layouts: 36.6 us -> 30.6 us
    ppermute x51, waiting for transfers between devices: 27.2 us -> 32.4 us  [flip(): return lax.ppermute(rows, EXPERT, [(i, i ^ j) for i in range(ex)])]
  transfers between devices with their start and end apart: 68 -> 68, of which waited for: 27 -> 23; matrix products, arithmetic and copies ran while one was open for 4% -> 4% of each run, Pallas kernels for 53% -> 54%
where the time goes in v4:
time: 443 us; the launch traced here: 436 us
  Pallas kernels  237 us (53%)
  starting transfers between devices  66.7 us (15%)
  waiting for transfers between devices  53.4 us (12%)
  local copies, waits for them, and re-layouts  43.4 us (10%)
  between operations  15.1 us (3%)
  blocking collectives  11.8 us (3%)
  other arithmetic  8.89 us (2%)
    pallas_call x15, Pallas kernels, call(): pl.pallas_call(kernel, out_shape=out_shape, compiler_params=pltpu.Compile...  128 us
    pallas_call x11, Pallas kernels, staged(): pl.pallas_call(kernel, out_shape=list(small_outs) + shapes, in_specs=spac...  109 us
    ppermute x51, starting transfers between devices, flip(): return lax.ppermute(rows, EXPERT, [(i, i ^ j) for i in range(ex)])  34.1 us
    ppermute x51, waiting for transfers between devices, flip(): return lax.ppermute(rows, EXPERT, [(i, i ^ j) for i in range(ex)])  32.4 us
    unnamed x135, local copies, waits for them, and re-layouts  30.6 us
    ppermute x9, starting transfers between devices, turn(): return lax.ppermute(rows, 'dp', [(i, (i + k) % dp) for i in range(dp)])  18.4 us
    ppermute x9, waiting for transfers between devices, turn(): return lax.ppermute(rows, 'dp', [(i, (i + k) % dp) for i in range(dp)])  17.8 us
    all_to_all x3, starting transfers between devices, swap(): return lax.all_to_all(parts, axis, split_axis=0, concat_axis=0, tiled=True)  13.6 us
  transfers between devices with their start and end apart: 68, of which 23 were waited for; matrix products, arithmetic and copies ran while one was open for 4% of the time, Pallas kernels for 54%

profile of v4, /device:TPU:0, one launch (start us, length us, event | category | flops | bytes accessed | tf_op | source)
XLA Modules:
  0.0 436.2 jit_solution(15410056651081629070)
XLA Ops:
  15.5 5.0 %collective-permute-start.2 = (bf16[272,512]{1,0:T(8,128)(2,1)S(1)}, bf16[272,512]{1,0:T(8,128)(2,1)S(1)}, u32[]{:S(2)}, u32[]{:S(2)}) collective-permute-start(bf16[272,512]{1,0:T(8,128)(2,1)S(1)} %get-tuple-element.280), channel_id=1, source_target_pairs={{0,24},{8,0},{16,8},{24,16},{1,25},{9,1},{17,9},{25,17},{2,26},{10... | collective-permute-start | bytes 835592 | tf_op jit(solution)/shard_map/ppermute | solution.py:894
  29.0 15.3 %collective-permute-done.1 = bf16[272,512]{1,0:T(8,128)(2,1)S(1)} collective-permute-done((bf16[272,512]{1,0:T(8,128)(2,1)S(1)}, bf16[272,512]{1,0:T(8,128)(2,1)S(1)}, u32[]{:S(2)}, u32[]{:S(2)}) %collective-permute-start.1) | collective-permute-done | bytes 278560 | tf_op jit(solution)/shard_map/ppermute | solution.py:894
  57.2 2.7 collective-permute-done.7
  64.9 4.4 %collective-permute-done.13.refs_7_ = bf16[4,80,512]{2,1,0:T(8,128)(2,1)S(1)} collective-permute-done((bf16[4,80,512]{2,1,0:T(8,128)(2,1)S(1)}, bf16[4,80,512]{2,1,0:T(8,128)(2,1)S(1)}, u32[]{:S(2)}, u32[]{:S(2)}) %collective-permute-start.13) | collective-permute-done | bytes 327712 | tf_op jit(solution)/shard_map/ppermute | solution.py:890
  76.2 3.1 shard_map.215
  81.1 6.8 %shard_map.216 = (bf16[2048,512]{1,0:T(8,128)(2,1)S(1)}, f32[2048,8]{1,0:T(8,128)S(1)}) custom-call(f32[64,128]{1,0:T(8,128)S(1)} %pad_maximum_fusion.3.refs_0_, bf16[1024,512]{1,0:T(8,128)(2,1)} %collective-permute-done.3.refs_1_, bf16[1024,512]{1,0:T(8,128)(2,1)S(1)} %collective-permute-done.16.refs_2_, bf16[1024,512]{1,0:T(8,128)(2,1)} %collective-permute-done.4.refs_3_, ...), custom_call_target="tpu_custom_call" | custom-call | flops 1073741824 | bytes 2097152 | tf_op jit(solution)/shard_map/pallas_call | solution.py:195
  90.2 7.4 %shard_map.217 = (f32[1024,512]{1,0:T(8,128)S(1)}, bf16[1024,512]{1,0:T(8,128)(2,1)S(1)}, bf16[1024,1536]{1,0:T(8,128)(2,1)S(1)}, bf16[1024,512]{1,0:T(8,128)(2,1)S(1)}) custom-call(bf16[1024,512]{1,0:T(8,128)(2,1)S(1)} %copy-done.22, f32[8,512]{1,0:T(8,128)S(1)} %get-tuple-element.151.np_ref.refs_0_.refs_1_, ...), custom_call_target="tpu_custom_call" | custom-call | flops 3000000000 | bytes 6291456 | tf_op jit(solution)/shard_map/pallas_call | solution.py:79
  106.5 10.7 %shard_map.219 = (f32[1024,512]{1,0:T(8,128)S(1)}, bf16[1024,512]{1,0:T(8,128)(2,1)S(1)}, bf16[1024,2048]{1,0:T(8,128)(2,1)S(1)}, bf16[1024,2048]{1,0:T(8,128)(2,1)S(1)}) custom-call(f32[8,512]{1,0:T(8,128)S(1)} %get-tuple-element.151.np_ref.refs_0_.refs_1_, f32[1024,512]{1,0:T(8,128)S(1)} %get-tuple-element.158.refs_1_.refs_8_, ...), custom_call_target="tpu_custom_call" | custom-call | flops 2150000128 | bytes 8912896 | tf_op jit(solution)/shard_map/pallas_call | solution.py:195
  126.2 15.5 %shard_map.221 = (f32[1024,512]{1,0:T(8,128)S(1)}, bf16[1024,512]{1,0:T(8,128)(2,1)S(1)}, bf16[1024,1536]{1,0:T(8,128)(2,1)}, bf16[1024,512]{1,0:T(8,128)(2,1)S(...) custom-call(f32[1024,512]{1,0:T(8,128)S(1)} %get-tuple-element.166.x, ...), custom_call_target="tpu_custom_call" | custom-call | flops 3000000000 | bytes 6291456 | tf_op jit(solution)/shard_map/pallas_call | solution.py:79
  150.2 16.5 %shard_map.222 = (bf16[1024,512]{1,0:T(8,128)(2,1)}, f32[8,128]{1,0:T(8,128)}, bf16[4096,512]{1,0:T(8,128)(2,1)}, bf16[4096,2048]{1,0:T(8,128)(2,1)}, bf16[4096,...) custom-call(s32[2]{0:T(128)} %copy-done.18, bf16[1024,512]{1,0:T(8,128)(2,1)} %copy-done.24, ...), custom_call_target="tpu_custom_call" | custom-call | flops 4294967296 | bytes 6815744 | tf_op jit(solution)/shard_map/pallas_call | solution.py:79
  166.7 3.4 shard_map.223
  177.7 29.0 %shard_map.224 = (bf16[1024,512]{1,0:T(8,128)(2,1)}, bf16[1024,512]{1,0:T(8,128)(2,1)}, f32[8,128]{1,0:T(8,128)}, bf16[4096,512]{1,0:T(8,128)(2,1)}, bf16[4096,2...) custom-call(s32[2]{0:T(128)} %copy-done.18, ...), custom_call_target="tpu_custom_call", output_to_operand_aliasing={{3}: (9, {}), {4}: (10, {}), {5}: (11, {}), {6}: (12, {}), ... | custom-call | flops 8589934592 | bytes 13631488 | tf_op jit(solution)/shard_map/pallas_call | solution.py:79
  210.7 17.0 %shard_map.225 = (bf16[1024,512]{1,0:T(8,128)(2,1)}, f32[8,128]{1,0:T(8,128)}, bf16[4096,512]{1,0:T(8,128)(2,1)}, bf16[4096,2048]{1,0:T(8,128)(2,1)}, bf16[4096,...) custom-call(s32[2]{0:T(128)} %copy-done.18, ...), custom_call_target="tpu_custom_call", output_to_operand_aliasing={{2}: (7, {}), {3}: (8, {}), {4}: (9, {}), {5}: (10, {}), {6... | custom-call | flops 4294967296 | bytes 6815744 | tf_op jit(solution)/shard_map/pallas_call | solution.py:79
  228.5 25.3 %shard_map.226 = (bf16[512,2048]{1,0:T(8,128)(2,1)}, bf16[2048,512]{1,0:T(8,128)(2,1)}) custom-call(bf16[4096,2048]{1,0:T(8,128)(2,1)} %get-tuple-element.206.act_ref, bf16[4096,2048]{1,0:T(8,128)(2,1)} %get-tuple-element.207.du_ref, bf16[4096,512]{1,0:T(8,128)(2,1)} %get-tuple-element.208.buf_ref, bf16[4096,512]{1,0:T(8,128)(2,1)} %get-tuple-element.209.dout_ref), custom_call_target="tpu_custom_call" | custom-call | flops 8589934592 | bytes 23068672 | tf_op jit(solution)/shard_map/pallas_call | solution.py:79
  256.4 4.6 %all-to-all-start = ((bf16[8,512,512]{2,1,0:T(8,128)(2,1)}), bf16[8,512,512]{2,1,0:T(8,128)(2,1)}, u32[]{:S(2)}, u32[]{:S(2)}) async-start(bf16[8,512,512]{2,1,0:T(8,128)(2,1)} %bitcast.89), calls=%async_computation | async-start | bytes 8388608 | tf_op jit(solution)/shard_map/all_to_all | solution.py:945
  262.2 27.6 %shard_map.227 = (f32[2,512]{1,0:T(2,128)}, f32[2,512]{1,0:T(2,128)}, f32[1024,512]{1,0:T(8,128)}, bf16[4,4,64,512]{3,2,1,0:T(8,128)(2,1)}, bf16[4,4,64,512]{3,2,1,0:T(8,128)(2,1)}) custom-call(s32[2]{0:T(128)} %copy-done.18, f32[8,512]{1,0:T(8,128)} %copy-done.20, f32[1024,8]{1,0:T(8,128)} %copy-done.17, f32[1024,512]{1,0:T(8,128)} %copy-done.6, ...), custom_call_target="tpu_custom_call" | custom-call | flops 8000000000 | bytes 10485760 | tf_op jit(solution)/shard_map/pallas_call | solution.py:195
  294.7 3.2 shard_map.228
  301.5 15.3 %shard_map.229 = (f32[2,512]{1,0:T(2,128)}, f32[1024,512]{1,0:T(8,128)}, bf16[4,4,128,512]{3,2,1,0:T(8,128)(2,1)}, bf16[4,4,128,512]{3,2,1,0:T(8,128)(2,1)}) custom-call(s32[2]{0:T(128)} %copy-done.18, f32[8,512]{1,0:T(8,128)} %copy-done.20, f32[1024,512]{1,0:T(8,128)} %get-tuple-element.224.refs_2_, bf16[2048,512]{1,0:T(8,128)(2,1)} %copy-done.8, ...), custom_call_target="tpu_custom_call" | custom-call | flops 4300000256 | bytes 12582912 | tf_op jit(solution)/shard_map/pallas_call | solution.py:195
  316.9 4.3 collective-permute-done.51.refs_4_
  321.9 3.8 collective-permute-done.52.refs_2_
  325.7 4.4 %shard_map.230 = bf16[4,4,128,512]{3,2,1,0:T(8,128)(2,1)} custom-call(s32[2]{0:T(128)} %copy-done.18, bf16[4,4,128,512]{3,2,1,0:T(8,128)(2,1)} %get-tuple-element.235.refs_1_, bf16[4,4,128,512]{3,2,1,0:T(8,128)(2,1)} %collective-permute-done.52.refs_2_), custom_call_target="tpu_custom_call" | custom-call | flops 500000 | bytes 3145728 | tf_op jit(solution)/shard_map/pallas_call | solution.py:195
  330.1 4.9 %all-to-all-start.2 = ((bf16[4,4,128,512]{3,2,1,0:T(8,128)(2,1)}), bf16[4,4,128,512]{3,2,1,0:T(8,128)(2,1)}, u32[]{:S(2)}, u32[]{:S(2)}) async-start(bf16[4,4,128,512]{3,2,1,0:T(8,128)(2,1)} %shard_map.230), calls=%async_computation.4 | async-start | bytes 4194304 | tf_op jit(solution)/shard_map/all_to_all | solution.py:945
  335.0 21.2 %shard_map.231 = (f32[2,512]{1,0:T(2,128)}, f32[1024,512]{1,0:T(8,128)}, bf16[4,4,80,512]{3,2,1,0:T(8,128)(2,1)}, bf16[4,4,80,512]{3,2,1,0:T(8,128)(2,1)}) custom-call(s32[2]{0:T(128)} %copy-done.18, f32[8,512]{1,0:T(8,128)} %copy-done.20, f32[2,512]{1,0:T(2,128)} %get-tuple-element.228.refs_2_, f32[2,512]{1,0:T(2,128)} %get-tuple-element.229.refs_3_, ...), custom_call_target="tpu_custom_call" | custom-call | flops 7000000000 | bytes 8388608 | tf_op jit(solution)/shard_map/pallas_call | solution.py:195
  356.4 3.1 collective-permute-done.53.refs_2_
  360.6 3.6 shard_map.232
  364.2 4.2 all-to-all-start.1
  368.4 3.0 shard_map.236
  374.3 3.1 collective-permute-start.59
  377.3 9.9 %shard_map.233 = bf16[1024,512]{1,0:T(8,128)(2,1)} custom-call(s32[2]{0:T(128)} %copy-done.18, f32[1024,8]{1,0:T(8,128)} %copy-done.17, f32[4096,8]{1,0:T(8,128)} %copy-done.4, bf16[4096,512]{1,0:T(8,128)(2,1)} %bitcast.29.refs_3_, f32[1024,512]{1,0:T(8,128)} %copy-done.6), custom_call_target="tpu_custom_call" | custom-call | flops 2147483648 | bytes 7340032 | tf_op jit(solution)/shard_map/pallas_call | solution.py:195
  395.0 4.0 collective-permute-start.54
  409.8 11.8 %all-gather.2 = bf16[640,512]{1,0:T(8,128)(2,1)S(1)} all-gather(bf16[80,512]{1,0:T(8,128)(2,1)} %shard_map.235), channel_id=4, replica_groups=mesh['dp'=4,'xy'=4,'core'=2] {'xy','core'}, dimensions={0}, use_global_device_ids=true | all-gather | bytes 737280 | tf_op jit(solution)/shard_map/all_gather | solution.py:1090
  421.6 3.2 all-gather.12.cloned.1.call-done
  (349 shorter events, 123.9 us)
Async XLA Ops:
  7.2 141.9 %all-gather.8.cloned.1.call-start = ((), (), s32[]{:S(2)}) async-start(), calls=%async_computation.7 | async-start | bytes 2621440 | tf_op jit(solution)/shard_map/all_gather | solution.py:1030
  20.6 23.7 %collective-permute-start.1 = (bf16[272,512]{1,0:T(8,128)(2,1)S(1)}, bf16[272,512]{1,0:T(8,128)(2,1)S(1)}, u32[]{:S(2)}, u32[]{:S(2)}) collective-permute-start(bf16[272,512]{1,0:T(8,128)(2,1)S(1)} %get-tuple-element.280), channel_id=1, source_target_pairs={{0,16},{8,24},{16,0},{24,8},{1,17},{9,25},{17,1},{25,9},{2,18},{10... | collective-permute-start | bytes 835592 | tf_op jit(solution)/shard_map/ppermute | solution.py:894
  20.6 23.7 %collective-permute-start = (bf16[272,512]{1,0:T(8,128)(2,1)S(1)}, bf16[272,512]{1,0:T(8,128)(2,1)S(1)}, u32[]{:S(2)}, u32[]{:S(2)}) collective-permute-start(bf16[272,512]{1,0:T(8,128)(2,1)S(1)} %get-tuple-element.280), channel_id=1, source_target_pairs={{0,8},{8,16},{16,24},{24,0},{1,9},{9,17},{17,25},{25,1},{2,10},{10... | collective-permute-start | bytes 835592 | tf_op jit(solution)/shard_map/ppermute | solution.py:894
  21.6 28.2 %collective-permute-start.3 = (bf16[1024,512]{1,0:T(8,128)(2,1)}, bf16[1024,512]{1,0:T(8,128)(2,1)}, u32[]{:S(2)}, u32[]{:S(2)}) collective-permute-start(bf16[1024,512]{1,0:T(8,128)(2,1)} %refs_4_.1), channel_id=1, source_target_pairs={{0,2},{1,3},{2,0},{3,1},{4,6},{5,7},{6,4},{7,5},{8,10},{9,11},{10,... | collective-permute-start | bytes 3145736 | tf_op jit(solution)/shard_map/ppermute | solution.py:890
  23.1 26.7 %collective-permute-start.4 = (bf16[1024,512]{1,0:T(8,128)(2,1)}, bf16[1024,512]{1,0:T(8,128)(2,1)}, u32[]{:S(2)}, u32[]{:S(2)}) collective-permute-start(bf16[1024,512]{1,0:T(8,128)(2,1)} %refs_4_.1), channel_id=1, source_target_pairs={{0,4},{1,5},{2,6},{3,7},{4,0},{5,1},{6,2},{7,3},{8,12},{9,13},{10,... | collective-permute-start | bytes 3145736 | tf_op jit(solution)/shard_map/ppermute | solution.py:890
  28.9 40.4 %collective-permute-start.15 = (bf16[1024,512]{1,0:T(8,128)(2,1)S(1)}, bf16[1024,512]{1,0:T(8,128)(2,1)S(1)}, u32[]{:S(2)}, u32[]{:S(2)}) collective-permute-start(bf16[1024,512]{1,0:T(8,128)(2,1)S(1)} %copy-done.15), channel_id=1, source_target_pairs={{0,1},{1,0},{2,3},{3,2},{4,5},{5,4},{6,7},{7,6},{8,9},{9,8},{10,11... | collective-permute-start | bytes 3145736 | tf_op jit(solution)/shard_map/ppermute | solution.py:890
  44.3 104.9 %all-gather.10.cloned.1.call-start = ((), (), s32[]{:S(2)}) async-start(), calls=%async_computation.8 | async-start | bytes 2621440 | tf_op jit(solution)/shard_map/all_gather | solution.py:1031
  62.5 18.6 %collective-permute-start.16 = (bf16[1024,512]{1,0:T(8,128)(2,1)}, bf16[1024,512]{1,0:T(8,128)(2,1)S(1)}, u32[]{:S(2)}, u32[]{:S(2)}) collective-permute-start(bf16[1024,512]{1,0:T(8,128)(2,1)} %collective-permute-done.3.refs_1_), channel_id=1, source_target_pairs={{0,1},{1,0},{2,3},{3,2},{4,5},{5,4},{6,7},{7,6},{8,9},{9,8},{10,11... | collective-permute-start | bytes 3145736 | tf_op jit(solution)/shard_map/ppermute | solution.py:890
  63.0 18.1 %collective-permute-start.17 = (bf16[1024,512]{1,0:T(8,128)(2,1)}, bf16[1024,512]{1,0:T(8,128)(2,1)S(1)}, u32[]{:S(2)}, u32[]{:S(2)}) collective-permute-start(bf16[1024,512]{1,0:T(8,128)(2,1)} %collective-permute-done.4.refs_3_), channel_id=1, source_target_pairs={{0,1},{1,0},{2,3},{3,2},{4,5},{5,4},{6,7},{7,6},{8,9},{9,8},{10,11... | collective-permute-start | bytes 3145736 | tf_op jit(solution)/shard_map/ppermute | solution.py:890
  71.8 27.4 %collective-permute-start.19 = (bf16[4,128,512]{2,1,0:T(8,128)(2,1)S(1)}, bf16[4,128,512]{2,1,0:T(8,128)(2,1)S(1)}, u32[]{:S(2)}, u32[]{:S(2)}) collective-permute-start(bf16[4,128,512]{2,1,0:T(8,128)(2,1)S(1)} %pad_maximum_fusion.refs_1_), channel_id=1, source_target_pairs={{0,2},{1,3},{2,0},{3,1},{4,6},{5,7},{6,4},{7,5},{8,10},{9,11},{10,... | collective-permute-start | bytes 1572872 | tf_op jit(solution)/shard_map/ppermute | solution.py:890
  73.4 26.4 %collective-permute-start.21 = (bf16[4,128,512]{2,1,0:T(8,128)(2,1)S(1)}, bf16[4,128,512]{2,1,0:T(8,128)(2,1)S(1)}, u32[]{:S(2)}, u32[]{:S(2)}) collective-permute-start(bf16[4,128,512]{2,1,0:T(8,128)(2,1)S(1)} %pad_maximum_fusion.refs_1_), channel_id=1, source_target_pairs={{0,4},{1,5},{2,6},{3,7},{4,0},{5,1},{6,2},{7,3},{8,12},{9,13},{10,... | collective-permute-start | bytes 1572872 | tf_op jit(solution)/shard_map/ppermute | solution.py:890
  74.9 24.9 %collective-permute-start.23 = (bf16[4,128,512]{2,1,0:T(8,128)(2,1)S(1)}, bf16[4,128,512]{2,1,0:T(8,128)(2,1)S(1)}, u32[]{:S(2)}, u32[]{:S(2)}) collective-permute-start(bf16[4,128,512]{2,1,0:T(8,128)(2,1)S(1)} %pad_maximum_fusion.refs_1_), channel_id=1, source_target_pairs={{0,6},{1,7},{2,4},{3,5},{4,2},{5,3},{6,0},{7,1},{8,14},{9,15},{10,... | collective-permute-start | bytes 1572872 | tf_op jit(solution)/shard_map/ppermute | solution.py:890
  102.1 18.2 %collective-permute-start.26 = (bf16[4,64,512]{2,1,0:T(8,128)(2,1)S(1)}, bf16[4,64,512]{2,1,0:T(8,128)(2,1)S(1)}, u32[]{:S(2)}, u32[]{:S(2)}) collective-permute-start(bf16[4,64,512]{2,1,0:T(8,128)(2,1)S(1)} %pad_maximum_fusion.2.refs_1_), channel_id=1, source_target_pairs={{0,2},{1,3},{2,0},{3,1},{4,6},{5,7},{6,4},{7,5},{8,10},{9,11},{10,... | collective-permute-start | bytes 786440 | tf_op jit(solution)/shard_map/ppermute | solution.py:890
  120.3 26.0 %collective-permute-start.32 = (bf16[1024,512]{1,0:T(8,128)(2,1)S(1)}, bf16[1024,512]{1,0:T(8,128)(2,1)}, u32[]{:S(2)}, u32[]{:S(2)}) collective-permute-start(bf16[1024,512]{1,0:T(8,128)(2,1)S(1)} %copy-done.15), channel_id=1, source_target_pairs={{0,6},{1,7},{2,4},{3,5},{4,2},{5,3},{6,0},{7,1},{8,14},{9,15},{10,... | collective-permute-start | bytes 3145736 | tf_op jit(solution)/shard_map/ppermute | solution.py:890
  147.3 19.3 %collective-permute-start.37 = (bf16[1024,512]{1,0:T(8,128)(2,1)}, bf16[1024,512]{1,0:T(8,128)(2,1)S(1)}, u32[]{:S(2)}, u32[]{:S(2)}) collective-permute-start(bf16[1024,512]{1,0:T(8,128)(2,1)} %collective-permute-done.32.refs_1_), channel_id=1, source_target_pairs={{0,1},{1,0},{2,3},{3,2},{4,5},{5,4},{6,7},{7,6},{8,9},{9,8},{10,11... | collective-permute-start | bytes 3145736 | tf_op jit(solution)/shard_map/ppermute | solution.py:890
  147.7 25.5 %collective-permute-start.33 = (bf16[1024,512]{1,0:T(8,128)(2,1)}, bf16[1024,512]{1,0:T(8,128)(2,1)}, u32[]{:S(2)}, u32[]{:S(2)}) collective-permute-start(bf16[1024,512]{1,0:T(8,128)(2,1)} %get-tuple-element.176), channel_id=1, source_target_pairs={{0,2},{1,3},{2,0},{3,1},{4,6},{5,7},{6,4},{7,5},{8,10},{9,11},{10,... | collective-permute-start | bytes 3145736 | tf_op jit(solution)/shard_map/ppermute | solution.py:890
  148.2 25.2 %collective-permute-start.34 = (bf16[1024,512]{1,0:T(8,128)(2,1)}, bf16[1024,512]{1,0:T(8,128)(2,1)}, u32[]{:S(2)}, u32[]{:S(2)}) collective-permute-start(bf16[1024,512]{1,0:T(8,128)(2,1)} %get-tuple-element.178), channel_id=1, source_target_pairs={{0,4},{1,5},{2,6},{3,7},{4,0},{5,1},{6,2},{7,3},{8,12},{9,13},{10,... | collective-permute-start | bytes 3145736 | tf_op jit(solution)/shard_map/ppermute | solution.py:890
  173.7 33.0 %collective-permute-start.36 = (bf16[1024,512]{1,0:T(8,128)(2,1)}, bf16[1024,512]{1,0:T(8,128)(2,1)}, u32[]{:S(2)}, u32[]{:S(2)}) collective-permute-start(bf16[1024,512]{1,0:T(8,128)(2,1)} %get-tuple-element.185), channel_id=1, source_target_pairs={{0,6},{1,7},{2,4},{3,5},{4,2},{5,3},{6,0},{7,1},{8,14},{9,15},{10,... | collective-permute-start | bytes 3145736 | tf_op jit(solution)/shard_map/ppermute | solution.py:890
  207.0 47.3 %collective-permute-start.42 = (bf16[1024,512]{1,0:T(8,128)(2,1)}, bf16[1024,512]{1,0:T(8,128)(2,1)}, u32[]{:S(2)}, u32[]{:S(2)}) collective-permute-start(bf16[1024,512]{1,0:T(8,128)(2,1)} %get-tuple-element.196), channel_id=1, source_target_pairs={{0,4},{1,5},{2,6},{3,7},{4,0},{5,1},{6,2},{7,3},{8,12},{9,13},{10,... | collective-permute-start | bytes 3145736 | tf_op jit(solution)/shard_map/ppermute | solution.py:890
  207.5 46.3 %collective-permute-start.41 = (bf16[1024,512]{1,0:T(8,128)(2,1)}, bf16[1024,512]{1,0:T(8,128)(2,1)}, u32[]{:S(2)}, u32[]{:S(2)}) collective-permute-start(bf16[1024,512]{1,0:T(8,128)(2,1)} %get-tuple-element.204), channel_id=1, source_target_pairs={{0,2},{1,3},{2,0},{3,1},{4,6},{5,7},{6,4},{7,5},{8,10},{9,11},{10,... | collective-permute-start | bytes 3145736 | tf_op jit(solution)/shard_map/ppermute | solution.py:890
  227.6 28.7 %collective-permute-start.43 = (bf16[1024,512]{1,0:T(8,128)(2,1)}, bf16[1024,512]{1,0:T(8,128)(2,1)}, u32[]{:S(2)}, u32[]{:S(2)}) collective-permute-start(bf16[1024,512]{1,0:T(8,128)(2,1)} %get-tuple-element.205), channel_id=1, source_target_pairs={{0,6},{1,7},{2,4},{3,5},{4,2},{5,3},{6,0},{7,1},{8,14},{9,15},{10,... | collective-permute-start | bytes 3145736 | tf_op jit(solution)/shard_map/ppermute | solution.py:890
  256.4 64.9 %all-to-all-start = ((bf16[8,512,512]{2,1,0:T(8,128)(2,1)}), bf16[8,512,512]{2,1,0:T(8,128)(2,1)}, u32[]{:S(2)}, u32[]{:S(2)}) async-start(bf16[8,512,512]{2,1,0:T(8,128)(2,1)} %bitcast.89), calls=%async_computation | async-start | bytes 8388608 | tf_op jit(solution)/shard_map/all_to_all | solution.py:945
  260.9 134.1 %reduce-scatter.3.cloned.1.call-start = ((), (), s32[]{:S(2)}) async-start(), calls=%async_computation.5 | async-start | bytes 2621440 | tf_op jit(solution)/shard_map/reduce_scatter | solution.py:1061
  289.8 105.2 %reduce-scatter.5.cloned.1.call-start = ((), (), s32[]{:S(2)}) async-start(), calls=%async_computation.6 | async-start | bytes 2621440 | tf_op jit(solution)/shard_map/reduce_scatter | solution.py:1062
  297.9 18.9 %collective-permute-start.49 = (bf16[4,64,512]{2,1,0:T(8,128)(2,1)}, bf16[4,64,512]{2,1,0:T(8,128)(2,1)S(1)}, u32[]{:S(2)}, u32[]{:S(2)}) collective-permute-start(bf16[4,64,512]{2,1,0:T(8,128)(2,1)} %get-tuple-element.237), channel_id=1, source_target_pairs={{0,2},{1,3},{2,0},{3,1},{4,6},{5,7},{6,4},{7,5},{8,10},{9,11},{10,... | collective-permute-start | bytes 786440 | tf_op jit(solution)/shard_map/ppermute | solution.py:890
  301.2 20.0 %collective-permute-start.51 = (bf16[4,64,512]{2,1,0:T(8,128)(2,1)}, bf16[4,64,512]{2,1,0:T(8,128)(2,1)S(1)}, u32[]{:S(2)}, u32[]{:S(2)}) collective-permute-start(bf16[4,64,512]{2,1,0:T(8,128)(2,1)} %get-tuple-element.239), channel_id=1, source_target_pairs={{0,6},{1,7},{2,4},{3,5},{4,2},{5,3},{6,0},{7,1},{8,14},{9,15},{10,... | collective-permute-start | bytes 786440 | tf_op jit(solution)/shard_map/ppermute | solution.py:890
  330.1 34.0 %all-to-all-start.2 = ((bf16[4,4,128,512]{3,2,1,0:T(8,128)(2,1)}), bf16[4,4,128,512]{3,2,1,0:T(8,128)(2,1)}, u32[]{:S(2)}, u32[]{:S(2)}) async-start(bf16[4,4,128,512]{3,2,1,0:T(8,128)(2,1)} %shard_map.230), calls=%async_computation.4 | async-start | bytes 4194304 | tf_op jit(solution)/shard_map/all_to_all | solution.py:945
  364.2 23.1 %all-to-all-start.1 = ((bf16[4,4,80,512]{3,2,1,0:T(8,128)(2,1)}), bf16[4,4,80,512]{3,2,1,0:T(8,128)(2,1)S(1)}, u32[]{:S(2)}, u32[]{:S(2)}) async-start(bf16[4,4,80,512]{3,2,1,0:T(8,128)(2,1)} %shard_map.232), calls=%async_computation.1 | async-start | bytes 2621440 | tf_op jit(solution)/shard_map/all_to_all | solution.py:945
  368.4 56.4 %all-gather.12.cloned.1.call-start = ((), (), s32[]{:S(2)}) async-start(), calls=%async_computation.9 | async-start | bytes 1769472 | tf_op jit(solution)/shard_map/all_gather | solution.py:1085
  371.4 19.1 %collective-permute-start.57 = (bf16[192,512]{1,0:T(8,128)(2,1)}, bf16[192,512]{1,0:T(8,128)(2,1)S(1)}, u32[]{:S(2)}, u32[]{:S(2)}) collective-permute-start(bf16[192,512]{1,0:T(8,128)(2,1)} %get-tuple-element.266), channel_id=1, source_target_pairs={{0,8},{8,16},{16,24},{24,0},{1,9},{9,17},{17,25},{25,1},{2,10},{10... | collective-permute-start | bytes 589832 | tf_op jit(solution)/shard_map/ppermute | solution.py:894
  372.3 19.3 %collective-permute-start.58 = (bf16[192,512]{1,0:T(8,128)(2,1)}, bf16[192,512]{1,0:T(8,128)(2,1)S(1)}, u32[]{:S(2)}, u32[]{:S(2)}) collective-permute-start(bf16[192,512]{1,0:T(8,128)(2,1)} %get-tuple-element.268), channel_id=1, source_target_pairs={{0,16},{8,24},{16,0},{24,8},{1,17},{9,25},{17,1},{25,9},{2,18},{10... | collective-permute-start | bytes 589832 | tf_op jit(solution)/shard_map/ppermute | solution.py:894
  374.3 17.3 %collective-permute-start.59 = (bf16[192,512]{1,0:T(8,128)(2,1)}, bf16[192,512]{1,0:T(8,128)(2,1)S(1)}, u32[]{:S(2)}, u32[]{:S(2)}) collective-permute-start(bf16[192,512]{1,0:T(8,128)(2,1)} %get-tuple-element.270), channel_id=1, source_target_pairs={{0,24},{8,0},{16,8},{24,16},{1,25},{9,1},{17,9},{25,17},{2,26},{10... | collective-permute-start | bytes 589832 | tf_op jit(solution)/shard_map/ppermute | solution.py:894
  (96 other events, 798.4 us)
Sparse Core Ops, SparseCore 0:
  44.4 46.3 all-gather.7
  92.4 44.6 all-gather.9
  289.9 44.6 reduce-scatter.2
  336.8 45.7 reduce-scatter.4
  395.1 29.6 all-gather.11

commit v5 on v4

--- a/solution.py
+++ b/solution.py
@@ -371,7 +371,7 @@
         acc_ref[pl.ds(k0, KB), :] += jnp.concatenate(dk + dv, axis=1)
         return carry
 
-    lax.fori_loop(0, PACK // QB, block, 0, unroll=2)
+    lax.fori_loop(0, PACK // QB, block, 0, unroll=4)
     dqkv_ref[:, D:] = acc_ref[...].astype(BF)
 
 

time: 443 us -> 443 us (level)
  no operation moved by 1% of the time
where the time goes in v5:
time: 443 us; the launch traced here: 436 us
  Pallas kernels  236 us (53%)
  starting transfers between devices  67 us (15%)
  waiting for transfers between devices  53.9 us (12%)
  local copies, waits for them, and re-layouts  43.4 us (10%)
  between operations  15.1 us (3%)
  blocking collectives  11.8 us (3%)
  other arithmetic  8.89 us (2%)
    pallas_call x15, Pallas kernels, call(): pl.pallas_call(kernel, out_shape=out_shape, compiler_params=pltpu.Compile...  128 us
    pallas_call x11, Pallas kernels, staged(): pl.pallas_call(kernel, out_shape=list(small_outs) + shapes, in_specs=spac...  109 us
    ppermute x51, starting transfers between devices, flip(): return lax.ppermute(rows, EXPERT, [(i, i ^ j) for i in range(ex)])  34.1 us
    ppermute x51, waiting for transfers between devices, flip(): return lax.ppermute(rows, EXPERT, [(i, i ^ j) for i in range(ex)])  32.5 us
    unnamed x135, local copies, waits for them, and re-layouts  30.6 us
    ppermute x9, starting transfers between devices, turn(): return lax.ppermute(rows, 'dp', [(i, (i + k) % dp) for i in range(dp)])  18.6 us
    ppermute x9, waiting for transfers between devices, turn(): return lax.ppermute(rows, 'dp', [(i, (i + k) % dp) for i in range(dp)])  18.2 us
    all_to_all x3, starting transfers between devices, swap(): return lax.all_to_all(parts, axis, split_axis=0, concat_axis=0, tiled=True)  13.6 us
  transfers between devices with their start and end apart: 68, of which 23 were waited for; matrix products, arithmetic and copies ran while one was open for 4% of the time, Pallas kernels for 54%

profile of v5, /device:TPU:0, one launch (start us, length us, event | category | flops | bytes accessed | tf_op | source)
XLA Modules:
  0.0 436.4 jit_solution(18067817955456560933)
XLA Ops:
  15.5 5.0 %collective-permute-start.2 = (bf16[272,512]{1,0:T(8,128)(2,1)S(1)}, bf16[272,512]{1,0:T(8,128)(2,1)S(1)}, u32[]{:S(2)}, u32[]{:S(2)}) collective-permute-start(bf16[272,512]{1,0:T(8,128)(2,1)S(1)} %get-tuple-element.280), channel_id=1, source_target_pairs={{0,24},{8,0},{16,8},{24,16},{1,25},{9,1},{17,9},{25,17},{2,26},{10... | collective-permute-start | bytes 835592 | tf_op jit(solution)/shard_map/ppermute | solution.py:894
  29.0 15.3 %collective-permute-done.1 = bf16[272,512]{1,0:T(8,128)(2,1)S(1)} collective-permute-done((bf16[272,512]{1,0:T(8,128)(2,1)S(1)}, bf16[272,512]{1,0:T(8,128)(2,1)S(1)}, u32[]{:S(2)}, u32[]{:S(2)}) %collective-permute-start.1) | collective-permute-done | bytes 278560 | tf_op jit(solution)/shard_map/ppermute | solution.py:894
  57.2 2.7 collective-permute-done.7
  64.9 4.4 %collective-permute-done.13.refs_7_ = bf16[4,80,512]{2,1,0:T(8,128)(2,1)S(1)} collective-permute-done((bf16[4,80,512]{2,1,0:T(8,128)(2,1)S(1)}, bf16[4,80,512]{2,1,0:T(8,128)(2,1)S(1)}, u32[]{:S(2)}, u32[]{:S(2)}) %collective-permute-start.13) | collective-permute-done | bytes 327712 | tf_op jit(solution)/shard_map/ppermute | solution.py:890
  76.2 3.1 shard_map.215
  81.1 6.8 %shard_map.216 = (bf16[2048,512]{1,0:T(8,128)(2,1)S(1)}, f32[2048,8]{1,0:T(8,128)S(1)}) custom-call(f32[64,128]{1,0:T(8,128)S(1)} %pad_maximum_fusion.3.refs_0_, bf16[1024,512]{1,0:T(8,128)(2,1)} %collective-permute-done.3.refs_1_, bf16[1024,512]{1,0:T(8,128)(2,1)S(1)} %collective-permute-done.16.refs_2_, bf16[1024,512]{1,0:T(8,128)(2,1)} %collective-permute-done.4.refs_3_, ...), custom_call_target="tpu_custom_call" | custom-call | flops 1073741824 | bytes 2097152 | tf_op jit(solution)/shard_map/pallas_call | solution.py:195
  90.2 7.4 %shard_map.217 = (f32[1024,512]{1,0:T(8,128)S(1)}, bf16[1024,512]{1,0:T(8,128)(2,1)S(1)}, bf16[1024,1536]{1,0:T(8,128)(2,1)S(1)}, bf16[1024,512]{1,0:T(8,128)(2,1)S(1)}) custom-call(bf16[1024,512]{1,0:T(8,128)(2,1)S(1)} %copy-done.22, f32[8,512]{1,0:T(8,128)S(1)} %get-tuple-element.151.np_ref.refs_0_.refs_1_, ...), custom_call_target="tpu_custom_call" | custom-call | flops 3000000000 | bytes 6291456 | tf_op jit(solution)/shard_map/pallas_call | solution.py:79
  106.5 10.7 %shard_map.219 = (f32[1024,512]{1,0:T(8,128)S(1)}, bf16[1024,512]{1,0:T(8,128)(2,1)S(1)}, bf16[1024,2048]{1,0:T(8,128)(2,1)S(1)}, bf16[1024,2048]{1,0:T(8,128)(2,1)S(1)}) custom-call(f32[8,512]{1,0:T(8,128)S(1)} %get-tuple-element.151.np_ref.refs_0_.refs_1_, f32[1024,512]{1,0:T(8,128)S(1)} %get-tuple-element.158.refs_1_.refs_8_, ...), custom_call_target="tpu_custom_call" | custom-call | flops 2150000128 | bytes 8912896 | tf_op jit(solution)/shard_map/pallas_call | solution.py:195
  126.2 15.5 %shard_map.221 = (f32[1024,512]{1,0:T(8,128)S(1)}, bf16[1024,512]{1,0:T(8,128)(2,1)S(1)}, bf16[1024,1536]{1,0:T(8,128)(2,1)}, bf16[1024,512]{1,0:T(8,128)(2,1)S(...) custom-call(f32[1024,512]{1,0:T(8,128)S(1)} %get-tuple-element.166.x, ...), custom_call_target="tpu_custom_call" | custom-call | flops 3000000000 | bytes 6291456 | tf_op jit(solution)/shard_map/pallas_call | solution.py:79
  150.2 16.5 %shard_map.222 = (bf16[1024,512]{1,0:T(8,128)(2,1)}, f32[8,128]{1,0:T(8,128)}, bf16[4096,512]{1,0:T(8,128)(2,1)}, bf16[4096,2048]{1,0:T(8,128)(2,1)}, bf16[4096,...) custom-call(s32[2]{0:T(128)} %copy-done.18, bf16[1024,512]{1,0:T(8,128)(2,1)} %copy-done.24, ...), custom_call_target="tpu_custom_call" | custom-call | flops 4294967296 | bytes 6815744 | tf_op jit(solution)/shard_map/pallas_call | solution.py:79
  166.7 3.4 shard_map.223
  177.7 29.0 %shard_map.224 = (bf16[1024,512]{1,0:T(8,128)(2,1)}, bf16[1024,512]{1,0:T(8,128)(2,1)}, f32[8,128]{1,0:T(8,128)}, bf16[4096,512]{1,0:T(8,128)(2,1)}, bf16[4096,2...) custom-call(s32[2]{0:T(128)} %copy-done.18, ...), custom_call_target="tpu_custom_call", output_to_operand_aliasing={{3}: (9, {}), {4}: (10, {}), {5}: (11, {}), {6}: (12, {}), ... | custom-call | flops 8589934592 | bytes 13631488 | tf_op jit(solution)/shard_map/pallas_call | solution.py:79
  210.7 16.8 %shard_map.225 = (bf16[1024,512]{1,0:T(8,128)(2,1)}, f32[8,128]{1,0:T(8,128)}, bf16[4096,512]{1,0:T(8,128)(2,1)}, bf16[4096,2048]{1,0:T(8,128)(2,1)}, bf16[4096,...) custom-call(s32[2]{0:T(128)} %copy-done.18, ...), custom_call_target="tpu_custom_call", output_to_operand_aliasing={{2}: (7, {}), {3}: (8, {}), {4}: (9, {}), {5}: (10, {}), {6... | custom-call | flops 4294967296 | bytes 6815744 | tf_op jit(solution)/shard_map/pallas_call | solution.py:79
  228.3 25.3 %shard_map.226 = (bf16[512,2048]{1,0:T(8,128)(2,1)}, bf16[2048,512]{1,0:T(8,128)(2,1)}) custom-call(bf16[4096,2048]{1,0:T(8,128)(2,1)} %get-tuple-element.206.act_ref, bf16[4096,2048]{1,0:T(8,128)(2,1)} %get-tuple-element.207.du_ref, bf16[4096,512]{1,0:T(8,128)(2,1)} %get-tuple-element.208.buf_ref, bf16[4096,512]{1,0:T(8,128)(2,1)} %get-tuple-element.209.dout_ref), custom_call_target="tpu_custom_call" | custom-call | flops 8589934592 | bytes 23068672 | tf_op jit(solution)/shard_map/pallas_call | solution.py:79
  256.4 4.6 %all-to-all-start = ((bf16[8,512,512]{2,1,0:T(8,128)(2,1)}), bf16[8,512,512]{2,1,0:T(8,128)(2,1)}, u32[]{:S(2)}, u32[]{:S(2)}) async-start(bf16[8,512,512]{2,1,0:T(8,128)(2,1)} %bitcast.89), calls=%async_computation | async-start | bytes 8388608 | tf_op jit(solution)/shard_map/all_to_all | solution.py:945
  262.4 27.5 %shard_map.227 = (f32[2,512]{1,0:T(2,128)}, f32[2,512]{1,0:T(2,128)}, f32[1024,512]{1,0:T(8,128)}, bf16[4,4,64,512]{3,2,1,0:T(8,128)(2,1)}, bf16[4,4,64,512]{3,2,1,0:T(8,128)(2,1)}) custom-call(s32[2]{0:T(128)} %copy-done.18, f32[8,512]{1,0:T(8,128)} %copy-done.20, f32[1024,8]{1,0:T(8,128)} %copy-done.17, f32[1024,512]{1,0:T(8,128)} %copy-done.6, ...), custom_call_target="tpu_custom_call" | custom-call | flops 8000000000 | bytes 10485760 | tf_op jit(solution)/shard_map/pallas_call | solution.py:195
  294.9 3.2 shard_map.228
  301.6 15.3 %shard_map.229 = (f32[2,512]{1,0:T(2,128)}, f32[1024,512]{1,0:T(8,128)}, bf16[4,4,128,512]{3,2,1,0:T(8,128)(2,1)}, bf16[4,4,128,512]{3,2,1,0:T(8,128)(2,1)}) custom-call(s32[2]{0:T(128)} %copy-done.18, f32[8,512]{1,0:T(8,128)} %copy-done.20, f32[1024,512]{1,0:T(8,128)} %get-tuple-element.224.refs_2_, bf16[2048,512]{1,0:T(8,128)(2,1)} %copy-done.8, ...), custom_call_target="tpu_custom_call" | custom-call | flops 4300000256 | bytes 12582912 | tf_op jit(solution)/shard_map/pallas_call | solution.py:195
  317.1 4.2 collective-permute-done.51.refs_4_
  321.9 3.8 collective-permute-done.52.refs_2_
  325.7 4.4 %shard_map.230 = bf16[4,4,128,512]{3,2,1,0:T(8,128)(2,1)} custom-call(s32[2]{0:T(128)} %copy-done.18, bf16[4,4,128,512]{3,2,1,0:T(8,128)(2,1)} %get-tuple-element.235.refs_1_, bf16[4,4,128,512]{3,2,1,0:T(8,128)(2,1)} %collective-permute-done.52.refs_2_), custom_call_target="tpu_custom_call" | custom-call | flops 500000 | bytes 3145728 | tf_op jit(solution)/shard_map/pallas_call | solution.py:195
  330.1 4.9 %all-to-all-start.2 = ((bf16[4,4,128,512]{3,2,1,0:T(8,128)(2,1)}), bf16[4,4,128,512]{3,2,1,0:T(8,128)(2,1)}, u32[]{:S(2)}, u32[]{:S(2)}) async-start(bf16[4,4,128,512]{3,2,1,0:T(8,128)(2,1)} %shard_map.230), calls=%async_computation.4 | async-start | bytes 4194304 | tf_op jit(solution)/shard_map/all_to_all | solution.py:945
  335.0 20.9 %shard_map.231 = (f32[2,512]{1,0:T(2,128)}, f32[1024,512]{1,0:T(8,128)}, bf16[4,4,80,512]{3,2,1,0:T(8,128)(2,1)}, bf16[4,4,80,512]{3,2,1,0:T(8,128)(2,1)}) custom-call(s32[2]{0:T(128)} %copy-done.18, f32[8,512]{1,0:T(8,128)} %copy-done.20, f32[2,512]{1,0:T(2,128)} %get-tuple-element.228.refs_2_, f32[2,512]{1,0:T(2,128)} %get-tuple-element.229.refs_3_, ...), custom_call_target="tpu_custom_call" | custom-call | flops 7000000000 | bytes 8388608 | tf_op jit(solution)/shard_map/pallas_call | solution.py:195
  356.1 3.1 collective-permute-done.53.refs_2_
  360.3 3.6 shard_map.232
  363.9 4.2 all-to-all-start.1
  368.1 3.0 shard_map.236
  374.0 3.1 collective-permute-start.59
  377.1 9.9 %shard_map.233 = bf16[1024,512]{1,0:T(8,128)(2,1)} custom-call(s32[2]{0:T(128)} %copy-done.18, f32[1024,8]{1,0:T(8,128)} %copy-done.17, f32[4096,8]{1,0:T(8,128)} %copy-done.4, bf16[4096,512]{1,0:T(8,128)(2,1)} %bitcast.29.refs_3_, f32[1024,512]{1,0:T(8,128)} %copy-done.6), custom_call_target="tpu_custom_call" | custom-call | flops 2147483648 | bytes 7340032 | tf_op jit(solution)/shard_map/pallas_call | solution.py:195
  395.1 4.2 collective-permute-start.54
  410.1 11.8 %all-gather.2 = bf16[640,512]{1,0:T(8,128)(2,1)S(1)} all-gather(bf16[80,512]{1,0:T(8,128)(2,1)} %shard_map.235), channel_id=4, replica_groups=mesh['dp'=4,'xy'=4,'core'=2] {'xy','core'}, dimensions={0}, use_global_device_ids=true | all-gather | bytes 737280 | tf_op jit(solution)/shard_map/all_gather | solution.py:1090
  421.9 3.1 all-gather.12.cloned.1.call-done
  (349 shorter events, 124.8 us)
Async XLA Ops:
  7.2 141.9 %all-gather.8.cloned.1.call-start = ((), (), s32[]{:S(2)}) async-start(), calls=%async_computation.7 | async-start | bytes 2621440 | tf_op jit(solution)/shard_map/all_gather | solution.py:1030
  20.6 23.7 %collective-permute-start.1 = (bf16[272,512]{1,0:T(8,128)(2,1)S(1)}, bf16[272,512]{1,0:T(8,128)(2,1)S(1)}, u32[]{:S(2)}, u32[]{:S(2)}) collective-permute-start(bf16[272,512]{1,0:T(8,128)(2,1)S(1)} %get-tuple-element.280), channel_id=1, source_target_pairs={{0,16},{8,24},{16,0},{24,8},{1,17},{9,25},{17,1},{25,9},{2,18},{10... | collective-permute-start | bytes 835592 | tf_op jit(solution)/shard_map/ppermute | solution.py:894
  20.6 23.7 %collective-permute-start = (bf16[272,512]{1,0:T(8,128)(2,1)S(1)}, bf16[272,512]{1,0:T(8,128)(2,1)S(1)}, u32[]{:S(2)}, u32[]{:S(2)}) collective-permute-start(bf16[272,512]{1,0:T(8,128)(2,1)S(1)} %get-tuple-element.280), channel_id=1, source_target_pairs={{0,8},{8,16},{16,24},{24,0},{1,9},{9,17},{17,25},{25,1},{2,10},{10... | collective-permute-start | bytes 835592 | tf_op jit(solution)/shard_map/ppermute | solution.py:894
  21.6 28.2 %collective-permute-start.3 = (bf16[1024,512]{1,0:T(8,128)(2,1)}, bf16[1024,512]{1,0:T(8,128)(2,1)}, u32[]{:S(2)}, u32[]{:S(2)}) collective-permute-start(bf16[1024,512]{1,0:T(8,128)(2,1)} %refs_4_.1), channel_id=1, source_target_pairs={{0,2},{1,3},{2,0},{3,1},{4,6},{5,7},{6,4},{7,5},{8,10},{9,11},{10,... | collective-permute-start | bytes 3145736 | tf_op jit(solution)/shard_map/ppermute | solution.py:890
  23.1 26.7 %collective-permute-start.4 = (bf16[1024,512]{1,0:T(8,128)(2,1)}, bf16[1024,512]{1,0:T(8,128)(2,1)}, u32[]{:S(2)}, u32[]{:S(2)}) collective-permute-start(bf16[1024,512]{1,0:T(8,128)(2,1)} %refs_4_.1), channel_id=1, source_target_pairs={{0,4},{1,5},{2,6},{3,7},{4,0},{5,1},{6,2},{7,3},{8,12},{9,13},{10,... | collective-permute-start | bytes 3145736 | tf_op jit(solution)/shard_map/ppermute | solution.py:890
  28.9 40.4 %collective-permute-start.15 = (bf16[1024,512]{1,0:T(8,128)(2,1)S(1)}, bf16[1024,512]{1,0:T(8,128)(2,1)S(1)}, u32[]{:S(2)}, u32[]{:S(2)}) collective-permute-start(bf16[1024,512]{1,0:T(8,128)(2,1)S(1)} %copy-done.15), channel_id=1, source_target_pairs={{0,1},{1,0},{2,3},{3,2},{4,5},{5,4},{6,7},{7,6},{8,9},{9,8},{10,11... | collective-permute-start | bytes 3145736 | tf_op jit(solution)/shard_map/ppermute | solution.py:890
  44.3 104.9 %all-gather.10.cloned.1.call-start = ((), (), s32[]{:S(2)}) async-start(), calls=%async_computation.8 | async-start | bytes 2621440 | tf_op jit(solution)/shard_map/all_gather | solution.py:1031
  62.5 18.6 %collective-permute-start.16 = (bf16[1024,512]{1,0:T(8,128)(2,1)}, bf16[1024,512]{1,0:T(8,128)(2,1)S(1)}, u32[]{:S(2)}, u32[]{:S(2)}) collective-permute-start(bf16[1024,512]{1,0:T(8,128)(2,1)} %collective-permute-done.3.refs_1_), channel_id=1, source_target_pairs={{0,1},{1,0},{2,3},{3,2},{4,5},{5,4},{6,7},{7,6},{8,9},{9,8},{10,11... | collective-permute-start | bytes 3145736 | tf_op jit(solution)/shard_map/ppermute | solution.py:890
  63.0 18.1 %collective-permute-start.17 = (bf16[1024,512]{1,0:T(8,128)(2,1)}, bf16[1024,512]{1,0:T(8,128)(2,1)S(1)}, u32[]{:S(2)}, u32[]{:S(2)}) collective-permute-start(bf16[1024,512]{1,0:T(8,128)(2,1)} %collective-permute-done.4.refs_3_), channel_id=1, source_target_pairs={{0,1},{1,0},{2,3},{3,2},{4,5},{5,4},{6,7},{7,6},{8,9},{9,8},{10,11... | collective-permute-start | bytes 3145736 | tf_op jit(solution)/shard_map/ppermute | solution.py:890
  71.8 27.4 %collective-permute-start.19 = (bf16[4,128,512]{2,1,0:T(8,128)(2,1)S(1)}, bf16[4,128,512]{2,1,0:T(8,128)(2,1)S(1)}, u32[]{:S(2)}, u32[]{:S(2)}) collective-permute-start(bf16[4,128,512]{2,1,0:T(8,128)(2,1)S(1)} %pad_maximum_fusion.refs_1_), channel_id=1, source_target_pairs={{0,2},{1,3},{2,0},{3,1},{4,6},{5,7},{6,4},{7,5},{8,10},{9,11},{10,... | collective-permute-start | bytes 1572872 | tf_op jit(solution)/shard_map/ppermute | solution.py:890
  73.4 26.4 %collective-permute-start.21 = (bf16[4,128,512]{2,1,0:T(8,128)(2,1)S(1)}, bf16[4,128,512]{2,1,0:T(8,128)(2,1)S(1)}, u32[]{:S(2)}, u32[]{:S(2)}) collective-permute-start(bf16[4,128,512]{2,1,0:T(8,128)(2,1)S(1)} %pad_maximum_fusion.refs_1_), channel_id=1, source_target_pairs={{0,4},{1,5},{2,6},{3,7},{4,0},{5,1},{6,2},{7,3},{8,12},{9,13},{10,... | collective-permute-start | bytes 1572872 | tf_op jit(solution)/shard_map/ppermute | solution.py:890
  74.9 24.9 %collective-permute-start.23 = (bf16[4,128,512]{2,1,0:T(8,128)(2,1)S(1)}, bf16[4,128,512]{2,1,0:T(8,128)(2,1)S(1)}, u32[]{:S(2)}, u32[]{:S(2)}) collective-permute-start(bf16[4,128,512]{2,1,0:T(8,128)(2,1)S(1)} %pad_maximum_fusion.refs_1_), channel_id=1, source_target_pairs={{0,6},{1,7},{2,4},{3,5},{4,2},{5,3},{6,0},{7,1},{8,14},{9,15},{10,... | collective-permute-start | bytes 1572872 | tf_op jit(solution)/shard_map/ppermute | solution.py:890
  102.1 18.2 %collective-permute-start.26 = (bf16[4,64,512]{2,1,0:T(8,128)(2,1)S(1)}, bf16[4,64,512]{2,1,0:T(8,128)(2,1)S(1)}, u32[]{:S(2)}, u32[]{:S(2)}) collective-permute-start(bf16[4,64,512]{2,1,0:T(8,128)(2,1)S(1)} %pad_maximum_fusion.2.refs_1_), channel_id=1, source_target_pairs={{0,2},{1,3},{2,0},{3,1},{4,6},{5,7},{6,4},{7,5},{8,10},{9,11},{10,... | collective-permute-start | bytes 786440 | tf_op jit(solution)/shard_map/ppermute | solution.py:890
  120.3 26.0 %collective-permute-start.32 = (bf16[1024,512]{1,0:T(8,128)(2,1)S(1)}, bf16[1024,512]{1,0:T(8,128)(2,1)}, u32[]{:S(2)}, u32[]{:S(2)}) collective-permute-start(bf16[1024,512]{1,0:T(8,128)(2,1)S(1)} %copy-done.15), channel_id=1, source_target_pairs={{0,6},{1,7},{2,4},{3,5},{4,2},{5,3},{6,0},{7,1},{8,14},{9,15},{10,... | collective-permute-start | bytes 3145736 | tf_op jit(solution)/shard_map/ppermute | solution.py:890
  147.3 19.3 %collective-permute-start.37 = (bf16[1024,512]{1,0:T(8,128)(2,1)}, bf16[1024,512]{1,0:T(8,128)(2,1)S(1)}, u32[]{:S(2)}, u32[]{:S(2)}) collective-permute-start(bf16[1024,512]{1,0:T(8,128)(2,1)} %collective-permute-done.32.refs_1_), channel_id=1, source_target_pairs={{0,1},{1,0},{2,3},{3,2},{4,5},{5,4},{6,7},{7,6},{8,9},{9,8},{10,11... | collective-permute-start | bytes 3145736 | tf_op jit(solution)/shard_map/ppermute | solution.py:890
  147.7 25.5 %collective-permute-start.33 = (bf16[1024,512]{1,0:T(8,128)(2,1)}, bf16[1024,512]{1,0:T(8,128)(2,1)}, u32[]{:S(2)}, u32[]{:S(2)}) collective-permute-start(bf16[1024,512]{1,0:T(8,128)(2,1)} %get-tuple-element.176), channel_id=1, source_target_pairs={{0,2},{1,3},{2,0},{3,1},{4,6},{5,7},{6,4},{7,5},{8,10},{9,11},{10,... | collective-permute-start | bytes 3145736 | tf_op jit(solution)/shard_map/ppermute | solution.py:890
  148.2 25.2 %collective-permute-start.34 = (bf16[1024,512]{1,0:T(8,128)(2,1)}, bf16[1024,512]{1,0:T(8,128)(2,1)}, u32[]{:S(2)}, u32[]{:S(2)}) collective-permute-start(bf16[1024,512]{1,0:T(8,128)(2,1)} %get-tuple-element.178), channel_id=1, source_target_pairs={{0,4},{1,5},{2,6},{3,7},{4,0},{5,1},{6,2},{7,3},{8,12},{9,13},{10,... | collective-permute-start | bytes 3145736 | tf_op jit(solution)/shard_map/ppermute | solution.py:890
  173.7 33.0 %collective-permute-start.36 = (bf16[1024,512]{1,0:T(8,128)(2,1)}, bf16[1024,512]{1,0:T(8,128)(2,1)}, u32[]{:S(2)}, u32[]{:S(2)}) collective-permute-start(bf16[1024,512]{1,0:T(8,128)(2,1)} %get-tuple-element.185), channel_id=1, source_target_pairs={{0,6},{1,7},{2,4},{3,5},{4,2},{5,3},{6,0},{7,1},{8,14},{9,15},{10,... | collective-permute-start | bytes 3145736 | tf_op jit(solution)/shard_map/ppermute | solution.py:890
  207.0 47.1 %collective-permute-start.42 = (bf16[1024,512]{1,0:T(8,128)(2,1)}, bf16[1024,512]{1,0:T(8,128)(2,1)}, u32[]{:S(2)}, u32[]{:S(2)}) collective-permute-start(bf16[1024,512]{1,0:T(8,128)(2,1)} %get-tuple-element.196), channel_id=1, source_target_pairs={{0,4},{1,5},{2,6},{3,7},{4,0},{5,1},{6,2},{7,3},{8,12},{9,13},{10,... | collective-permute-start | bytes 3145736 | tf_op jit(solution)/shard_map/ppermute | solution.py:890
  207.5 46.1 %collective-permute-start.41 = (bf16[1024,512]{1,0:T(8,128)(2,1)}, bf16[1024,512]{1,0:T(8,128)(2,1)}, u32[]{:S(2)}, u32[]{:S(2)}) collective-permute-start(bf16[1024,512]{1,0:T(8,128)(2,1)} %get-tuple-element.204), channel_id=1, source_target_pairs={{0,2},{1,3},{2,0},{3,1},{4,6},{5,7},{6,4},{7,5},{8,10},{9,11},{10,... | collective-permute-start | bytes 3145736 | tf_op jit(solution)/shard_map/ppermute | solution.py:890
  227.4 28.9 %collective-permute-start.43 = (bf16[1024,512]{1,0:T(8,128)(2,1)}, bf16[1024,512]{1,0:T(8,128)(2,1)}, u32[]{:S(2)}, u32[]{:S(2)}) collective-permute-start(bf16[1024,512]{1,0:T(8,128)(2,1)} %get-tuple-element.205), channel_id=1, source_target_pairs={{0,6},{1,7},{2,4},{3,5},{4,2},{5,3},{6,0},{7,1},{8,14},{9,15},{10,... | collective-permute-start | bytes 3145736 | tf_op jit(solution)/shard_map/ppermute | solution.py:890
  256.4 64.9 %all-to-all-start = ((bf16[8,512,512]{2,1,0:T(8,128)(2,1)}), bf16[8,512,512]{2,1,0:T(8,128)(2,1)}, u32[]{:S(2)}, u32[]{:S(2)}) async-start(bf16[8,512,512]{2,1,0:T(8,128)(2,1)} %bitcast.89), calls=%async_computation | async-start | bytes 8388608 | tf_op jit(solution)/shard_map/all_to_all | solution.py:945
  260.9 134.1 %reduce-scatter.3.cloned.1.call-start = ((), (), s32[]{:S(2)}) async-start(), calls=%async_computation.5 | async-start | bytes 2621440 | tf_op jit(solution)/shard_map/reduce_scatter | solution.py:1061
  290.0 105.1 %reduce-scatter.5.cloned.1.call-start = ((), (), s32[]{:S(2)}) async-start(), calls=%async_computation.6 | async-start | bytes 2621440 | tf_op jit(solution)/shard_map/reduce_scatter | solution.py:1062
  298.1 18.9 %collective-permute-start.49 = (bf16[4,64,512]{2,1,0:T(8,128)(2,1)}, bf16[4,64,512]{2,1,0:T(8,128)(2,1)S(1)}, u32[]{:S(2)}, u32[]{:S(2)}) collective-permute-start(bf16[4,64,512]{2,1,0:T(8,128)(2,1)} %get-tuple-element.237), channel_id=1, source_target_pairs={{0,2},{1,3},{2,0},{3,1},{4,6},{5,7},{6,4},{7,5},{8,10},{9,11},{10,... | collective-permute-start | bytes 786440 | tf_op jit(solution)/shard_map/ppermute | solution.py:890
  301.4 19.9 %collective-permute-start.51 = (bf16[4,64,512]{2,1,0:T(8,128)(2,1)}, bf16[4,64,512]{2,1,0:T(8,128)(2,1)S(1)}, u32[]{:S(2)}, u32[]{:S(2)}) collective-permute-start(bf16[4,64,512]{2,1,0:T(8,128)(2,1)} %get-tuple-element.239), channel_id=1, source_target_pairs={{0,6},{1,7},{2,4},{3,5},{4,2},{5,3},{6,0},{7,1},{8,14},{9,15},{10,... | collective-permute-start | bytes 786440 | tf_op jit(solution)/shard_map/ppermute | solution.py:890
  330.1 33.8 %all-to-all-start.2 = ((bf16[4,4,128,512]{3,2,1,0:T(8,128)(2,1)}), bf16[4,4,128,512]{3,2,1,0:T(8,128)(2,1)}, u32[]{:S(2)}, u32[]{:S(2)}) async-start(bf16[4,4,128,512]{3,2,1,0:T(8,128)(2,1)} %shard_map.230), calls=%async_computation.4 | async-start | bytes 4194304 | tf_op jit(solution)/shard_map/all_to_all | solution.py:945
  363.9 23.1 %all-to-all-start.1 = ((bf16[4,4,80,512]{3,2,1,0:T(8,128)(2,1)}), bf16[4,4,80,512]{3,2,1,0:T(8,128)(2,1)S(1)}, u32[]{:S(2)}, u32[]{:S(2)}) async-start(bf16[4,4,80,512]{3,2,1,0:T(8,128)(2,1)} %shard_map.232), calls=%async_computation.1 | async-start | bytes 2621440 | tf_op jit(solution)/shard_map/all_to_all | solution.py:945
  368.1 56.9 %all-gather.12.cloned.1.call-start = ((), (), s32[]{:S(2)}) async-start(), calls=%async_computation.9 | async-start | bytes 1769472 | tf_op jit(solution)/shard_map/all_gather | solution.py:1085
  371.1 19.1 %collective-permute-start.57 = (bf16[192,512]{1,0:T(8,128)(2,1)}, bf16[192,512]{1,0:T(8,128)(2,1)S(1)}, u32[]{:S(2)}, u32[]{:S(2)}) collective-permute-start(bf16[192,512]{1,0:T(8,128)(2,1)} %get-tuple-element.266), channel_id=1, source_target_pairs={{0,8},{8,16},{16,24},{24,0},{1,9},{9,17},{17,25},{25,1},{2,10},{10... | collective-permute-start | bytes 589832 | tf_op jit(solution)/shard_map/ppermute | solution.py:894
  372.0 19.6 %collective-permute-start.58 = (bf16[192,512]{1,0:T(8,128)(2,1)}, bf16[192,512]{1,0:T(8,128)(2,1)S(1)}, u32[]{:S(2)}, u32[]{:S(2)}) collective-permute-start(bf16[192,512]{1,0:T(8,128)(2,1)} %get-tuple-element.268), channel_id=1, source_target_pairs={{0,16},{8,24},{16,0},{24,8},{1,17},{9,25},{17,1},{25,9},{2,18},{10... | collective-permute-start | bytes 589832 | tf_op jit(solution)/shard_map/ppermute | solution.py:894
  374.0 17.6 %collective-permute-start.59 = (bf16[192,512]{1,0:T(8,128)(2,1)}, bf16[192,512]{1,0:T(8,128)(2,1)S(1)}, u32[]{:S(2)}, u32[]{:S(2)}) collective-permute-start(bf16[192,512]{1,0:T(8,128)(2,1)} %get-tuple-element.270), channel_id=1, source_target_pairs={{0,24},{8,0},{16,8},{24,16},{1,25},{9,1},{17,9},{25,17},{2,26},{10... | collective-permute-start | bytes 589832 | tf_op jit(solution)/shard_map/ppermute | solution.py:894
  (96 other events, 800.2 us)
Sparse Core Ops, SparseCore 0:
  44.4 46.3 all-gather.7
  92.4 44.6 all-gather.9
  290.1 44.6 reduce-scatter.2
  337.0 46.2 reduce-scatter.4
  395.1 29.7 all-gather.11
